TPU v7x, 32 devices: a whole 2x2x4 slice. The times are simulated.
32 devices in a mesh: dp: 4 (over y, core), ctx: 2 (over x), tensor: 4 (over z).
Axes of the slice: x: 2, y: 2, z: 4, core: 2. Of those that a mesh axis runs over, the one named last changes fastest.
Arguments:
- stream: bfloat16 [4, 1024, 2048], P('dp', 'ctx'), may hold values from -6 to 6
- cotangent: bfloat16 [4, 1024, 2048], P('dp', 'ctx'), may hold values from -6 to 6
- prefixes: int32 [4], P('dp'), may hold values from 102 to 512
- attention_gain: float32 [2, 2048], replicated, may hold values from 0.5 to 1.5
- query_weight: bfloat16 [2, 2048, 2048], P(None, None, 'tensor'), may hold values from -0.125 to 0.125
- key_weight: bfloat16 [2, 2048, 1024], P(None, None, 'tensor'), may hold values from -0.125 to 0.125
- value_weight: bfloat16 [2, 2048, 1024], P(None, None, 'tensor'), may hold values from -0.125 to 0.125
- gate_heads: bfloat16 [2, 2048, 16], P(None, None, 'tensor'), may hold values from -0.25 to 0.25
- query_gain: float32 [2, 128], replicated, may hold values from 0.5 to 1.5
- key_gain: float32 [2, 128], replicated, may hold values from 0.5 to 1.5
- output_weight: bfloat16 [2, 2048, 2048], P(None, 'tensor'), may hold values from -0.75 to 0.75
- feed_gain: float32 [2, 2048], replicated, may hold values from 0.5 to 1.5
- gate_weight: bfloat16 [2, 2048, 6144], P(None, None, 'tensor'), may hold values from -0.125 to 0.125
- up_weight: bfloat16 [2, 2048, 6144], P(None, None, 'tensor'), may hold values from -0.125 to 0.125
- down_weight: bfloat16 [2, 6144, 2048], P(None, 'tensor'), may hold values from -0.15625 to 0.15625
Outputs:
- result: bfloat16 [4, 1024, 2048], P('dp', 'ctx')
- stream_grad: float32 [4, 1024, 2048], P('dp', 'ctx')
- attention_gain_grad: float32 [2, 2048], P(None, ('dp', 'ctx'))
- query_weight_grad: float32 [2, 2048, 2048], P(None, ('dp', 'ctx'), 'tensor')
- key_weight_grad: float32 [2, 2048, 1024], P(None, ('dp', 'ctx'), 'tensor')
- value_weight_grad: float32 [2, 2048, 1024], P(None, ('dp', 'ctx'), 'tensor')
- gate_heads_grad: float32 [2, 2048, 16], P(None, ('dp', 'ctx'), 'tensor')
- query_gain_grad: float32 [2, 128], P(None, ('dp', 'ctx'))
- key_gain_grad: float32 [2, 128], P(None, ('dp', 'ctx'))
- output_weight_grad: float32 [2, 2048, 2048], P(None, 'tensor', ('dp', 'ctx'))
- feed_gain_grad: float32 [2, 2048], P(None, ('dp', 'ctx'))
- gate_weight_grad: float32 [2, 2048, 6144], P(None, ('dp', 'ctx'), 'tensor')
- up_weight_grad: float32 [2, 2048, 6144], P(None, ('dp', 'ctx'), 'tensor')
- down_weight_grad: float32 [2, 6144, 2048], P(None, 'tensor', ('dp', 'ctx'))
Inputs may be any that keep to these rules, and one draw needn't show every extreme that they name: `prefixes`: tokens from the start of each sequence that attend both ways.
All inputs are finite; a program needn't handle non-finite values.
Results may differ from a plain program's by a relative error of at most 0.035.
Values may be sent and summed in bfloat16 or wider, within the bound.
A program may use at most 256 MiB of HBM per device.

v0:
```python
from functools import partial

import jax
import jax.numpy as jnp
from jax import lax
from jax.sharding import PartitionSpec as P

HD = 128
LAYERS = 2


epsilon = 1e-06
theta = 1000000.0
masked = -1000000000.0


def rms_scale(values, gain):
    return values * lax.rsqrt(jnp.mean(values * values, axis=-1, keepdims=True) + epsilon) * gain


def rotary_tables(positions, width):
    counter = jnp.arange(width // 2, dtype=jnp.float32)
    frequency = theta ** (-2.0 * counter / width)
    angles = positions.astype(jnp.float32)[:, None] * frequency[None, :]
    return (jnp.cos(angles), jnp.sin(angles))


def rotate(values, cos_table, sin_table):
    width = values.shape[-1]
    leading = values[..., : width // 2]
    trailing = values[..., width // 2 :]
    cos_part = cos_table[:, None, :]
    sin_part = sin_table[:, None, :]
    return jnp.concatenate(
        [leading * cos_part - trailing * sin_part, trailing * cos_part + leading * sin_part],
        axis=-1,
    )


def rotated_norm(raw, gain, cos_table, sin_table):
    return rotate(rms_scale(raw, gain), cos_table, sin_table)


def swiglu(gate_pre, up_pre):
    return jax.nn.silu(gate_pre) * up_pre


def gated(attended, logits):
    return attended * jax.nn.sigmoid(logits)[:, :, None]


def matmul(left, right):
    return jnp.dot(left, right, preferred_element_type=jnp.float32)


def weight_product(left, right):
    return lax.dot_general(
        left, right, (((0,), (0,)), ((), ())), preferred_element_type=jnp.float32
    )


def back_product(gradient, weight):
    return lax.dot_general(
        gradient, weight, (((1,), (1,)), ((), ())), preferred_element_type=jnp.float32
    )


def masked_scores(query, keys, prefix, query_pos, key_pos):
    scale = query.shape[-1] ** (-0.5)
    scores = jnp.einsum("qkgd,tkd->kgqt", query, keys, preferred_element_type=jnp.float32) * scale
    visible = (key_pos[None, :] <= query_pos[:, None]) | (key_pos[None, :] < prefix)
    return jnp.where(visible, scores, masked)


def attend_forward(inputs, query_pos, key_pos):
    query, keys, values, prefix = inputs
    scores = masked_scores(query, keys, prefix, query_pos, key_pos)
    highest = jnp.max(scores, axis=-1, keepdims=True)
    logsum = highest + jnp.log(jnp.sum(jnp.exp(scores - highest), axis=-1, keepdims=True))
    weights = jnp.exp(scores - logsum).astype(jnp.bfloat16)
    attended = jnp.einsum("kgqt,tkd->qkgd", weights, values, preferred_element_type=jnp.float32)
    return (attended, logsum)


def attend_backward(inputs, query_pos, key_pos):
    query, keys, values, prefix, logsum, out_grad = inputs
    scale = query.shape[-1] ** (-0.5)
    weights = jnp.exp(masked_scores(query, keys, prefix, query_pos, key_pos) - logsum)
    weight_grad = jnp.einsum("qkgd,tkd->kgqt", out_grad, values, preferred_element_type=jnp.float32)
    score_grad = weights * (weight_grad - jnp.sum(weights * weight_grad, axis=-1, keepdims=True))
    score_low = score_grad.astype(jnp.bfloat16)
    query_grad = (
        jnp.einsum("kgqt,tkd->qkgd", score_low, keys, preferred_element_type=jnp.float32) * scale
    )
    key_grad = (
        jnp.einsum("kgqt,qkgd->tkd", score_low, query, preferred_element_type=jnp.float32) * scale
    )
    value_grad = jnp.einsum(
        "kgqt,qkgd->tkd", weights.astype(jnp.bfloat16), out_grad, preferred_element_type=jnp.float32
    )
    return (query_grad, key_grad, value_grad)


def rounded_rows(gradient):
    branch_low = gradient.astype(jnp.bfloat16)
    return branch_low


def layer_forward(flat_rows, params, tables, prefixes):
    (
        attention_gain,
        query_weight,
        key_weight,
        value_weight,
        gate_heads,
        query_gain,
        key_gain,
        output_weight,
        feed_gain,
        gate_weight,
        up_weight,
        down_weight,
    ) = params
    query_pos, key_pos, cos_table, sin_table = tables
    seq_count = prefixes.shape[0]
    row_count = query_pos.shape[0]
    tokens_here = seq_count * row_count
    normed = rms_scale(flat_rows, attention_gain).astype(jnp.bfloat16)
    query_raw = matmul(normed, query_weight).reshape(seq_count, row_count, -1, HD)
    key_raw = matmul(normed, key_weight).reshape(seq_count, row_count, -1, HD)
    values = matmul(normed, value_weight).astype(jnp.bfloat16).reshape(seq_count, row_count, -1, HD)
    logits = matmul(normed, gate_heads)
    query_rot = rotated_norm(query_raw, query_gain, cos_table, sin_table).astype(jnp.bfloat16)
    key_rot = rotated_norm(key_raw, key_gain, cos_table, sin_table).astype(jnp.bfloat16)
    key_full, value_full = (
        lax.all_gather(key_rot, "ctx", axis=1, tiled=True),
        lax.all_gather(values, "ctx", axis=1, tiled=True),
    )
    key_heads = key_rot.shape[2]
    grouped = query_rot.reshape(seq_count, row_count, key_heads, -1, HD)
    attended, logsum = lax.map(
        partial(attend_forward, query_pos=query_pos, key_pos=key_pos),
        (grouped, key_full, value_full, prefixes),
    )
    attended = attended.reshape(tokens_here, -1, HD)
    mixed_heads = gated(attended, logits).reshape(tokens_here, -1).astype(jnp.bfloat16)
    middle = flat_rows + lax.psum(
        matmul(mixed_heads, output_weight).astype(jnp.bfloat16), "tensor"
    ).astype(jnp.float32)
    normed_two = rms_scale(middle, feed_gain).astype(jnp.bfloat16)
    gate_pre = matmul(normed_two, gate_weight)
    up_pre = matmul(normed_two, up_weight)
    hidden = swiglu(gate_pre, up_pre).astype(jnp.bfloat16)
    layer_out = middle + lax.psum(
        matmul(hidden, down_weight).astype(jnp.bfloat16), "tensor"
    ).astype(jnp.float32)
    saved_state = (
        flat_rows,
        normed,
        query_raw,
        key_raw,
        logits,
        grouped,
        key_full,
        value_full,
        logsum,
        attended,
        mixed_heads,
        middle,
        normed_two,
        gate_pre,
        up_pre,
        hidden,
    )
    return (layer_out, saved_state)


def layer_backward(gradient, params, saved_state, tables, prefixes):
    (
        attention_gain,
        query_weight,
        key_weight,
        value_weight,
        gate_heads,
        query_gain,
        key_gain,
        output_weight,
        feed_gain,
        gate_weight,
        up_weight,
        down_weight,
    ) = params
    query_pos, key_pos, cos_table, sin_table = tables
    (
        flat_rows,
        normed,
        query_raw,
        key_raw,
        logits,
        grouped,
        key_full,
        value_full,
        logsum,
        attended,
        mixed_heads,
        middle,
        normed_two,
        gate_pre,
        up_pre,
        hidden,
    ) = saved_state
    tokens_here = normed.shape[0]
    branch_low = rounded_rows(gradient)
    grad_down = weight_product(hidden, branch_low)
    hidden_grad = back_product(branch_low, down_weight)
    unused_out, swiglu_pull = jax.vjp(swiglu, gate_pre, up_pre)
    gate_grad, up_grad = swiglu_pull(hidden_grad)
    gate_low = gate_grad.astype(jnp.bfloat16)
    up_low = up_grad.astype(jnp.bfloat16)
    grad_gate = weight_product(normed_two, gate_low)
    grad_up = weight_product(normed_two, up_low)
    feed_partial = back_product(gate_low, gate_weight) + back_product(up_low, up_weight)
    feed_total = lax.psum(feed_partial.astype(jnp.bfloat16), "tensor").astype(jnp.float32)
    unused_norm, feed_pull = jax.vjp(rms_scale, middle, feed_gain)
    middle_grad, grad_feed_gain = feed_pull(feed_total)
    gradient = gradient + middle_grad
    branch_low = rounded_rows(gradient)
    grad_output = weight_product(mixed_heads, branch_low)
    mixed_grad = back_product(branch_low, output_weight).reshape(attended.shape)
    unused_gate, gate_pull = jax.vjp(gated, attended, logits)
    attended_grad, logits_grad = gate_pull(mixed_grad)
    attended_low = attended_grad.astype(jnp.bfloat16).reshape(grouped.shape)
    logits_low = logits_grad.astype(jnp.bfloat16)
    query_grad, key_grad, value_grad = lax.map(
        partial(attend_backward, query_pos=query_pos, key_pos=key_pos),
        (grouped, key_full, value_full, prefixes, logsum, attended_low),
    )
    key_grad, value_grad = (
        lax.psum_scatter(
            key_grad.astype(jnp.bfloat16), "ctx", scatter_dimension=1, tiled=True
        ).astype(jnp.float32),
        lax.psum_scatter(
            value_grad.astype(jnp.bfloat16), "ctx", scatter_dimension=1, tiled=True
        ).astype(jnp.float32),
    )
    rotation = partial(rotated_norm, cos_table=cos_table, sin_table=sin_table)
    unused_query, query_pull = jax.vjp(rotation, query_raw, query_gain)
    query_raw_grad, grad_query_gain = query_pull(query_grad.reshape(query_raw.shape))
    unused_key, key_pull = jax.vjp(rotation, key_raw, key_gain)
    key_raw_grad, grad_key_gain = key_pull(key_grad)
    query_low = query_raw_grad.astype(jnp.bfloat16).reshape(tokens_here, -1)
    key_low = key_raw_grad.astype(jnp.bfloat16).reshape(tokens_here, -1)
    value_low = value_grad.astype(jnp.bfloat16).reshape(tokens_here, -1)
    grad_query = weight_product(normed, query_low)
    grad_key = weight_product(normed, key_low)
    grad_value = weight_product(normed, value_low)
    grad_heads = weight_product(normed, logits_low)
    attention_partial = (
        back_product(query_low, query_weight)
        + back_product(key_low, key_weight)
        + back_product(value_low, value_weight)
        + back_product(logits_low, gate_heads)
    )
    unused_first, attention_pull = jax.vjp(rms_scale, flat_rows, attention_gain)
    attention_total, grad_query_gain, grad_key_gain = (
        lax.psum(attention_partial.astype(jnp.bfloat16), "tensor").astype(jnp.float32),
        lax.psum(grad_query_gain.astype(jnp.bfloat16), "tensor").astype(jnp.float32),
        lax.psum(grad_key_gain.astype(jnp.bfloat16), "tensor").astype(jnp.float32),
    )
    flat_grad, grad_attention_gain = attention_pull(attention_total)
    gradient = gradient + flat_grad
    return (
        gradient,
        (
            grad_attention_gain,
            grad_query,
            grad_key,
            grad_value,
            grad_heads,
            grad_query_gain,
            grad_key_gain,
            grad_output,
            grad_feed_gain,
            grad_gate,
            grad_up,
            grad_down,
        ),
    )


def shards(
    stream,
    cotangent,
    prefixes,
    attention_gain,
    query_weight,
    key_weight,
    value_weight,
    gate_heads,
    query_gain,
    key_gain,
    output_weight,
    feed_gain,
    gate_weight,
    up_weight,
    down_weight,
):
    params_all = (
        attention_gain,
        query_weight,
        key_weight,
        value_weight,
        gate_heads,
        query_gain,
        key_gain,
        output_weight,
        feed_gain,
        gate_weight,
        up_weight,
        down_weight,
    )
    seq_count, row_count, model_width = stream.shape
    tokens_here = seq_count * row_count
    halves = lax.axis_size("ctx")
    offset = lax.axis_index("ctx") * row_count
    query_pos = offset + jnp.arange(row_count, dtype=jnp.int32)
    key_pos = jnp.arange(row_count * halves, dtype=jnp.int32)
    cos_table, sin_table = rotary_tables(query_pos, HD)
    tables = (query_pos, key_pos, cos_table, sin_table)
    current = stream.astype(jnp.float32).reshape(tokens_here, model_width)
    gradient = cotangent.astype(jnp.float32).reshape(tokens_here, model_width)
    states = []
    for depth in range(LAYERS):
        current, saved_state = layer_forward(
            current, tuple((entry[depth] for entry in params_all)), tables, prefixes
        )
        states.append(saved_state)
    result = current.astype(jnp.bfloat16)
    layer_sums = [None] * LAYERS
    for depth in reversed(range(LAYERS)):
        gradient, grads_here = layer_backward(
            gradient, tuple((entry[depth] for entry in params_all)), states[depth], tables, prefixes
        )
        layer_sums[depth] = grads_here
    stacked = tuple(
        (jnp.stack([layer_sums[depth][entry] for depth in range(LAYERS)]) for entry in range(12))
    )
    stacked = (
        lax.psum_scatter(
            stacked[0].astype(jnp.bfloat16), ("dp", "ctx"), scatter_dimension=1, tiled=True
        ).astype(jnp.float32),
        lax.psum_scatter(
            stacked[1].astype(jnp.bfloat16), ("dp", "ctx"), scatter_dimension=1, tiled=True
        ).astype(jnp.float32),
        lax.psum_scatter(
            stacked[2].astype(jnp.bfloat16), ("dp", "ctx"), scatter_dimension=1, tiled=True
        ).astype(jnp.float32),
        lax.psum_scatter(
            stacked[3].astype(jnp.bfloat16), ("dp", "ctx"), scatter_dimension=1, tiled=True
        ).astype(jnp.float32),
        lax.psum_scatter(
            stacked[4].astype(jnp.bfloat16), ("dp", "ctx"), scatter_dimension=1, tiled=True
        ).astype(jnp.float32),
        lax.psum_scatter(
            stacked[5].astype(jnp.bfloat16), ("dp", "ctx"), scatter_dimension=1, tiled=True
        ).astype(jnp.float32),
        lax.psum_scatter(
            stacked[6].astype(jnp.bfloat16), ("dp", "ctx"), scatter_dimension=1, tiled=True
        ).astype(jnp.float32),
        lax.psum_scatter(
            stacked[7].astype(jnp.bfloat16), ("dp", "ctx"), scatter_dimension=2, tiled=True
        ).astype(jnp.float32),
        lax.psum_scatter(
            stacked[8].astype(jnp.bfloat16), ("dp", "ctx"), scatter_dimension=1, tiled=True
        ).astype(jnp.float32),
        lax.psum_scatter(
            stacked[9].astype(jnp.bfloat16), ("dp", "ctx"), scatter_dimension=1, tiled=True
        ).astype(jnp.float32),
        lax.psum_scatter(
            stacked[10].astype(jnp.bfloat16), ("dp", "ctx"), scatter_dimension=1, tiled=True
        ).astype(jnp.float32),
        lax.psum_scatter(
            stacked[11].astype(jnp.bfloat16), ("dp", "ctx"), scatter_dimension=2, tiled=True
        ).astype(jnp.float32),
    )
    result = result.reshape(seq_count, row_count, model_width)
    input_grad = gradient.reshape(seq_count, row_count, model_width)
    return (
        result,
        input_grad,
        stacked[0],
        stacked[1],
        stacked[2],
        stacked[3],
        stacked[4],
        stacked[5],
        stacked[6],
        stacked[7],
        stacked[8],
        stacked[9],
        stacked[10],
        stacked[11],
    )


def solution(mesh):
    return jax.shard_map(
        shards,
        mesh=mesh,
        in_specs=(
            P("dp", "ctx", None),
            P("dp", "ctx", None),
            P("dp"),
            P(),
            P(None, None, "tensor"),
            P(None, None, "tensor"),
            P(None, None, "tensor"),
            P(None, None, "tensor"),
            P(),
            P(),
            P(None, "tensor", None),
            P(),
            P(None, None, "tensor"),
            P(None, None, "tensor"),
            P(None, "tensor", None),
        ),
        out_specs=(
            P("dp", "ctx", None),
            P("dp", "ctx", None),
            P(None, ("dp", "ctx")),
            P(None, ("dp", "ctx"), "tensor"),
            P(None, ("dp", "ctx"), "tensor"),
            P(None, ("dp", "ctx"), "tensor"),
            P(None, ("dp", "ctx"), "tensor"),
            P(None, ("dp", "ctx")),
            P(None, ("dp", "ctx")),
            P(None, "tensor", ("dp", "ctx")),
            P(None, ("dp", "ctx")),
            P(None, ("dp", "ctx"), "tensor"),
            P(None, ("dp", "ctx"), "tensor"),
            P(None, "tensor", ("dp", "ctx")),
        ),
        check_vma=False,
    )
```

profile of v0, /device:TPU:0, one launch (start us, length us, event | category | flops | bytes accessed | tf_op | source)
XLA Modules:
  0.0 1680.4 jit_solution(952413888828226144)
XLA Ops:
  16.5 10.1 all_gather.13
  42.7 8.4 all_gather.12
  51.1 7.0 fusion.166
  61.4 87.2 %all-reduce.18.cloned.1.call-done = bf16[512,2048]{1,0:T(8,128)(2,1)} async-done(((bf16[512,2048]{1,0:T(8,128)(2,1)}), bf16[512,2048]{1,0:T(8,128)(2,1)}) %all-reduce.18.cloned.1.call-update) | async-done | bytes 2097168 | tf_op jit(solution)/shard_map/psum | solution.py:147
  152.2 8.8 fusion.36
  161.1 6.5 multiply_convert_fusion.6
  173.7 85.2 %all-reduce.20.cloned.1.call-done = bf16[512,2048]{1,0:T(8,128)(2,1)} async-done(((bf16[512,2048]{1,0:T(8,128)(2,1)}), bf16[512,2048]{1,0:T(8,128)(2,1)}) %all-reduce.20.cloned.1.call-update) | async-done | bytes 2097168 | tf_op jit(solution)/shard_map/psum | solution.py:154
  275.7 8.7 all_gather.15
  293.5 7.9 all_gather.14
  301.4 7.0 fusion.158
  311.2 7.9 fusion.14
  319.1 77.9 %all-reduce.22.cloned.1.call-done = bf16[512,2048]{1,0:T(8,128)(2,1)} async-done(((bf16[512,2048]{1,0:T(8,128)(2,1)}), bf16[512,2048]{1,0:T(8,128)(2,1)}) %all-reduce.22.cloned.1.call-update) | async-done | bytes 2097168 | tf_op jit(solution)/shard_map/psum | solution.py:147
  403.0 6.3 fusion.20
  409.4 8.7 fusion.84
  421.6 7.4 add_convert_fusion.3
  429.3 4.9 fusion.242
  434.2 80.5 %all-reduce.24.cloned.1.call-done = bf16[512,2048]{1,0:T(8,128)(2,1)} async-done(((bf16[512,2048]{1,0:T(8,128)(2,1)}), bf16[512,2048]{1,0:T(8,128)(2,1)}) %all-reduce.24.cloned.1.call-update) | async-done | bytes 2097168 | tf_op jit(solution)/shard_map/psum | solution.py:223
  514.7 4.9 fusion.73
  548.4 6.7 fusion.145
  563.9 8.2 reduce-scatter.29.cloned.1.call-done
  579.0 86.4 %all-reduce.26.cloned.1.call-done = bf16[512,2048]{1,0:T(8,128)(2,1)} async-done(((bf16[512,2048]{1,0:T(8,128)(2,1)}), bf16[512,2048]{1,0:T(8,128)(2,1)}) %all-reduce.26.cloned.1.call-update) | async-done | bytes 2097168 | tf_op jit(solution)/shard_map/psum | solution.py:266
  665.4 4.9 fusion.74
  673.6 10.6 fusion.87
  684.3 6.7 fusion.30
  696.0 8.1 fusion.97
  704.2 77.2 %all-reduce.28.cloned.1.call-done = bf16[512,2048]{1,0:T(8,128)(2,1)} async-done(((bf16[512,2048]{1,0:T(8,128)(2,1)}), bf16[512,2048]{1,0:T(8,128)(2,1)}) %all-reduce.28.cloned.1.call-update) | async-done | bytes 2097168 | tf_op jit(solution)/shard_map/psum | solution.py:223
  827.2 10.9 reduce-scatter.33.cloned.1.call-done
  855.3 13.1 all-reduce.8
  882.6 5.0 fusion.103
  890.2 110.6 %all-reduce.30.cloned.1.call-done = (bf16[512,2048]{1,0:T(8,128)(2,1)}, bf16[512,2048]{1,0:T(8,128)(2,1)}) async-done(((bf16[512,2048]{1,0:T(8,128)(2,1)}, bf16[512,2048]{1,0:T(8,128)(2,1)}), (bf16[512,2048]{1,0:T(8,128)(2,1)}, bf16[512,2048]{1,0:T(8,128)(2,1)})) %all-reduce.30.cloned.1.call-update) | async-done | bytes 4194320 | tf_op jit(solution)/shard_map/psum | solution.py:154
  1017.8 5.7 fusion.9
  1027.2 5.7 pad_maximum_fusion.1
  1032.9 5.7 fusion.11
  1042.3 5.4 pad_maximum_fusion.2
  1048.0 5.7 fusion.7
  1057.5 5.5 pad_maximum_fusion
  1064.6 11.0 reduce-scatter.51.cloned.1.call-done
  1077.3 32.7 %reduce-scatter.53.cloned.1.call-done = bf16[16,2]{1,0:T(8,128)(2,1)} async-done(((bf16[128,2]{1,0:T(8,128)(2,1)}), bf16[16,2]{1,0:T(8,128)(2,1)}) %reduce-scatter.53.cloned.1.call-update) | async-done | bytes 80
  1111.4 32.8 %reduce-scatter.55.cloned.1.call-done = bf16[16,2]{1,0:T(8,128)(2,1)} async-done(((bf16[128,2]{1,0:T(8,128)(2,1)}), bf16[16,2]{1,0:T(8,128)(2,1)}) %reduce-scatter.55.cloned.1.call-update) | async-done | bytes 80
  1145.5 44.0 %reduce-scatter.39.cloned.1.call-done = bf16[2,256,256]{2,1,0:T(8,128)(2,1)} async-done(((bf16[2,2048,256]{2,1,0:T(8,128)(2,1)}), bf16[2,256,256]{2,1,0:T(8,128)(2,1)}) %reduce-scatter.39.cloned.1.call-update) | async-done | bytes 262160 | tf_op jit(solution)/shard_map/reduce_scatter | solution.py:358
  1191.3 43.2 %reduce-scatter.37.cloned.1.call-done = bf16[2,256,256]{2,1,0:T(8,128)(2,1)} async-done(((bf16[2,2048,256]{2,1,0:T(8,128)(2,1)}), bf16[2,256,256]{2,1,0:T(8,128)(2,1)}) %reduce-scatter.37.cloned.1.call-update) | async-done | bytes 262160 | tf_op jit(solution)/shard_map/reduce_scatter | solution.py:355
  1236.3 7.4 fusion.81
  1243.7 28.8 %reduce-scatter.49.cloned.1.call-done = bf16[256,2]{1,0:T(8,128)(2,1)} async-done(((bf16[2048,2]{1,0:T(8,128)(2,1)}), bf16[256,2]{1,0:T(8,128)(2,1)}) %reduce-scatter.49.cloned.1.call-update) | async-done | bytes 1040
  1274.0 53.2 %reduce-scatter.41.cloned.1.call-done = bf16[2,512,256]{2,1,0:T(8,128)(2,1)} async-done(((bf16[2,512,2048]{2,1,0:T(8,128)(2,1)}), bf16[2,512,256]{2,1,0:T(8,128)(2,1)}) %reduce-scatter.41.cloned.1.call-update) | async-done | bytes 524304 | tf_op jit(solution)/shard_map/reduce_scatter | solution.py:370
  1329.3 52.8 %reduce-scatter.35.cloned.1.call-done = bf16[2,256,512]{2,1,0:T(8,128)(2,1)} async-done(((bf16[2,2048,512]{2,1,0:T(8,128)(2,1)}), bf16[2,256,512]{2,1,0:T(8,128)(2,1)}) %reduce-scatter.35.cloned.1.call-update) | async-done | bytes 524304 | tf_op jit(solution)/shard_map/reduce_scatter | solution.py:352
  1384.3 93.8 %reduce-scatter.45.cloned.1.call-done = bf16[2,256,1536]{2,1,0:T(8,128)(2,1)} async-done(((bf16[2,2048,1536]{2,1,0:T(8,128)(2,1)}), bf16[2,256,1536]{2,1,0:T(8,128)(2,1)}) %reduce-scatter.45.cloned.1.call-update) | async-done | bytes 1572880 | tf_op jit(solution)/shard_map/reduce_scatter | solution.py:379
  1481.5 92.4 %reduce-scatter.47.cloned.1.call-done = bf16[2,1536,256]{2,1,0:T(8,128)(2,1)} async-done(((bf16[2,1536,2048]{2,1,0:T(8,128)(2,1)}), bf16[2,1536,256]{2,1,0:T(8,128)(2,1)}) %reduce-scatter.47.cloned.1.call-update) | async-done | bytes 1572880 | tf_op jit(solution)/shard_map/reduce_scatter | solution.py:382
  1577.3 92.6 %reduce-scatter.43.cloned.1.call-done = bf16[2,256,1536]{2,1,0:T(8,128)(2,1)} async-done(((bf16[2,2048,1536]{2,1,0:T(8,128)(2,1)}), bf16[2,256,1536]{2,1,0:T(8,128)(2,1)}) %reduce-scatter.43.cloned.1.call-update) | async-done | bytes 1572880 | tf_op jit(solution)/shard_map/reduce_scatter | solution.py:376
  (582 shorter events, 260.5 us)
Async XLA Ops:
  7.2 141.4 %all-reduce.18.cloned.1.call-start = ((), (), s32[]{:S(2)}) async-start(), calls=%async_computation.16 | async-start | bytes 4194304 | tf_op jit(solution)/shard_map/psum | solution.py:147
  8.0 18.6 %copy-start.99 = (f32[1,2048]{1,0:T(1,128)}, f32[1,2048]{1,0:T(1,128)S(1)}, u32[]{:S(2)}) copy-start(f32[1,2048]{1,0:T(1,128)S(1)} %get-tuple-element.196) | copy-start | bytes 24580
  13.5 13.1 copy-start
  13.8 14.3 copy-start.28
  13.8 12.8 copy-start.132
  14.4 13.6 copy-start.106
  15.0 13.1 copy-start.140
  15.5 13.8 copy-start.35
  60.7 198.2 %all-reduce.20.cloned.1.call-start = ((), (), s32[]{:S(2)}) async-start(), calls=%async_computation.17 | async-start | bytes 4194304 | tf_op jit(solution)/shard_map/psum | solution.py:154
  61.4 90.8 %copy-start.84 = (f32[1,2048]{1,0:T(1,128)}, f32[1,2048]{1,0:T(1,128)S(1)}, u32[]{:S(2)}) copy-start(f32[1,2048]{1,0:T(1,128)S(1)} %get-tuple-element.194) | copy-start | bytes 24580
  152.2 16.5 slice-start.15
  152.2 16.5 slice-start.16
  173.3 223.8 %all-reduce.22.cloned.1.call-start = ((), (), s32[]{:S(2)}) async-start(), calls=%async_computation.18 | async-start | bytes 4194304 | tf_op jit(solution)/shard_map/psum | solution.py:147
  293.5 14.9 copy-start.97
  311.0 203.7 %all-reduce.24.cloned.1.call-start = ((), (), s32[]{:S(2)}) async-start(), calls=%async_computation.19 | async-start | bytes 4194304 | tf_op jit(solution)/shard_map/psum | solution.py:223
  403.0 15.1 slice-start.9
  403.0 15.1 slice-start.10
  429.0 126.1 %reduce-scatter.27.cloned.1.call-start = ((), (), s32[]{:S(2)}) async-start(), calls=%async_computation.20 | async-start | bytes 786432 | tf_op jit(solution)/shard_map/reduce_scatter | solution.py:239
  541.1 31.0 %reduce-scatter.29.cloned.1.call-start = ((), (), s32[]{:S(2)}) async-start(), calls=%async_computation.21 | async-start | bytes 786432 | tf_op jit(solution)/shard_map/reduce_scatter | solution.py:242
  555.1 110.4 %all-reduce.26.cloned.1.call-start = ((), (), s32[]{:S(2)}) async-start(), calls=%async_computation.22 | async-start | bytes 4194304 | tf_op jit(solution)/shard_map/psum | solution.py:266
  558.5 13.6 copy-start.75
  559.7 14.3 copy-start.76
  574.4 91.0 %copy-start.122 = (f32[512]{0:T(512)S(1)}, f32[512]{0:T(512)}, u32[]{:S(2)}) copy-start(f32[512]{0:T(512)} %copy-done.121) | copy-start | bytes 6148
  578.7 91.6 %copy-start.128 = (f32[512]{0:T(512)S(1)}, f32[512]{0:T(512)}, u32[]{:S(2)}) copy-start(f32[512]{0:T(512)} %copy-done.127) | copy-start | bytes 6148
  578.8 202.6 %all-reduce.28.cloned.1.call-start = ((), (), s32[]{:S(2)}) async-start(), calls=%async_computation.23 | async-start | bytes 4194304 | tf_op jit(solution)/shard_map/psum | solution.py:223
  673.6 17.4 %slice-start.12 = ((s8[12582912]{0:T(1024)(128)(4,1)}), s8[4194304]{0:T(1024)(128)(4,1)S(1)}, s32[]{:S(2)}) async-start(s8[12582912]{0:T(1024)(128)(4,1)} %bitcast.595), calls=%async_computation.51 | async-start | bytes 8388608
  673.6 17.4 %slice-start.13 = ((s8[12582912]{0:T(1024)(128)(4,1)}), s8[4194304]{0:T(1024)(128)(4,1)S(1)}, s32[]{:S(2)}) async-start(s8[12582912]{0:T(1024)(128)(4,1)} %bitcast.595), calls=%async_computation.52 | async-start | bytes 8388608
  695.7 125.1 %reduce-scatter.31.cloned.1.call-start = ((), (), s32[]{:S(2)}) async-start(), calls=%async_computation.24 | async-start | bytes 786432 | tf_op jit(solution)/shard_map/reduce_scatter | solution.py:239
  696.0 85.4 %copy-start.1 = (bf16[1,512,2048]{2,1,0:T(8,128)(2,1)S(1)}, bf16[1,512,2048]{2,1,0:T(8,128)(2,1)}, u32[]{:S(2)}) copy-start(bf16[1,512,2048]{2,1,0:T(8,128)(2,1)} %param.15) | copy-start | bytes 6291460
  696.0 85.4 %copy-start.85 = (f32[1,2048]{1,0:T(1,128)S(1)}, f32[1,2048]{1,0:T(1,128)}, u32[]{:S(2)}) copy-start(f32[1,2048]{1,0:T(1,128)} %copy-done.84) | copy-start | bytes 24580
  696.0 85.3 %copy-start.120 = (f32[512]{0:T(512)S(1)}, f32[512]{0:T(512)}, u32[]{:S(2)}) copy-start(f32[512]{0:T(512)} %copy-done.119) | copy-start | bytes 6148
  704.2 81.9 %copy-start.126 = (f32[512]{0:T(512)S(1)}, f32[512]{0:T(512)}, u32[]{:S(2)}) copy-start(f32[512]{0:T(512)} %copy-done.125) | copy-start | bytes 6148
  807.1 31.0 %reduce-scatter.33.cloned.1.call-start = ((), (), s32[]{:S(2)}) async-start(), calls=%async_computation.25 | async-start | bytes 786432 | tf_op jit(solution)/shard_map/reduce_scatter | solution.py:242
  819.7 181.1 %all-reduce.30.cloned.1.call-start = ((), (), s32[]{:S(2)}) async-start(), calls=%async_computation.38 | async-start | bytes 8388608 | tf_op jit(solution)/shard_map/psum | solution.py:154
  827.2 13.1 copy-start.93
  845.1 218.0 %reduce-scatter.57.cloned.1.call-start = ((), (), s32[]{:S(2)}) async-start(), calls=%async_computation.37 | async-start | bytes 589824
  852.9 222.7 %reduce-scatter.51.cloned.1.call-start = ((), (), s32[]{:S(2)}) async-start(), calls=%async_computation.34 | async-start | bytes 589824
  855.2 254.8 %reduce-scatter.53.cloned.1.call-start = ((), (), s32[]{:S(2)}) async-start(), calls=%async_computation.35 | async-start | bytes 36864
  869.2 275.0 %reduce-scatter.55.cloned.1.call-start = ((), (), s32[]{:S(2)}) async-start(), calls=%async_computation.36 | async-start | bytes 36864
  872.9 316.6 %reduce-scatter.39.cloned.1.call-start = ((), (), s32[]{:S(2)}) async-start(), calls=%async_computation.28 | async-start | bytes 2359296 | tf_op jit(solution)/shard_map/reduce_scatter | solution.py:358
  876.0 358.5 %reduce-scatter.37.cloned.1.call-start = ((), (), s32[]{:S(2)}) async-start(), calls=%async_computation.27 | async-start | bytes 2359296 | tf_op jit(solution)/shard_map/reduce_scatter | solution.py:355
  881.0 391.5 %reduce-scatter.49.cloned.1.call-start = ((), (), s32[]{:S(2)}) async-start(), calls=%async_computation.33 | async-start | bytes 589824
  1005.2 322.0 %reduce-scatter.41.cloned.1.call-start = ((), (), s32[]{:S(2)}) async-start(), calls=%async_computation.29 | async-start | bytes 4718592 | tf_op jit(solution)/shard_map/reduce_scatter | solution.py:370
  1009.9 372.2 %reduce-scatter.35.cloned.1.call-start = ((), (), s32[]{:S(2)}) async-start(), calls=%async_computation.26 | async-start | bytes 4718592 | tf_op jit(solution)/shard_map/reduce_scatter | solution.py:352
  1017.7 460.4 %reduce-scatter.45.cloned.1.call-start = ((), (), s32[]{:S(2)}) async-start(), calls=%async_computation.31 | async-start | bytes 14155776 | tf_op jit(solution)/shard_map/reduce_scatter | solution.py:379
  1032.8 541.1 %reduce-scatter.47.cloned.1.call-start = ((), (), s32[]{:S(2)}) async-start(), calls=%async_computation.32 | async-start | bytes 14155776 | tf_op jit(solution)/shard_map/reduce_scatter | solution.py:382
  1047.7 622.2 %reduce-scatter.43.cloned.1.call-start = ((), (), s32[]{:S(2)}) async-start(), calls=%async_computation.30 | async-start | bytes 14155776 | tf_op jit(solution)/shard_map/reduce_scatter | solution.py:376
  1063.0 173.3 %copy-start.124 = (f32[512]{0:T(512)S(1)}, f32[512]{0:T(512)}, u32[]{:S(2)}) copy-start(f32[512]{0:T(512)} %copy-done.123) | copy-start | bytes 6148
  (154 other events, 765.1 us)
Sparse Core Ops, SparseCore 0:
  60.8 87.7 all-reduce.17
  173.4 85.4 all-reduce.19
  311.1 85.9 all-reduce.21
  429.2 85.4 all-reduce.23
  541.2 13.5 reduce-scatter.26
  557.5 14.5 reduce-scatter.28
  578.9 86.4 all-reduce.25
  695.8 85.4 all-reduce.27
  807.3 13.4 reduce-scatter.30
  823.5 14.5 reduce-scatter.32
  845.2 155.5 all-reduce.29
  1004.6 33.1 reduce-scatter.56
  1041.4 34.1 reduce-scatter.50
  1078.8 31.2 reduce-scatter.52
  1112.9 31.2 reduce-scatter.54
  1148.3 41.2 reduce-scatter.38
  1193.3 41.2 reduce-scatter.36
  1238.3 34.1 reduce-scatter.48
  1275.9 51.3 reduce-scatter.40
  1330.8 51.2 reduce-scatter.34
  1385.6 92.3 reduce-scatter.44
  1481.5 92.3 reduce-scatter.46
  1577.5 92.3 reduce-scatter.42
where the time goes:
time: 1690 us; the launch traced here: 1680 us
  waiting for transfers between devices  1200 us (71%)
  matrix products  233 us (14%)
  other arithmetic  128 us (8%)
  blocking collectives  48.2 us (3%)
  local copies, waits for them, and re-layouts  47.2 us (3%)
  between operations  17.6 us (1%)
    psum x2, waiting for transfers between devices, layer_forward(): lax.psum(matmul(hidden, down_weight).astype(jnp.bfloat16), 'tensor')  196 us
    psum x2, waiting for transfers between devices, layer_forward(): lax.psum(matmul(mixed_heads, output_weight).astype(jnp.bfloat16), 'tensor')  165 us
    psum x2, waiting for transfers between devices, layer_backward(): lax.psum(feed_partial.astype(jnp.bfloat16), 'tensor').astype(jnp.float32)  158 us
    unnamed x28, waiting for transfers between devices  106 us
    reduce_scatter x1, waiting for transfers between devices, shards(): lax.psum_scatter(stacked[10].astype(jnp.bfloat16), ('dp', 'ctx'), scatter...  93.8 us
    reduce_scatter x1, waiting for transfers between devices, shards(): lax.psum_scatter(stacked[9].astype(jnp.bfloat16), ('dp', 'ctx'), scatter_...  92.6 us
    reduce_scatter x1, waiting for transfers between devices, shards(): lax.psum_scatter(stacked[11].astype(jnp.bfloat16), ('dp', 'ctx'), scatter...  92.4 us
    psum x1, waiting for transfers between devices, layer_backward(): lax.psum(attention_partial.astype(jnp.bfloat16), 'tensor')  86.4 us
  transfers between devices with their start and end apart: 23, of which 21 were waited for; matrix products, arithmetic and copies ran while one was open for 11% of the time, Pallas kernels for 0%

commit v1 on v0

v1 whole, which is shorter than its diff:
```python
from functools import partial

import jax
import jax.numpy as jnp
from jax import lax
from jax.experimental import pallas as pl
from jax.experimental.pallas import tpu as pltpu
from jax.sharding import PartitionSpec as P

HD = 128
LAYERS = 2
LANES = 128

epsilon = 1e-06
theta = 1000000.0
masked = -1000000000.0

BF = jnp.bfloat16
F32 = jnp.float32
ANY = pl.BlockSpec(memory_space=pl.ANY)
WHOLE = pl.BlockSpec(memory_space=pltpu.VMEM)
MESH = pl.DeviceIdType.MESH

BLOCKS = 8
PIECES = 2
LAG = 4
STRIP = 16
VMEM_LIMIT = 62 * 1024 * 1024


def rms_scale(values, gain):
    return values * lax.rsqrt(jnp.mean(values * values, axis=-1, keepdims=True) + epsilon) * gain


def rotary_tables(positions, width):
    counter = jnp.arange(width // 2, dtype=jnp.float32)
    frequency = theta ** (-2.0 * counter / width)
    angles = positions.astype(jnp.float32)[:, None] * frequency[None, :]
    return (jnp.cos(angles), jnp.sin(angles))


def rotate(values, cos_table, sin_table):
    width = values.shape[-1]
    leading = values[..., : width // 2]
    trailing = values[..., width // 2 :]
    cos_part = cos_table[:, None, :]
    sin_part = sin_table[:, None, :]
    return jnp.concatenate(
        [leading * cos_part - trailing * sin_part, trailing * cos_part + leading * sin_part],
        axis=-1,
    )


def rotated_norm(raw, gain, cos_table, sin_table):
    return rotate(rms_scale(raw, gain), cos_table, sin_table)


def gated(attended, logits):
    return attended * jax.nn.sigmoid(logits)[:, :, None]


def matmul(left, right):
    return jnp.dot(left, right, preferred_element_type=F32)


def weight_product(left, right):
    return lax.dot_general(left, right, (((0,), (0,)), ((), ())), preferred_element_type=F32)


def back_product(gradient, weight):
    return lax.dot_general(gradient, weight, (((1,), (1,)), ((), ())), preferred_element_type=F32)


def masked_scores(query, keys, prefix, query_pos, key_pos):
    scale = query.shape[-1] ** (-0.5)
    scores = jnp.einsum("qkgd,tkd->kgqt", query, keys, preferred_element_type=F32) * scale
    visible = (key_pos[None, :] <= query_pos[:, None]) | (key_pos[None, :] < prefix)
    return jnp.where(visible, scores, masked)


def attend_forward(inputs, query_pos, key_pos):
    query, keys, values, prefix = inputs
    scores = masked_scores(query, keys, prefix, query_pos, key_pos)
    highest = jnp.max(scores, axis=-1, keepdims=True)
    logsum = highest + jnp.log(jnp.sum(jnp.exp(scores - highest), axis=-1, keepdims=True))
    weights = jnp.exp(scores - logsum).astype(BF)
    attended = jnp.einsum("kgqt,tkd->qkgd", weights, values, preferred_element_type=F32)
    return (attended, logsum)


def attend_backward(inputs, query_pos, key_pos):
    query, keys, values, prefix, logsum, out_grad = inputs
    scale = query.shape[-1] ** (-0.5)
    weights = jnp.exp(masked_scores(query, keys, prefix, query_pos, key_pos) - logsum)
    weight_grad = jnp.einsum("qkgd,tkd->kgqt", out_grad, values, preferred_element_type=F32)
    score_grad = weights * (weight_grad - jnp.sum(weights * weight_grad, axis=-1, keepdims=True))
    score_low = score_grad.astype(BF)
    query_grad = jnp.einsum("kgqt,tkd->qkgd", score_low, keys, preferred_element_type=F32) * scale
    key_grad = jnp.einsum("kgqt,qkgd->tkd", score_low, query, preferred_element_type=F32) * scale
    value_grad = jnp.einsum(
        "kgqt,qkgd->tkd", weights.astype(BF), out_grad, preferred_element_type=F32
    )
    return (query_grad, key_grad, value_grad)


def tile_of(width):
    for size in (512, 384, 256, 128):
        if width % size == 0:
            return size
    return width


def loop(count, body):
    def step(i, carry):
        body(i)
        return carry

    lax.fori_loop(0, count, step, 0)


class Chain:
    def __init__(self, size):
        self.size = size
        self.spot = lax.axis_index("tensor")
        half = size // 2
        on_left = self.spot < half
        self.end = (self.spot == 0) | (self.spot == size - 1)
        self.mid = (self.spot == half - 1) | (self.spot == half)
        self.first_mid = self.spot == half - 1
        self.inward = jnp.where(on_left, self.spot + 1, self.spot - 1)
        self.outward = jnp.where(on_left, self.spot - 1, self.spot + 1)

    def greet(self):
        barrier = pltpu.get_barrier_semaphore()
        pl.semaphore_signal(barrier, inc=1, device_id={"tensor": self.inward}, device_id_type=MESH)

        @pl.when(jnp.logical_not(self.end))
        def _():
            pl.semaphore_signal(
                barrier, inc=1, device_id={"tensor": self.outward}, device_id_type=MESH
            )
            pl.semaphore_wait(barrier, 2)

        @pl.when(self.end)
        def _():
            pl.semaphore_wait(barrier, 1)


class Sum:
    def __init__(self, chain, refs, rows, width):
        self.chain = chain
        self.part, self.landed, self.spread, self.s_in, self.r_in, self.s_out, self.r_out = refs
        self.block = rows // BLOCKS
        self.piece = width // PIECES

    @staticmethod
    def scratch(rows, width):
        return [
            pltpu.VMEM((rows, width), BF),
            pltpu.VMEM((2, rows, width), BF),
            pltpu.VMEM((rows, width), BF),
            pltpu.SemaphoreType.DMA((BLOCKS, PIECES)),
            pltpu.SemaphoreType.DMA((2, BLOCKS, PIECES)),
            pltpu.SemaphoreType.DMA((BLOCKS,)),
            pltpu.SemaphoreType.DMA((BLOCKS,)),
        ]

    def rows(self, r):
        return pl.ds(pl.multiple_of(r * self.block, self.block), self.block)

    def cols(self, p):
        return pl.ds(pl.multiple_of(p * self.piece, self.piece), self.piece)

    def hop(self, r, p, slot):
        where = (self.rows(r), self.cols(p))
        return pltpu.make_async_remote_copy(
            src_ref=self.part.at[where],
            dst_ref=self.landed.at[(slot,) + where],
            send_sem=self.s_in.at[r, p],
            recv_sem=self.r_in.at[slot, r, p],
            device_id={"tensor": self.chain.inward},
            device_id_type=MESH,
        )

    def out_hop(self, r):
        return pltpu.make_async_remote_copy(
            src_ref=self.spread.at[self.rows(r)],
            dst_ref=self.spread.at[self.rows(r)],
            send_sem=self.s_out.at[r],
            recv_sem=self.r_out.at[r],
            device_id={"tensor": self.chain.outward},
            device_id_type=MESH,
        )

    def offer(self, r, p):
        @pl.when(self.chain.end)
        def _():
            self.hop(r, p, 0).start()

    def relay(self, r):
        @pl.when(jnp.logical_not(self.chain.end))
        def _():
            for p in range(PIECES):
                self.hop(r, p, 0).wait_recv()

                def strip(i, p=p):
                    at = pl.ds(pl.multiple_of(r * self.block + i * STRIP, STRIP), STRIP)
                    col = self.cols(p)
                    total = self.part[at, col].astype(F32) + self.landed[0, at, col].astype(F32)
                    self.part[at, col] = total.astype(BF)

                loop(self.block // STRIP, strip)

                @pl.when(self.chain.mid)
                def _(p=p):
                    self.hop(r, p, 1).start()

                @pl.when(jnp.logical_not(self.chain.mid))
                def _(p=p):
                    self.hop(r, p, 0).start()

    def finish(self, r, make):
        @pl.when(self.chain.mid)
        def _():
            for p in range(PIECES):
                self.hop(r, p, 1).wait_recv()

            def strip(i):
                at = pl.ds(pl.multiple_of(r * self.block + i * STRIP, STRIP), STRIP)
                total = self.part[at, :].astype(F32) + self.landed[1, at, :].astype(F32)
                self.spread[at, :] = make(at, total)

            loop(self.block // STRIP, strip)
            self.out_hop(r).start()

        @pl.when(jnp.logical_not(self.chain.mid))
        def _():
            self.out_hop(r).wait_recv()

            @pl.when(jnp.logical_not(self.chain.end))
            def _():
                self.out_hop(r).start()

    def close(self):
        def block(r):
            for p in range(PIECES):
                self.hop(r, p, 0).wait_send()

            @pl.when(jnp.logical_not(self.chain.end))
            def _():
                self.out_hop(r).wait_send()

        loop(BLOCKS, block)


class Small:
    def __init__(self, chain, ref, send, receive):
        self.chain = chain
        self.copy = pltpu.make_async_remote_copy(
            src_ref=ref,
            dst_ref=ref,
            send_sem=send,
            recv_sem=receive,
            device_id={"tensor": chain.outward},
            device_id_type=MESH,
        )

    @staticmethod
    def scratch(width):
        return [
            pltpu.VMEM((8, width), F32),
            pltpu.SemaphoreType.DMA(()),
            pltpu.SemaphoreType.DMA(()),
        ]

    def run(self):
        @pl.when(jnp.logical_not(self.chain.mid))
        def _():
            self.copy.wait_recv()

        @pl.when(jnp.logical_not(self.chain.end))
        def _():
            self.copy.start()
            self.copy.wait_send()


def two_sums(first, second, start, made_one, between, made_two, after):
    loop(BLOCKS, start)

    def step(s):
        @pl.when(s < BLOCKS)
        def _():
            first.relay(s)

        @pl.when((s >= 1) & (s <= BLOCKS))
        def _():
            first.finish(s - 1, made_one)
            between(s - 1)

        @pl.when((s >= LAG) & (s < BLOCKS + LAG))
        def _():
            second.relay(s - LAG)

        @pl.when(s >= LAG + 1)
        def _():
            second.finish(s - LAG - 1, made_two)
            after(s - LAG - 1)

    loop(BLOCKS + LAG + 1, step)


def one_sum(first, start, made, after):
    loop(BLOCKS, start)

    def step(s):
        @pl.when(s < BLOCKS)
        def _():
            first.relay(s)

        @pl.when(s >= 1)
        def _():
            first.finish(s - 1, made)
            after(s - 1)

    loop(BLOCKS + 1, step)


def rows_of(r, block):
    return pl.ds(pl.multiple_of(r * block, block), block)


def columns(j, width):
    return pl.ds(pl.multiple_of(j * width, width), width)


def back_norm(value, gain, grad):
    spread = lax.rsqrt(jnp.mean(value * value, axis=-1, keepdims=True) + epsilon)
    scaled = grad * gain
    pulled = jnp.mean(scaled * value, axis=-1, keepdims=True)
    terms = grad * value * spread
    return spread * scaled - value * (spread * spread * spread * pulled), terms


def fold(terms):
    folded = terms[:8]
    for k in range(8, terms.shape[0], 8):
        folded = folded + terms[k : k + 8]
    return folded


def load_all(pairs, sems):
    copies = [pltpu.make_async_copy(src, dst, sems.at[k]) for k, (src, dst) in enumerate(pairs)]
    for copy in copies:
        copy.start()
    return copies


def forward_kernel(
    size, depth, rows, width,
    mixed, stream, wo, feed_gain, wg, wu, wd, next_gain, wq, wk, wv, gh,
    middle_o, two_o, slope_o, silu_o, hidden_o, x_o, normed_o, q_o, k_o, v_o, logit_o,
    *scratch,
):
    (wo_v, wg_v, wu_v, wd_v, wq_v, wk_v, wv_v, x_v, middle_v, stage_v,
     slope_v, silu_v, hidden_v, q_v, k_v, v_v, logit_v, load_sem, out_sem) = scratch[:19]
    chain = Chain(size)
    one = Sum(chain, scratch[19:26], rows, width)
    two = Sum(chain, scratch[26:33], rows, width)
    block = one.block
    loads = load_all(
        [(wo.at[depth], wo_v), (stream, x_v), (wg.at[depth], wg_v), (wu.at[depth], wu_v),
         (wd.at[depth], wd_v), (wq.at[depth + 1], wq_v), (wk.at[depth + 1], wk_v),
         (wv.at[depth + 1], wv_v)],
        load_sem,
    )
    chain.greet()
    loads[0].wait()
    units = wg_v.shape[1]
    tile = tile_of(units)
    piece = one.piece
    gain_one = feed_gain[depth : depth + 1, :]
    gain_two = next_gain[depth + 1 : depth + 2, :]

    def out(k, r, src, dst):
        at = rows_of(r, block)
        return pltpu.make_async_copy(src.at[at], dst.at[at], out_sem.at[k, r])

    def staged(r):
        return pltpu.make_async_copy(
            stage_v.at[lax.rem(r, 2)], x_o.at[rows_of(r, block)], out_sem.at[5, r]
        )

    def start(r):
        at = rows_of(r, block)
        for p in range(PIECES):
            col = one.cols(p)
            one.part[at, col] = matmul(mixed[at, :], wo_v[:, col]).astype(BF)
            one.offer(r, p)

        @pl.when(r == 0)
        def _():
            loads[1].wait()

    def made_one(at, total):
        value = x_v[at, :].astype(F32) + total
        middle_v[at, :] = value
        return rms_scale(value, gain_one).astype(BF)

    def between(r):
        @pl.when(r == 0)
        def _():
            for copy in loads[2:5]:
                copy.wait()

        at = rows_of(r, block)

        @pl.when(chain.mid)
        def _():
            out(0, r, middle_v, middle_o).start()

        out(1, r, one.spread, two_o).start()

        def units_of(j):
            col = columns(j, tile)
            gate = matmul(one.spread[at, :], wg_v[:, col])
            up = matmul(one.spread[at, :], wu_v[:, col])
            sig = jax.nn.sigmoid(gate)
            act = gate * sig
            hidden_v[at, col] = (act * up).astype(BF)
            silu_v[at, col] = act.astype(BF)
            slope_v[at, col] = (up * (sig * (1.0 + gate * (1.0 - sig)))).astype(BF)

        loop(units // tile, units_of)
        for p in range(PIECES):
            col = two.cols(p)
            two.part[at, col] = matmul(hidden_v[at, :], wd_v[:, col]).astype(BF)
            two.offer(r, p)
        out(2, r, slope_v, slope_o).start()
        out(3, r, silu_v, silu_o).start()
        out(4, r, hidden_v, hidden_o).start()

    def made_two(at, total):
        value = middle_v[at, :] + total
        r = at.start // block
        stage_v[lax.rem(r, 2), pl.ds(pl.multiple_of(lax.rem(at.start, block), STRIP), STRIP), :] = value
        return rms_scale(value, gain_two).astype(BF)

    def after(r):
        @pl.when(r == 0)
        def _():
            for copy in loads[5:]:
                copy.wait()

        at = rows_of(r, block)

        @pl.when(chain.mid)
        def _():
            staged(r).start()

        out(6, r, two.spread, normed_o).start()
        q_v[at, :] = matmul(two.spread[at, :], wq_v[...])
        k_v[at, :] = matmul(two.spread[at, :], wk_v[...])
        v_v[at, :] = matmul(two.spread[at, :], wv_v[...]).astype(BF)
        logit_v[at, :] = matmul(two.spread[at, :], gh[...])
        out(7, r, q_v, q_o).start()
        out(8, r, k_v, k_o).start()
        out(9, r, v_v, v_o).start()
        out(10, r, logit_v, logit_o).start()

        @pl.when(chain.mid)
        def _():
            staged(r).wait()

    two_sums(one, two, start, made_one, between, made_two, after)
    one.close()
    two.close()

    def drain(r):
        @pl.when(chain.mid)
        def _():
            out(0, r, middle_v, middle_o).wait()

        for k, src, dst in (
            (1, one.spread, two_o), (2, slope_v, slope_o), (3, silu_v, silu_o),
            (4, hidden_v, hidden_o), (6, two.spread, normed_o), (7, q_v, q_o),
            (8, k_v, k_o), (9, v_v, v_o), (10, logit_v, logit_o),
        ):
            out(k, r, src, dst).wait()

    loop(BLOCKS, drain)


def turn_kernel(
    size, depth, rows, width,
    mixed, x_in, cot, wo, feed_gain, wg, wu, wd,
    two_o, hidden_o, down_o, gate_o, up_o, grad_o, low_o, mixed_o, gain_o,
    *scratch,
):
    (wo_v, wg_v, wu_v, wd_v, middle_v, cot_v, hidden_v, gate_v, up_v, mixed_v, down_v,
     load_sem, out_sem) = scratch[:13]
    chain = Chain(size)
    one = Sum(chain, scratch[13:20], rows, width)
    two = Sum(chain, scratch[20:27], rows, width)
    gain_v = scratch[27]
    small = Small(chain, *scratch[27:30])
    block = one.block
    loads = load_all(
        [(wo.at[depth], wo_v), (x_in, middle_v), (wg.at[depth], wg_v), (wu.at[depth], wu_v),
         (wd.at[depth], wd_v), (cot, cot_v)],
        load_sem,
    )
    chain.greet()
    loads[0].wait()
    units = wg_v.shape[1]
    tile = tile_of(units)
    gain_one = feed_gain[depth : depth + 1, :]

    def out(k, r, src, dst):
        at = rows_of(r, block)
        return pltpu.make_async_copy(src.at[at], dst.at[at], out_sem.at[k, r])

    def start(r):
        at = rows_of(r, block)
        for p in range(PIECES):
            col = one.cols(p)
            one.part[at, col] = matmul(mixed[at, :], wo_v[:, col]).astype(BF)
            one.offer(r, p)

        @pl.when(r == 0)
        def _():
            loads[1].wait()

    def made_one(at, total):
        value = middle_v[at, :] + total
        middle_v[at, :] = value
        return rms_scale(value, gain_one).astype(BF)

    def between(r):
        @pl.when(r == 0)
        def _():
            for copy in loads[2:]:
                copy.wait()

        at = rows_of(r, block)
        out(0, r, one.spread, two_o).start()

        def units_of(j):
            col = columns(j, tile)
            gate = matmul(one.spread[at, :], wg_v[:, col])
            up = matmul(one.spread[at, :], wu_v[:, col])
            pulled = back_product(cot_v[at, :], wd_v[col, :])
            sig = jax.nn.sigmoid(gate)
            act = gate * sig
            hidden_v[at, col] = (act * up).astype(BF)
            gate_v[at, col] = (pulled * up * (sig * (1.0 + gate * (1.0 - sig)))).astype(BF)
            up_v[at, col] = (pulled * act).astype(BF)

        loop(units // tile, units_of)
        for p in range(PIECES):
            col = two.cols(p)
            two.part[at, col] = (
                back_product(gate_v[at, :], wg_v[col, :]) + back_product(up_v[at, :], wu_v[col, :])
            ).astype(BF)
            two.offer(r, p)
        out(1, r, hidden_v, hidden_o).start()
        out(2, r, gate_v, gate_o).start()
        out(3, r, up_v, up_o).start()
        for p in range(PIECES):
            col = two.cols(p)
            partial_sum = matmul(hidden_v[at, :], wd_v[:, col])

            @pl.when(chain.first_mid)
            def _(col=col, partial_sum=partial_sum):
                down_v[at, col] = (partial_sum + middle_v[at, col]).astype(BF)

            @pl.when(jnp.logical_not(chain.first_mid))
            def _(col=col, partial_sum=partial_sum):
                down_v[at, col] = partial_sum.astype(BF)

        out(4, r, down_v, down_o).start()

    @pl.when(chain.mid)
    def _():
        gain_v[...] = jnp.zeros_like(gain_v)

    def made_two(at, total):
        pulled, terms = back_norm(middle_v[at, :], gain_one, total)
        gain_v[...] += fold(terms)
        value = cot_v[at, :].astype(F32) + pulled
        middle_v[at, :] = value
        return value.astype(BF)

    def after(r):
        at = rows_of(r, block)

        @pl.when(chain.mid)
        def _():
            out(5, r, middle_v, grad_o).start()

        out(6, r, two.spread, low_o).start()
        mixed_v[at, :] = back_product(two.spread[at, :], wo_v[...])
        out(7, r, mixed_v, mixed_o).start()

    two_sums(one, two, start, made_one, between, made_two, after)
    small.run()
    gain_out = pltpu.make_async_copy(gain_v, gain_o, out_sem.at[8, 0])
    gain_out.start()
    one.close()
    two.close()

    def drain(r):
        @pl.when(chain.mid)
        def _():
            out(5, r, middle_v, grad_o).wait()

        for k, src, dst in (
            (0, one.spread, two_o), (1, hidden_v, hidden_o), (2, gate_v, gate_o),
            (3, up_v, up_o), (4, down_v, down_o), (6, two.spread, low_o), (7, mixed_v, mixed_o),
        ):
            out(k, r, src, dst).wait()

    loop(BLOCKS, drain)
    gain_out.wait()


def back_kernel(
    size, depth, rows, width,
    q_low, k_low, v_low, l_low, gh, x_in, grad_in, attention_gain, wq, wk, wv,
    wd, wg, wu, slope_in, silu_in, middle_in, feed_gain, wo,
    gate_o, up_o, first_o, grad_o, low_o, mixed_o, gain_o, feed_gain_o,
    *scratch,
):
    (wq_v, wk_v, wv_v, wd_v, wg_v, wu_v, wo_v, x_v, grad_v, middle_v, slope_v, silu_v,
     gate_v, up_v, mixed_v, load_sem, out_sem) = scratch[:17]
    chain = Chain(size)
    one = Sum(chain, scratch[17:24], rows, width)
    two = Sum(chain, scratch[24:31], rows, width)
    gain_v = scratch[31]
    small = Small(chain, *scratch[31:34])
    feed_v = scratch[34]
    small_two = Small(chain, *scratch[34:37])
    block = one.block
    below = depth - 1
    loads = load_all(
        [(wq.at[depth], wq_v), (wk.at[depth], wk_v), (wv.at[depth], wv_v), (x_in, x_v),
         (grad_in, grad_v), (wd.at[below], wd_v), (wg.at[below], wg_v), (wu.at[below], wu_v),
         (slope_in, slope_v), (silu_in, silu_v), (middle_in, middle_v), (wo.at[below], wo_v)],
        load_sem,
    )
    chain.greet()
    for copy in loads[:3]:
        copy.wait()
    units = wg_v.shape[1]
    tile = tile_of(units)
    gain_one = attention_gain[depth : depth + 1, :]
    gain_two = feed_gain[below : below + 1, :]

    def out(k, r, src, dst):
        at = rows_of(r, block)
        return pltpu.make_async_copy(src.at[at], dst.at[at], out_sem.at[k, r])

    def start(r):
        at = rows_of(r, block)
        for p in range(PIECES):
            col = one.cols(p)
            one.part[at, col] = (
                back_product(q_low[at, :], wq_v[col, :])
                + back_product(k_low[at, :], wk_v[col, :])
                + back_product(v_low[at, :], wv_v[col, :])
                + back_product(l_low[at, :], gh[col, :])
            ).astype(BF)
            one.offer(r, p)

        @pl.when(r == 0)
        def _():
            for copy in loads[3:5]:
                copy.wait()

    @pl.when(chain.mid)
    def _():
        gain_v[...] = jnp.zeros_like(gain_v)
        feed_v[...] = jnp.zeros_like(feed_v)

    def made_one(at, total):
        pulled, terms = back_norm(x_v[at, :], gain_one, total)
        gain_v[...] += fold(terms)
        value = grad_v[at, :] + pulled
        grad_v[at, :] = value
        return value.astype(BF)

    def between(r):
        @pl.when(r == 0)
        def _():
            for copy in loads[5:]:
                copy.wait()

        at = rows_of(r, block)
        out(0, r, one.spread, first_o).start()

        def units_of(j):
            col = columns(j, tile)
            pulled = back_product(one.spread[at, :], wd_v[col, :])
            gate_v[at, col] = (pulled * slope_v[at, col].astype(F32)).astype(BF)
            up_v[at, col] = (pulled * silu_v[at, col].astype(F32)).astype(BF)

        loop(units // tile, units_of)
        for p in range(PIECES):
            col = two.cols(p)
            two.part[at, col] = (
                back_product(gate_v[at, :], wg_v[col, :]) + back_product(up_v[at, :], wu_v[col, :])
            ).astype(BF)
            two.offer(r, p)
        out(1, r, gate_v, gate_o).start()
        out(2, r, up_v, up_o).start()

    def made_two(at, total):
        pulled, terms = back_norm(middle_v[at, :], gain_two, total)
        feed_v[...] += fold(terms)
        value = grad_v[at, :] + pulled
        grad_v[at, :] = value
        return value.astype(BF)

    def after(r):
        at = rows_of(r, block)

        @pl.when(chain.mid)
        def _():
            out(5, r, grad_v, grad_o).start()

        out(3, r, two.spread, low_o).start()
        mixed_v[at, :] = back_product(two.spread[at, :], wo_v[...])
        out(4, r, mixed_v, mixed_o).start()

    two_sums(one, two, start, made_one, between, made_two, after)
    small.run()
    small_two.run()
    gain_out = pltpu.make_async_copy(gain_v, gain_o, out_sem.at[6, 0])
    feed_out = pltpu.make_async_copy(feed_v, feed_gain_o, out_sem.at[7, 0])
    gain_out.start()
    feed_out.start()
    one.close()
    two.close()

    def drain(r):
        @pl.when(chain.mid)
        def _():
            out(5, r, grad_v, grad_o).wait()

        for k, src, dst in (
            (0, one.spread, first_o), (1, gate_v, gate_o), (2, up_v, up_o),
            (3, two.spread, low_o), (4, mixed_v, mixed_o),
        ):
            out(k, r, src, dst).wait()

    loop(BLOCKS, drain)
    gain_out.wait()
    feed_out.wait()


def last_kernel(
    size, depth, rows, width,
    q_low, k_low, v_low, l_low, gh, x_in, grad_in, attention_gain, wq, wk, wv,
    grad_o, gain_o,
    *scratch,
):
    (wq_v, wk_v, wv_v, x_v, grad_v, load_sem, out_sem) = scratch[:7]
    chain = Chain(size)
    one = Sum(chain, scratch[7:14], rows, width)
    gain_v = scratch[14]
    small = Small(chain, *scratch[14:17])
    block = one.block
    loads = load_all(
        [(wq.at[depth], wq_v), (wk.at[depth], wk_v), (wv.at[depth], wv_v), (x_in, x_v),
         (grad_in, grad_v)],
        load_sem,
    )
    chain.greet()
    for copy in loads[:3]:
        copy.wait()
    gain_one = attention_gain[depth : depth + 1, :]

    def out(k, r, src, dst):
        at = rows_of(r, block)
        return pltpu.make_async_copy(src.at[at], dst.at[at], out_sem.at[k, r])

    def start(r):
        at = rows_of(r, block)
        for p in range(PIECES):
            col = one.cols(p)
            one.part[at, col] = (
                back_product(q_low[at, :], wq_v[col, :])
                + back_product(k_low[at, :], wk_v[col, :])
                + back_product(v_low[at, :], wv_v[col, :])
                + back_product(l_low[at, :], gh[col, :])
            ).astype(BF)
            one.offer(r, p)

        @pl.when(r == 0)
        def _():
            for copy in loads[3:]:
                copy.wait()

    @pl.when(chain.mid)
    def _():
        gain_v[...] = jnp.zeros_like(gain_v)

    def made_one(at, total):
        pulled, terms = back_norm(x_v[at, :].astype(F32), gain_one, total)
        gain_v[...] += fold(terms)
        return (grad_v[at, :] + pulled).astype(BF)

    def after(r):
        out(0, r, one.spread, grad_o).start()

    one_sum(one, start, made_one, after)
    small.run()
    gain_out = pltpu.make_async_copy(gain_v, gain_o, out_sem.at[1, 0])
    gain_out.start()
    one.close()

    def drain(r):
        out(0, r, one.spread, grad_o).wait()

    loop(BLOCKS, drain)
    gain_out.wait()


def call(kernel, collective_id, in_specs, outs, scratch, flops):
    return pl.pallas_call(
        kernel,
        out_shape=tuple(jax.ShapeDtypeStruct(shape, kind) for shape, kind in outs),
        in_specs=in_specs,
        out_specs=tuple(ANY for _ in outs),
        scratch_shapes=scratch,
        cost_estimate=pl.CostEstimate(flops=flops, bytes_accessed=40_000_000, transcendentals=0),
        compiler_params=pltpu.CompilerParams(
            collective_id=collective_id, has_side_effects=True, vmem_limit_bytes=VMEM_LIMIT
        ),
    )


def dma(*shape):
    return pltpu.SemaphoreType.DMA(shape)


def shards(
    size,
    stream,
    cotangent,
    prefixes,
    attention_gain,
    query_weight,
    key_weight,
    value_weight,
    gate_heads,
    query_gain,
    key_gain,
    output_weight,
    feed_gain,
    gate_weight,
    up_weight,
    down_weight,
):
    seq_count, row_count, width = stream.shape
    rows = seq_count * row_count
    block = rows // BLOCKS
    heads_wide = query_weight.shape[2]
    keys_wide = key_weight.shape[2]
    units = gate_weight.shape[2]
    gates = gate_heads.shape[2]
    halves = lax.axis_size("ctx")
    offset = lax.axis_index("ctx") * row_count
    query_pos = offset + jnp.arange(row_count, dtype=jnp.int32)
    key_pos = jnp.arange(row_count * halves, dtype=jnp.int32)
    cos_table, sin_table = rotary_tables(query_pos, HD)
    stream_flat = stream.reshape(rows, width)
    cot_flat = cotangent.reshape(rows, width)
    heads_padded = [
        jnp.pad(gate_heads[depth], ((0, 0), (0, LANES - gates))) for depth in range(LAYERS)
    ]
    sum_scratch = Sum.scratch(rows, width)

    def attention(depth, q_raw, k_raw, values, logits):
        q_raw = q_raw.reshape(seq_count, row_count, -1, HD)
        k_raw = k_raw.reshape(seq_count, row_count, -1, HD)
        values = values.reshape(seq_count, row_count, -1, HD)
        query_rot = rotated_norm(q_raw, query_gain[depth], cos_table, sin_table).astype(BF)
        key_rot = rotated_norm(k_raw, key_gain[depth], cos_table, sin_table).astype(BF)
        key_full = lax.all_gather(key_rot, "ctx", axis=1, tiled=True)
        value_full = lax.all_gather(values, "ctx", axis=1, tiled=True)
        key_heads = key_rot.shape[2]
        grouped = query_rot.reshape(seq_count, row_count, key_heads, -1, HD)
        attended, logsum = lax.map(
            partial(attend_forward, query_pos=query_pos, key_pos=key_pos),
            (grouped, key_full, value_full, prefixes),
        )
        attended = attended.reshape(rows, -1, HD)
        mixed = gated(attended, logits).reshape(rows, -1).astype(BF)
        return mixed, (q_raw, k_raw, logits, grouped, key_full, value_full, logsum, attended)

    def attention_back(depth, mixed_grad, saved):
        q_raw, k_raw, logits, grouped, key_full, value_full, logsum, attended = saved
        unused, gate_pull = jax.vjp(gated, attended, logits)
        attended_grad, logits_grad = gate_pull(mixed_grad.reshape(attended.shape))
        attended_low = attended_grad.astype(BF).reshape(grouped.shape)
        logits_low = logits_grad.astype(BF)
        query_grad, key_grad, value_grad = lax.map(
            partial(attend_backward, query_pos=query_pos, key_pos=key_pos),
            (grouped, key_full, value_full, prefixes, logsum, attended_low),
        )
        key_grad = lax.psum_scatter(
            key_grad.astype(BF), "ctx", scatter_dimension=1, tiled=True
        ).astype(F32)
        value_grad = lax.psum_scatter(
            value_grad.astype(BF), "ctx", scatter_dimension=1, tiled=True
        ).astype(F32)
        rotation = partial(rotated_norm, cos_table=cos_table, sin_table=sin_table)
        unused, query_pull = jax.vjp(rotation, q_raw, query_gain[depth])
        query_raw_grad, grad_query_gain = query_pull(query_grad.reshape(q_raw.shape))
        unused, key_pull = jax.vjp(rotation, k_raw, key_gain[depth])
        key_raw_grad, grad_key_gain = key_pull(key_grad)
        query_low = query_raw_grad.astype(BF).reshape(rows, -1)
        key_low = key_raw_grad.astype(BF).reshape(rows, -1)
        value_low = value_grad.astype(BF).reshape(rows, -1)
        return query_low, key_low, value_low, logits_low, grad_query_gain, grad_key_gain

    normed_zero = rms_scale(stream_flat.astype(F32), attention_gain[0]).astype(BF)
    mixed_zero, saved_zero = attention(
        0,
        matmul(normed_zero, query_weight[0]),
        matmul(normed_zero, key_weight[0]),
        matmul(normed_zero, value_weight[0]).astype(BF),
        matmul(normed_zero, gate_heads[0]),
    )
    middle_zero, two_zero, slope, silu, hidden_zero, x_one, normed_one, q_raw, k_raw, values, logits = call(
        partial(forward_kernel, size, 0, rows, width),
        0,
        [WHOLE, ANY, ANY, WHOLE, ANY, ANY, ANY, WHOLE, ANY, ANY, ANY, WHOLE],
        [
            ((rows, width), F32), ((rows, width), BF), ((rows, units), BF), ((rows, units), BF),
            ((rows, units), BF), ((rows, width), F32), ((rows, width), BF),
            ((rows, heads_wide), F32), ((rows, keys_wide), F32), ((rows, keys_wide), BF),
            ((rows, LANES), F32),
        ],
        [
            pltpu.VMEM((heads_wide, width), BF), pltpu.VMEM((width, units), BF),
            pltpu.VMEM((width, units), BF), pltpu.VMEM((units, width), BF),
            pltpu.VMEM((width, heads_wide), BF), pltpu.VMEM((width, keys_wide), BF),
            pltpu.VMEM((width, keys_wide), BF), pltpu.VMEM((rows, width), BF),
            pltpu.VMEM((rows, width), F32), pltpu.VMEM((2, block, width), F32),
            pltpu.VMEM((rows, units), BF), pltpu.VMEM((rows, units), BF),
            pltpu.VMEM((rows, units), BF), pltpu.VMEM((rows, heads_wide), F32),
            pltpu.VMEM((rows, keys_wide), F32), pltpu.VMEM((rows, keys_wide), BF),
            pltpu.VMEM((rows, LANES), F32), dma(8), dma(11, BLOCKS),
        ]
        + sum_scratch + sum_scratch,
        13_000_000_000,
    )(
        mixed_zero, stream_flat, output_weight, feed_gain, gate_weight, up_weight, down_weight,
        attention_gain, query_weight, key_weight, value_weight, heads_padded[1],
    )
    mixed_one, saved_one = attention(1, q_raw, k_raw, values, logits[:, :gates])
    two_one, hidden_one, down_part, gate_low, up_low, grad, low, mixed_grad, feed_one = call(
        partial(turn_kernel, size, 1, rows, width),
        1,
        [WHOLE, ANY, ANY, ANY, WHOLE, ANY, ANY, ANY],
        [
            ((rows, width), BF), ((rows, units), BF), ((rows, width), BF), ((rows, units), BF),
            ((rows, units), BF), ((rows, width), F32), ((rows, width), BF),
            ((rows, heads_wide), F32), ((8, width), F32),
        ],
        [
            pltpu.VMEM((heads_wide, width), BF), pltpu.VMEM((width, units), BF),
            pltpu.VMEM((width, units), BF), pltpu.VMEM((units, width), BF),
            pltpu.VMEM((rows, width), F32), pltpu.VMEM((rows, width), BF),
            pltpu.VMEM((rows, units), BF),
            pltpu.VMEM((rows, units), BF), pltpu.VMEM((rows, units), BF),
            pltpu.VMEM((rows, heads_wide), F32), pltpu.VMEM((rows, width), BF),
            dma(6), dma(9, BLOCKS),
        ]
        + sum_scratch + sum_scratch + Small.scratch(width),
        24_000_000_000,
    )(mixed_one, x_one, cot_flat, output_weight, feed_gain, gate_weight, up_weight, down_weight)
    result = lax.psum(down_part, "tensor")
    q_low, k_low, v_low, l_low, q_gain_one, k_gain_one = attention_back(1, mixed_grad, saved_one)

    grads = [[None] * 12 for _ in range(LAYERS)]

    def scatter(value, dimension):
        return lax.psum_scatter(
            value.astype(BF), ("dp", "ctx"), scatter_dimension=dimension, tiled=True
        ).astype(F32)

    def feed_grads(depth, hidden, low_in, two, gate, up):
        grads[depth][11] = scatter(weight_product(hidden, low_in), 1)
        grads[depth][9] = scatter(weight_product(two, gate), 0)
        grads[depth][10] = scatter(weight_product(two, up), 0)

    def head_grads(depth, mixed, low_in, normed, q, k, v, l):
        grads[depth][7] = scatter(weight_product(mixed, low_in), 1)
        grads[depth][1] = scatter(weight_product(normed, q), 0)
        grads[depth][2] = scatter(weight_product(normed, k), 0)
        grads[depth][3] = scatter(weight_product(normed, v), 0)
        grads[depth][4] = scatter(weight_product(normed, l), 0)

    feed_grads(1, hidden_one, cot_flat, two_one, gate_low, up_low)
    head_grads(1, mixed_one, low, normed_one, q_low, k_low, v_low, l_low)

    def padded(l):
        return jnp.pad(l, ((0, 0), (0, LANES - gates)))

    gate_low, up_low, first_low, grad, low, mixed_grad, gain_one, feed_zero = call(
        partial(back_kernel, size, 1, rows, width),
        2,
        [WHOLE] * 5 + [ANY, ANY, WHOLE] + [ANY] * 9 + [WHOLE, ANY],
        [
            ((rows, units), BF), ((rows, units), BF), ((rows, width), BF), ((rows, width), F32),
            ((rows, width), BF), ((rows, heads_wide), F32), ((8, width), F32), ((8, width), F32),
        ],
        [
            pltpu.VMEM((width, heads_wide), BF), pltpu.VMEM((width, keys_wide), BF),
            pltpu.VMEM((width, keys_wide), BF), pltpu.VMEM((units, width), BF),
            pltpu.VMEM((width, units), BF), pltpu.VMEM((width, units), BF),
            pltpu.VMEM((heads_wide, width), BF), pltpu.VMEM((rows, width), F32),
            pltpu.VMEM((rows, width), F32), pltpu.VMEM((rows, width), F32),
            pltpu.VMEM((rows, units), BF), pltpu.VMEM((rows, units), BF),
            pltpu.VMEM((rows, units), BF),
            pltpu.VMEM((rows, units), BF), pltpu.VMEM((rows, heads_wide), F32),
            dma(12), dma(8, BLOCKS),
        ]
        + sum_scratch + sum_scratch + Small.scratch(width) + Small.scratch(width),
        13_000_000_000,
    )(
        q_low, k_low, v_low, padded(l_low), heads_padded[1], x_one, grad, attention_gain,
        query_weight, key_weight, value_weight, down_weight, gate_weight, up_weight, slope, silu,
        middle_zero, feed_gain, output_weight,
    )
    feed_grads(0, hidden_zero, first_low, two_zero, gate_low, up_low)
    q_low, k_low, v_low, l_low, q_gain_zero, k_gain_zero = attention_back(0, mixed_grad, saved_zero)
    head_grads(0, mixed_zero, low, normed_zero, q_low, k_low, v_low, l_low)
    stream_low, gain_zero = call(
        partial(last_kernel, size, 0, rows, width),
        3,
        [WHOLE] * 5 + [ANY, ANY, WHOLE, ANY, ANY, ANY],
        [((rows, width), BF), ((8, width), F32)],
        [
            pltpu.VMEM((width, heads_wide), BF), pltpu.VMEM((width, keys_wide), BF),
            pltpu.VMEM((width, keys_wide), BF), pltpu.VMEM((rows, width), BF),
            pltpu.VMEM((rows, width), F32), dma(5), dma(2, BLOCKS),
        ]
        + sum_scratch + Small.scratch(width),
        4_000_000_000,
    )(
        q_low, k_low, v_low, padded(l_low), heads_padded[0], stream_flat, grad, attention_gain,
        query_weight, key_weight, value_weight,
    )
    grads[1][0], grads[0][0] = gain_one.sum(0), gain_zero.sum(0)
    grads[1][8], grads[0][8] = feed_one.sum(0), feed_zero.sum(0)
    grads[1][5], grads[0][5] = q_gain_one, q_gain_zero
    grads[1][6], grads[0][6] = k_gain_one, k_gain_zero
    stacked = [jnp.stack([grads[depth][entry] for depth in range(LAYERS)]) for entry in range(12)]
    stacked[5] = lax.psum(stacked[5], "tensor")
    stacked[6] = lax.psum(stacked[6], "tensor")
    for entry in (0, 5, 6, 8):
        stacked[entry] = lax.psum_scatter(
            stacked[entry], ("dp", "ctx"), scatter_dimension=1, tiled=True
        )
    return (
        result.reshape(seq_count, row_count, width),
        stream_low.astype(F32).reshape(seq_count, row_count, width),
        *stacked,
    )


def solution(mesh):
    return jax.shard_map(
        partial(shards, mesh.shape["tensor"]),
        mesh=mesh,
        in_specs=(
            P("dp", "ctx", None),
            P("dp", "ctx", None),
            P("dp"),
            P(),
            P(None, None, "tensor"),
            P(None, None, "tensor"),
            P(None, None, "tensor"),
            P(None, None, "tensor"),
            P(),
            P(),
            P(None, "tensor", None),
            P(),
            P(None, None, "tensor"),
            P(None, None, "tensor"),
            P(None, "tensor", None),
        ),
        out_specs=(
            P("dp", "ctx", None),
            P("dp", "ctx", None),
            P(None, ("dp", "ctx")),
            P(None, ("dp", "ctx"), "tensor"),
            P(None, ("dp", "ctx"), "tensor"),
            P(None, ("dp", "ctx"), "tensor"),
            P(None, ("dp", "ctx"), "tensor"),
            P(None, ("dp", "ctx")),
            P(None, ("dp", "ctx")),
            P(None, "tensor", ("dp", "ctx")),
            P(None, ("dp", "ctx")),
            P(None, ("dp", "ctx"), "tensor"),
            P(None, ("dp", "ctx"), "tensor"),
            P(None, "tensor", ("dp", "ctx")),
        ),
        check_vma=False,
    )
```

time: 1690 us -> 1570 us (0.929)
  Pallas kernels: 0 us -> 512 us
  waiting for transfers between devices: 1200 us -> 707 us
  matrix products: 233 us -> 127 us
  other arithmetic: 128 us -> 78.4 us
  local copies, waits for them, and re-layouts: 47.2 us -> 74.5 us
    psum x7 -> x1, waiting for transfers between devices: 605 us -> 0.01 us  [shards(): result = lax.psum(down_part, 'tensor')]
    pallas_call x0 -> x4, Pallas kernels: none -> 512 us  [the longest x1 135 us: shards(): call(partial(turn_kernel, size, 1, rows, width), 1, [WHOLE, ANY, ANY, ANY...]
    reduce_scatter x11 -> x18, waiting for transfers between devices: 492 us -> 706 us  [the longest x14 706 us: scatter(): lax.psum_scatter(value.astype(BF), ('dp', 'ctx'), scatter_dimension=dimen...]
    dot_general x44 -> x16, matrix products: 181 us -> 54.3 us  [the longest x2 13.2 us: attend_backward(): jnp.einsum('kgqt,qkgd->tkd', weights.astype(BF), out_grad, preferred_elem...]
    unnamed x28 -> x31, waiting for transfers between devices: 106 us -> 0.94 us
    dot_general x16, matrix products: 52.5 us -> 72.6 us  [weight_product(): lax.dot_general(left, right, (((0,), (0,)), ((), ())), preferred_element_...]
    unnamed x370 -> x181, local copies, waits for them, and re-layouts: 33.4 us -> 42 us
    convert_element_type x27 -> x12, other arithmetic: 35.6 us -> 27.5 us  [the longest x2 11.9 us: attend_backward(): score_low = score_grad.astype(BF)]
  transfers between devices with their start and end apart: 23 -> 25, of which waited for: 21 -> 14; matrix products, arithmetic and copies ran while one was open for 11% -> 11% of each run, Pallas kernels for 0% -> 8%
where the time goes in v1:
time: 1570 us; the launch traced here: 1560 us
  waiting for transfers between devices  707 us (45%)
  Pallas kernels  512 us (33%)
  matrix products  127 us (8%)
  other arithmetic  78.4 us (5%)
  local copies, waits for them, and re-layouts  74.5 us (5%)
  blocking collectives  45.8 us (3%)
  between operations  18.2 us (1%)
    reduce_scatter x14, waiting for transfers between devices, scatter(): lax.psum_scatter(value.astype(BF), ('dp', 'ctx'), scatter_dimension=dimen...  706 us
    pallas_call x1, Pallas kernels, shards(): call(partial(turn_kernel, size, 1, rows, width), 1, [WHOLE, ANY, ANY, ANY...  135 us
    pallas_call x1, Pallas kernels, shards(): call(partial(forward_kernel, size, 0, rows, width), 0, [WHOLE, ANY, ANY,...  128 us
    pallas_call x1, Pallas kernels, shards(): call(partial(back_kernel, size, 1, rows, width), 2, [WHOLE] * 5 + [ANY, A...  126 us
    pallas_call x1, Pallas kernels, shards(): call(partial(last_kernel, size, 0, rows, width), 3, [WHOLE] * 5 + [ANY, A...  123 us
    dot_general x16, matrix products, weight_product(): lax.dot_general(left, right, (((0,), (0,)), ((), ())), preferred_element_...  72.6 us
    unnamed x181, local copies, waits for them, and re-layouts  42 us
  transfers between devices with their start and end apart: 25, of which 14 were waited for; matrix products, arithmetic and copies ran while one was open for 11% of the time, Pallas kernels for 8%

profile of v1, /device:TPU:0, one launch (start us, length us, event | category | flops | bytes accessed | tf_op | source)
XLA Modules:
  0.0 1564.3 jit_solution(12480747217557553513)
XLA Ops:
  18.0 3.2 fusion.15
  27.7 10.1 all_gather.12
  40.5 8.4 all_gather.13
  65.4 127.8 %shard_map.254 = (f32[512,2048]{1,0:T(8,128)}, bf16[512,2048]{1,0:T(8,128)(2,1)}, bf16[512,1536]{1,0:T(8,128)(2,1)}, bf16[512,1536]{1,0:T(8,128)(2,1)}, bf16[512...) custom-call(bf16[512,512]{1,0:T(8,128)(2,1)} %fusion.37.mixed, ...), custom_call_target="tpu_custom_call" | custom-call | flops 12999999488 | bytes 40000000 | tf_op jit(solution)/shard_map/pallas_call | solution.py:935
  194.3 7.3 all_gather.14
  206.0 7.4 all_gather.15
  230.3 134.7 %shard_map.255 = (bf16[512,2048]{1,0:T(8,128)(2,1)}, bf16[512,1536]{1,0:T(8,128)(2,1)}, bf16[512,2048]{1,0:T(8,128)(2,1)}, bf16[512,1536]{1,0:T(8,128)(2,1)}, bf...) custom-call(bf16[512,512]{1,0:T(8,128)(2,1)} %fusion.36.mixed, ...), custom_call_target="tpu_custom_call" | custom-call | flops 24000000000 | bytes 40000000 | tf_op jit(solution)/shard_map/pallas_call | solution.py:963
  366.5 6.6 fusion.30
  373.2 5.3 fusion.3
  378.6 4.9 fusion.5
  404.2 3.7 multiply_reduce_fusion
  409.8 3.7 fusion.34
  419.6 126.4 %shard_map.256 = (bf16[512,1536]{1,0:T(8,128)(2,1)}, bf16[512,1536]{1,0:T(8,128)(2,1)}, bf16[512,2048]{1,0:T(8,128)(2,1)}, f32[512,2048]{1,0:T(8,128)}, bf16[512...) custom-call(bf16[512,512]{1,0:T(8,128)(2,1)} %bitcast.346, ...), custom_call_target="tpu_custom_call" | custom-call | flops 12999999488 | bytes 40000000 | tf_op jit(solution)/shard_map/pallas_call | solution.py:1012
  547.6 6.6 fusion.29
  554.3 7.2 fusion
  561.5 7.0 fusion.2
  584.4 4.4 multiply_reduce_fusion.1
  597.4 3.5 fusion.35
  608.5 122.9 %shard_map.257 = (bf16[512,2048]{1,0:T(8,128)(2,1)}, f32[8,2048]{1,0:T(8,128)}) custom-call(bf16[512,512]{1,0:T(8,128)(2,1)} %bitcast.351, bf16[512,256]{1,0:T(8,128)(2,1)} %bitcast.366, bf16[512,256]{1,0:T(8,128)(2,1)} %copy.416.v_low, bf16[512,128]{1,0:T(8,128)(2,1)} %pad.48.l_low, bf16[2048,128]{1,0:T(8,128)(2,1)} %pad.49.gh, ...), custom_call_target="tpu_custom_call" | custom-call | flops 4000000000 | bytes 40000000 | tf_op jit(solution)/shard_map/pallas_call | solution.py:1041
  733.8 3.6 convolution_convert_fusion.10
  739.5 3.4 convolution_convert_fusion.12
  745.2 4.2 convolution_convert_fusion.6
  749.6 4.2 convolution_convert_fusion.7
  753.9 4.3 convolution_convert_fusion.8
  761.1 8.2 convolution_convert_fusion
  770.9 6.8 convolution_convert_fusion.1
  779.3 6.7 convolution_convert_fusion.4
  787.6 6.7 convolution_convert_fusion.5
  794.4 8.3 convolution_convert_fusion.2
  802.8 6.7 convolution_convert_fusion.3
  817.9 12.6 all-reduce.12
  832.1 28.7 %reduce-scatter.55.cloned.1.call-done = bf16[256,256]{1,0:T(8,128)(2,1)} async-done(((bf16[2048,256]{1,0:T(8,128)(2,1)}), bf16[256,256]{1,0:T(8,128)(2,1)}) %reduce-scatter.55.cloned.1.call-update) | async-done | bytes 131088 | tf_op jit(solution)/shard_map/reduce_scatter | solution.py:990
  860.7 39.4 %reduce-scatter.53.cloned.1.call-done = bf16[256,256]{1,0:T(8,128)(2,1)} async-done(((bf16[2048,256]{1,0:T(8,128)(2,1)}), bf16[256,256]{1,0:T(8,128)(2,1)}) %reduce-scatter.53.cloned.1.call-update) | async-done | bytes 131088 | tf_op jit(solution)/shard_map/reduce_scatter | solution.py:990
  902.0 38.3 %reduce-scatter.51.cloned.1.call-done = bf16[256,256]{1,0:T(8,128)(2,1)} async-done(((bf16[2048,256]{1,0:T(8,128)(2,1)}), bf16[256,256]{1,0:T(8,128)(2,1)}) %reduce-scatter.51.cloned.1.call-update) | async-done | bytes 131088 | tf_op jit(solution)/shard_map/reduce_scatter | solution.py:990
  940.3 39.4 %reduce-scatter.49.cloned.1.call-done = bf16[256,256]{1,0:T(8,128)(2,1)} async-done(((bf16[2048,256]{1,0:T(8,128)(2,1)}), bf16[256,256]{1,0:T(8,128)(2,1)}) %reduce-scatter.49.cloned.1.call-update) | async-done | bytes 131088 | tf_op jit(solution)/shard_map/reduce_scatter | solution.py:990
  981.5 43.5 %reduce-scatter.59.cloned.1.call-done = bf16[512,256]{1,0:T(8,128)(2,1)} async-done(((bf16[512,2048]{1,0:T(8,128)(2,1)}), bf16[512,256]{1,0:T(8,128)(2,1)}) %reduce-scatter.59.cloned.1.call-update) | async-done | bytes 262160 | tf_op jit(solution)/shard_map/reduce_scatter | solution.py:990
  1025.1 45.0 %reduce-scatter.57.cloned.1.call-done = bf16[512,256]{1,0:T(8,128)(2,1)} async-done(((bf16[512,2048]{1,0:T(8,128)(2,1)}), bf16[512,256]{1,0:T(8,128)(2,1)}) %reduce-scatter.57.cloned.1.call-update) | async-done | bytes 262160 | tf_op jit(solution)/shard_map/reduce_scatter | solution.py:990
  1072.1 43.3 %reduce-scatter.47.cloned.1.call-done = bf16[256,512]{1,0:T(8,128)(2,1)} async-done(((bf16[2048,512]{1,0:T(8,128)(2,1)}), bf16[256,512]{1,0:T(8,128)(2,1)}) %reduce-scatter.47.cloned.1.call-update) | async-done | bytes 262160 | tf_op jit(solution)/shard_map/reduce_scatter | solution.py:990
  1115.4 45.0 %reduce-scatter.45.cloned.1.call-done = bf16[256,512]{1,0:T(8,128)(2,1)} async-done(((bf16[2048,512]{1,0:T(8,128)(2,1)}), bf16[256,512]{1,0:T(8,128)(2,1)}) %reduce-scatter.45.cloned.1.call-update) | async-done | bytes 262160 | tf_op jit(solution)/shard_map/reduce_scatter | solution.py:990
  1162.4 63.5 %reduce-scatter.71.cloned.1.call-done = bf16[1536,256]{1,0:T(8,128)(2,1)} async-done(((bf16[1536,2048]{1,0:T(8,128)(2,1)}), bf16[1536,256]{1,0:T(8,128)(2,1)}) %reduce-scatter.71.cloned.1.call-update) | async-done | bytes 786448 | tf_op jit(solution)/shard_map/reduce_scatter | solution.py:990
  1225.9 65.0 %reduce-scatter.69.cloned.1.call-done = bf16[1536,256]{1,0:T(8,128)(2,1)} async-done(((bf16[1536,2048]{1,0:T(8,128)(2,1)}), bf16[1536,256]{1,0:T(8,128)(2,1)}) %reduce-scatter.69.cloned.1.call-update) | async-done | bytes 786448 | tf_op jit(solution)/shard_map/reduce_scatter | solution.py:990
  1290.9 3.2 maximum_convert_fusion.2
  1294.1 62.3 %reduce-scatter.63.cloned.1.call-done = bf16[256,1536]{1,0:T(8,128)(2,1)} async-done(((bf16[2048,1536]{1,0:T(8,128)(2,1)}), bf16[256,1536]{1,0:T(8,128)(2,1)}) %reduce-scatter.63.cloned.1.call-update) | async-done | bytes 786448 | tf_op jit(solution)/shard_map/reduce_scatter | solution.py:990
  1356.4 65.2 %reduce-scatter.61.cloned.1.call-done = bf16[256,1536]{1,0:T(8,128)(2,1)} async-done(((bf16[2048,1536]{1,0:T(8,128)(2,1)}), bf16[256,1536]{1,0:T(8,128)(2,1)}) %reduce-scatter.61.cloned.1.call-update) | async-done | bytes 786448 | tf_op jit(solution)/shard_map/reduce_scatter | solution.py:990
  1421.6 3.4 maximum_convert_fusion
  1425.0 62.1 %reduce-scatter.67.cloned.1.call-done = bf16[256,1536]{1,0:T(8,128)(2,1)} async-done(((bf16[2048,1536]{1,0:T(8,128)(2,1)}), bf16[256,1536]{1,0:T(8,128)(2,1)}) %reduce-scatter.67.cloned.1.call-update) | async-done | bytes 786448 | tf_op jit(solution)/shard_map/reduce_scatter | solution.py:990
  1487.1 65.0 %reduce-scatter.65.cloned.1.call-done = bf16[256,1536]{1,0:T(8,128)(2,1)} async-done(((bf16[2048,1536]{1,0:T(8,128)(2,1)}), bf16[256,1536]{1,0:T(8,128)(2,1)}) %reduce-scatter.65.cloned.1.call-update) | async-done | bytes 786448 | tf_op jit(solution)/shard_map/reduce_scatter | solution.py:990
  1552.1 3.2 maximum_convert_fusion.1
  (368 shorter events, 153.7 us)
Async XLA Ops:
  8.0 406.5 %reduce-scatter.39.cloned.1.call-start = ((), (), s32[]{:S(2)}) async-start(), calls=%async_computation.26 | async-start | bytes 786432 | tf_op jit(solution)/shard_map/reduce_scatter | solution.py:914
  10.4 15.1 copy-start.72
  14.8 47.7 %copy-start.29 = (f32[512,4]{1,0:T(8,128)}, f32[512,4]{1,0:T(8,128)S(1)}, u32[]{:S(2)}) copy-start(f32[512,4]{1,0:T(8,128)S(1)} %fusion.33) | copy-start | bytes 24580
  16.7 22.2 %copy-start.67 = (f32[512,2]{0,1:T(2,128)}, f32[512,2]{0,1:T(2,128)S(1)}, u32[]{:S(2)}) copy-start(f32[512,2]{0,1:T(2,128)S(1)} %multiply_reduce_fusion.11) | copy-start | bytes 12292
  17.9 21.9 %copy-start.21 = (f32[1,512,2,128]{3,1,2,0:T(8,128)}, f32[1,512,2,128]{3,1,2,0:T(8,128)S(1)}, u32[]{:S(2)}) copy-start(f32[1,512,2,128]{3,1,2,0:T(8,128)S(1)} %copy.310) | copy-start | bytes 1572868
  25.5 14.6 copy-start.69
  27.6 21.5 %copy-start.12 = (f32[1,512,4,128]{3,2,1,0:T(4,128)S(1)}, f32[1,512,4,128]{3,2,1,0:T(4,128)}, u32[]{:S(2)}) copy-start(f32[1,512,4,128]{3,2,1,0:T(4,128)} %copy.312) | copy-start | bytes 3145732
  38.9 11.8 copy-start.61
  39.9 165.7 %copy-start.4 = (f32[512,64]{1,0:T(8,128)}, f32[512,64]{1,0:T(8,128)S(1)}, u32[]{:S(2)}) copy-start(f32[512,64]{1,0:T(8,128)S(1)} %get-tuple-element.233) | copy-start | bytes 393220
  194.3 19.1 %copy-start.55 = (f32[512,512]{1,0:T(8,128)S(1)}, f32[512,512]{1,0:T(8,128)}, u32[]{:S(2)}) copy-start(f32[512,512]{1,0:T(8,128)} %get-tuple-element.172) | copy-start | bytes 3145732
  204.6 8.8 copy-start.14
  205.9 11.2 copy-start.5
  373.1 43.2 %reduce-scatter.37.cloned.1.call-start = ((), (), s32[]{:S(2)}) async-start(), calls=%async_computation.25 | async-start | bytes 786432 | tf_op jit(solution)/shard_map/reduce_scatter | solution.py:911
  387.6 215.0 %reduce-scatter.43.cloned.1.call-start = ((), (), s32[]{:S(2)}) async-start(), calls=%async_computation.28 | async-start | bytes 786432 | tf_op jit(solution)/shard_map/reduce_scatter | solution.py:914
  392.5 8.5 copy-start.6
  409.8 7.7 copy-start.15
  418.9 127.2 %copy-start.56 = (bf16[1,512,2,128]{3,2,1,0:T(2,128)(2,1)}, bf16[1,512,2,128]{3,2,1,0:T(2,128)(2,1)S(1)}, u32[]{:S(2)}) copy-start(bf16[1,512,2,128]{3,2,1,0:T(2,128)(2,1)S(1)} %copy.348) | copy-start | bytes 786436
  561.5 43.0 %reduce-scatter.41.cloned.1.call-start = ((), (), s32[]{:S(2)}) async-start(), calls=%async_computation.27 | async-start | bytes 786432 | tf_op jit(solution)/shard_map/reduce_scatter | solution.py:911
  561.5 9.1 copy-start.47
  561.5 9.1 copy-start.49
  572.8 236.8 %reduce-scatter.77.cloned.1.call-start = ((), (), s32[]{:S(2)}) async-start(), calls=%async_computation.45 | async-start | bytes 589824
  576.0 234.7 %reduce-scatter.81.cloned.1.call-start = ((), (), s32[]{:S(2)}) async-start(), calls=%async_computation.47 | async-start | bytes 73728
  583.5 7.7 copy-start.9
  583.5 7.6 copy-start.73
  589.6 221.8 %reduce-scatter.79.cloned.1.call-start = ((), (), s32[]{:S(2)}) async-start(), calls=%async_computation.46 | async-start | bytes 1179648
  591.1 221.9 %reduce-scatter.75.cloned.1.call-start = ((), (), s32[]{:S(2)}) async-start(), calls=%async_computation.44 | async-start | bytes 589824
  592.9 221.7 %all-reduce.15.cloned.1.call-start = ((), (), s32[]{:S(2)}) async-start(), calls=%async_computation.24 | async-start | bytes 4194304 | tf_op jit(solution)/shard_map/psum | solution.py:984
  593.5 223.6 %reduce-scatter.83.cloned.1.call-start = ((), (), s32[]{:S(2)}) async-start(), calls=%async_computation.48 | async-start | bytes 73728
  597.4 8.3 copy-start.22
  597.4 8.3 copy-start.62
  597.4 8.3 copy-start.70
  608.5 125.3 %copy-start.59 = (bf16[1,512,2,128]{1,3,2,0:T(8,128)(2,1)S(1)}, bf16[1,512,2,128]{1,3,2,0:T(8,128)(2,1)}, u32[]{:S(2)}) copy-start(bf16[1,512,2,128]{1,3,2,0:T(8,128)(2,1)} %reduce-scatter.39.cloned.1.call-done) | copy-start | bytes 786436
  732.3 98.2 %reduce-scatter.73.cloned.1.call-start = ((), (), s32[]{:S(2)}) async-start(), calls=%async_computation.43 | async-start | bytes 1179648
  733.8 127.0 %reduce-scatter.55.cloned.1.call-start = ((), (), s32[]{:S(2)}) async-start(), calls=%async_computation.34 | async-start | bytes 1179648 | tf_op jit(solution)/shard_map/reduce_scatter | solution.py:990
  737.4 162.7 %reduce-scatter.53.cloned.1.call-start = ((), (), s32[]{:S(2)}) async-start(), calls=%async_computation.33 | async-start | bytes 1179648 | tf_op jit(solution)/shard_map/reduce_scatter | solution.py:990
  739.5 200.8 %reduce-scatter.51.cloned.1.call-start = ((), (), s32[]{:S(2)}) async-start(), calls=%async_computation.32 | async-start | bytes 1179648 | tf_op jit(solution)/shard_map/reduce_scatter | solution.py:990
  742.9 236.8 %reduce-scatter.49.cloned.1.call-start = ((), (), s32[]{:S(2)}) async-start(), calls=%async_computation.31 | async-start | bytes 1179648 | tf_op jit(solution)/shard_map/reduce_scatter | solution.py:990
  745.2 279.9 %reduce-scatter.59.cloned.1.call-start = ((), (), s32[]{:S(2)}) async-start(), calls=%async_computation.36 | async-start | bytes 2359296 | tf_op jit(solution)/shard_map/reduce_scatter | solution.py:990
  749.5 320.5 %reduce-scatter.57.cloned.1.call-start = ((), (), s32[]{:S(2)}) async-start(), calls=%async_computation.35 | async-start | bytes 2359296 | tf_op jit(solution)/shard_map/reduce_scatter | solution.py:990
  753.8 361.5 %reduce-scatter.47.cloned.1.call-start = ((), (), s32[]{:S(2)}) async-start(), calls=%async_computation.30 | async-start | bytes 2359296 | tf_op jit(solution)/shard_map/reduce_scatter | solution.py:990
  758.2 402.2 %reduce-scatter.45.cloned.1.call-start = ((), (), s32[]{:S(2)}) async-start(), calls=%async_computation.29 | async-start | bytes 2359296 | tf_op jit(solution)/shard_map/reduce_scatter | solution.py:990
  761.0 464.9 %reduce-scatter.71.cloned.1.call-start = ((), (), s32[]{:S(2)}) async-start(), calls=%async_computation.42 | async-start | bytes 7077888 | tf_op jit(solution)/shard_map/reduce_scatter | solution.py:990
  769.4 521.5 %reduce-scatter.69.cloned.1.call-start = ((), (), s32[]{:S(2)}) async-start(), calls=%async_computation.41 | async-start | bytes 7077888 | tf_op jit(solution)/shard_map/reduce_scatter | solution.py:990
  777.7 578.7 %reduce-scatter.63.cloned.1.call-start = ((), (), s32[]{:S(2)}) async-start(), calls=%async_computation.38 | async-start | bytes 7077888 | tf_op jit(solution)/shard_map/reduce_scatter | solution.py:990
  786.0 635.5 %reduce-scatter.61.cloned.1.call-start = ((), (), s32[]{:S(2)}) async-start(), calls=%async_computation.37 | async-start | bytes 7077888 | tf_op jit(solution)/shard_map/reduce_scatter | solution.py:990
  794.3 692.8 %reduce-scatter.67.cloned.1.call-start = ((), (), s32[]{:S(2)}) async-start(), calls=%async_computation.40 | async-start | bytes 7077888 | tf_op jit(solution)/shard_map/reduce_scatter | solution.py:990
  802.7 749.3 %reduce-scatter.65.cloned.1.call-start = ((), (), s32[]{:S(2)}) async-start(), calls=%async_computation.39 | async-start | bytes 7077888 | tf_op jit(solution)/shard_map/reduce_scatter | solution.py:990
  1421.6 133.8 %copy-start.43 = (bf16[1,512,2048]{2,1,0:T(8,128)(2,1)S(1)}, bf16[1,512,2048]{2,1,0:T(8,128)(2,1)}, u32[]{:S(2)}) copy-start(bf16[1,512,2048]{2,1,0:T(8,128)(2,1)} %all-reduce.15.cloned.1.call-done) | copy-start | bytes 6291460
  (56 other events, 211.2 us)
Sparse Core Ops, SparseCore 0:
  373.3 14.8 reduce-scatter.38
  390.4 14.5 reduce-scatter.36
  561.6 14.8 reduce-scatter.42
  579.2 14.5 reduce-scatter.40
  597.0 34.1 reduce-scatter.76
  634.1 33.1 reduce-scatter.80
  671.4 36.0 reduce-scatter.78
  710.8 34.1 reduce-scatter.74
  748.0 33.1 reduce-scatter.82
  785.1 36.0 reduce-scatter.72
  824.7 36.0 reduce-scatter.54
  864.1 36.0 reduce-scatter.52
  904.2 36.0 reduce-scatter.50
  943.6 36.0 reduce-scatter.48
  983.8 41.2 reduce-scatter.58
  1028.8 41.2 reduce-scatter.56
  1074.1 41.2 reduce-scatter.46
  1119.1 41.2 reduce-scatter.44
  1164.1 61.7 reduce-scatter.70
  1229.1 61.7 reduce-scatter.68
  1294.7 61.7 reduce-scatter.62
  1359.8 61.7 reduce-scatter.60
  1425.3 61.7 reduce-scatter.66
  1490.3 61.7 reduce-scatter.64
Sparse Core Ops, SparseCore 1:
  595.7 130.1 all-reduce.14

commit v2 on v1

v2 whole, which is shorter than its diff:
```python
from functools import partial

import jax
import jax.numpy as jnp
from jax import lax
from jax.experimental import pallas as pl
from jax.experimental.pallas import tpu as pltpu
from jax.sharding import PartitionSpec as P

HD = 128
LAYERS = 2
LANES = 128

epsilon = 1e-06
theta = 1000000.0
masked = -1000000000.0

BF = jnp.bfloat16
F32 = jnp.float32
ANY = pl.BlockSpec(memory_space=pl.ANY)
WHOLE = pl.BlockSpec(memory_space=pltpu.VMEM)
MESH = pl.DeviceIdType.MESH

BLOCKS = 8
PIECES = 2
GROUP = 4
STRIP = 16
VMEM_LIMIT = 63 * 1024 * 1024


def rms_scale(values, gain):
    return values * lax.rsqrt(jnp.mean(values * values, axis=-1, keepdims=True) + epsilon) * gain


def rotary_tables(positions, width):
    counter = jnp.arange(width // 2, dtype=jnp.float32)
    frequency = theta ** (-2.0 * counter / width)
    angles = positions.astype(jnp.float32)[:, None] * frequency[None, :]
    return (jnp.cos(angles), jnp.sin(angles))


def rotate(values, cos_table, sin_table):
    width = values.shape[-1]
    leading = values[..., : width // 2]
    trailing = values[..., width // 2 :]
    cos_part = cos_table[:, None, :]
    sin_part = sin_table[:, None, :]
    return jnp.concatenate(
        [leading * cos_part - trailing * sin_part, trailing * cos_part + leading * sin_part],
        axis=-1,
    )


def rotated_norm(raw, gain, cos_table, sin_table):
    return rotate(rms_scale(raw, gain), cos_table, sin_table)


def gated(attended, logits):
    return attended * jax.nn.sigmoid(logits)[:, :, None]


def matmul(left, right):
    return jnp.dot(left, right, preferred_element_type=F32)


def weight_product(left, right):
    return lax.dot_general(left, right, (((0,), (0,)), ((), ())), preferred_element_type=F32)


def back_product(gradient, weight):
    return lax.dot_general(gradient, weight, (((1,), (1,)), ((), ())), preferred_element_type=F32)


def masked_scores(query, keys, prefix, query_pos, key_pos):
    scale = query.shape[-1] ** (-0.5)
    scores = jnp.einsum("qkgd,tkd->kgqt", query, keys, preferred_element_type=F32) * scale
    visible = (key_pos[None, :] <= query_pos[:, None]) | (key_pos[None, :] < prefix)
    return jnp.where(visible, scores, masked)


def attend_forward(inputs, query_pos, key_pos):
    query, keys, values, prefix = inputs
    scores = masked_scores(query, keys, prefix, query_pos, key_pos)
    highest = jnp.max(scores, axis=-1, keepdims=True)
    logsum = highest + jnp.log(jnp.sum(jnp.exp(scores - highest), axis=-1, keepdims=True))
    weights = jnp.exp(scores - logsum).astype(BF)
    attended = jnp.einsum("kgqt,tkd->qkgd", weights, values, preferred_element_type=F32)
    return (attended, logsum)


def attend_backward(inputs, query_pos, key_pos):
    query, keys, values, prefix, logsum, out_grad = inputs
    scale = query.shape[-1] ** (-0.5)
    weights = jnp.exp(masked_scores(query, keys, prefix, query_pos, key_pos) - logsum)
    weight_grad = jnp.einsum("qkgd,tkd->kgqt", out_grad, values, preferred_element_type=F32)
    score_grad = weights * (weight_grad - jnp.sum(weights * weight_grad, axis=-1, keepdims=True))
    score_low = score_grad.astype(BF)
    query_grad = jnp.einsum("kgqt,tkd->qkgd", score_low, keys, preferred_element_type=F32) * scale
    key_grad = jnp.einsum("kgqt,qkgd->tkd", score_low, query, preferred_element_type=F32) * scale
    value_grad = jnp.einsum(
        "kgqt,qkgd->tkd", weights.astype(BF), out_grad, preferred_element_type=F32
    )
    return (query_grad, key_grad, value_grad)


def loop(count, body):
    def step(i, carry):
        body(i)
        return carry

    lax.fori_loop(0, count, step, 0)


def rows_of(r, block):
    return pl.ds(pl.multiple_of(r * block, block), block)


def columns(j, width):
    return pl.ds(pl.multiple_of(j * width, width), width)


def greet(targets, extra, has_extra):
    barrier = pltpu.get_barrier_semaphore()
    for target in targets:
        pl.semaphore_signal(barrier, inc=1, device_id=target, device_id_type=MESH)

    @pl.when(has_extra)
    def _():
        pl.semaphore_signal(barrier, inc=1, device_id=extra, device_id_type=MESH)
        pl.semaphore_wait(barrier, len(targets) + 1)

    @pl.when(jnp.logical_not(has_extra))
    def _():
        pl.semaphore_wait(barrier, len(targets))


class Chain:
    def __init__(self, size):
        self.size = size
        self.spot = lax.axis_index("tensor")
        half = size // 2
        on_left = self.spot < half
        self.end = (self.spot == 0) | (self.spot == size - 1)
        self.inner = jnp.logical_not(self.end)
        self.mid = (self.spot == half - 1) | (self.spot == half)
        self.outer = jnp.logical_not(self.mid)
        self.first_mid = self.spot == half - 1
        self.inward = {"tensor": jnp.where(on_left, self.spot + 1, self.spot - 1)}
        self.outward = {"tensor": jnp.where(on_left, self.spot - 1, self.spot + 1)}

    def greet(self, others=()):
        greet([self.inward, *others], self.outward, self.inner)


class Sum:
    def __init__(self, chain, refs, rows, width):
        self.chain = chain
        self.part, self.landed, self.spread, self.s_in, self.r_in, self.s_out, self.r_out = refs
        self.block = rows // BLOCKS
        self.piece = width // PIECES

    @staticmethod
    def scratch(rows, width):
        return [
            pltpu.VMEM((rows, width), BF),
            pltpu.VMEM((2, rows, width), BF),
            pltpu.VMEM((rows, width), BF),
            pltpu.SemaphoreType.DMA((BLOCKS, PIECES)),
            pltpu.SemaphoreType.DMA((2, BLOCKS, PIECES)),
            pltpu.SemaphoreType.DMA((BLOCKS,)),
            pltpu.SemaphoreType.DMA((BLOCKS,)),
        ]

    def hop(self, r, p, slot):
        where = (rows_of(r, self.block), columns(p, self.piece))
        return pltpu.make_async_remote_copy(
            src_ref=self.part.at[where],
            dst_ref=self.landed.at[(slot,) + where],
            send_sem=self.s_in.at[r, p],
            recv_sem=self.r_in.at[slot, r, p],
            device_id=self.chain.inward,
            device_id_type=MESH,
        )

    def out_hop(self, r):
        at = rows_of(r, self.block)
        return pltpu.make_async_remote_copy(
            src_ref=self.spread.at[at],
            dst_ref=self.spread.at[at],
            send_sem=self.s_out.at[r],
            recv_sem=self.r_out.at[r],
            device_id=self.chain.outward,
            device_id_type=MESH,
        )

    def offer(self, g):
        @pl.when(self.chain.end)
        def _():
            def one(k):
                for p in range(PIECES):
                    self.hop(g * GROUP + k, p, 0).start()

            loop(GROUP, one)

    def relay(self, r):
        @pl.when(self.chain.inner)
        def _():
            for p in range(PIECES):
                self.hop(r, p, 0).wait_recv()
                col = columns(p, self.piece)

                def strip(i, col=col):
                    at = pl.ds(pl.multiple_of(r * self.block + i * STRIP, STRIP), STRIP)
                    total = self.part[at, col].astype(F32) + self.landed[0, at, col].astype(F32)
                    self.part[at, col] = total.astype(BF)

                loop(self.block // STRIP, strip)

                @pl.when(self.chain.mid)
                def _(p=p):
                    self.hop(r, p, 1).start()

                @pl.when(self.chain.outer)
                def _(p=p):
                    self.hop(r, p, 0).start()

    def finish(self, r, make):
        @pl.when(self.chain.mid)
        def _():
            for p in range(PIECES):
                self.hop(r, p, 1).wait_recv()

            def strip(i):
                at = pl.ds(pl.multiple_of(r * self.block + i * STRIP, STRIP), STRIP)
                total = self.part[at, :].astype(F32) + self.landed[1, at, :].astype(F32)
                self.spread[at, :] = make(at, total)

            loop(self.block // STRIP, strip)
            self.out_hop(r).start()

    def receive(self, g):
        @pl.when(self.chain.outer)
        def _():
            def one(k):
                self.out_hop(g * GROUP + k).wait_recv()

                @pl.when(self.chain.inner)
                def _():
                    self.out_hop(g * GROUP + k).start()

            loop(GROUP, one)

    def close(self):
        def block(r):
            for p in range(PIECES):
                self.hop(r, p, 0).wait_send()

            @pl.when(self.chain.inner)
            def _():
                self.out_hop(r).wait_send()

        loop(BLOCKS, block)


PARTS = GROUP
GROUPS = BLOCKS // GROUP
STEPS = 2 * BLOCKS + 1


def two_sums(s, first, second, made_one, between, ahead, made_two, after):
    @pl.when(s < BLOCKS)
    def _():
        first.relay(s)

    @pl.when((s >= 1) & (s <= BLOCKS))
    def _():
        first.finish(s - 1, made_one)

    @pl.when((s >= GROUP) & (s < BLOCKS + GROUP))
    def _():
        part = lax.rem(s - GROUP, PARTS)
        group = lax.div(s - GROUP, PARTS)

        @pl.when(part == 0)
        def _():
            first.receive(group)

        between(group, part)

    @pl.when((s >= BLOCKS) & (s < 2 * BLOCKS))
    def _():
        second.relay(s - BLOCKS)

    @pl.when((s >= BLOCKS + 1) & (s < STEPS))
    def _():
        @pl.when(lax.rem(s - BLOCKS - 1, GROUP) == 0)
        def _():
            ahead(lax.div(s - BLOCKS - 1, GROUP))

        second.finish(s - BLOCKS - 1, made_two)

        @pl.when(lax.rem(s - BLOCKS, GROUP) == 0)
        def _():
            group = lax.div(s - BLOCKS, GROUP) - 1
            second.receive(group)
            after(group)


def back_norm(value, gain, grad):
    spread = lax.rsqrt(jnp.mean(value * value, axis=-1, keepdims=True) + epsilon)
    scaled = grad * gain
    pulled = jnp.mean(scaled * value, axis=-1, keepdims=True)
    terms = grad * value * spread
    return spread * scaled - value * (spread * spread * spread * pulled), terms


def fold(terms):
    folded = terms[:8]
    for k in range(8, terms.shape[0], 8):
        folded = folded + terms[k : k + 8]
    return folded


def load_all(pairs, sems):
    copies = [pltpu.make_async_copy(src, dst, sems.at[k]) for k, (src, dst) in enumerate(pairs)]
    for copy in copies:
        copy.start()
    return copies


def wait_all(copies):
    for copy in copies:
        copy.wait()


def wide(width):
    return 512 if width % 512 == 0 else 256


def fill(target, at, make):
    width = target.shape[1]
    tile = wide(width)

    def one(p):
        col = columns(p, tile)
        target[at, col] = make(col).astype(target.dtype)

    loop(width // tile, one)


def flip(value, bit):
    return value + bit * (1 - 2 * lax.rem(lax.div(value, bit), 2))


class Plane:
    def __init__(self, dp_size, ctx_size):
        self.count = dp_size * ctx_size
        self.ctx_size = ctx_size
        self.me = lax.axis_index("dp") * ctx_size + lax.axis_index("ctx")
        bits = [1 << k for k in range(self.count.bit_length() - 1)]
        near = [bit for bit in bits if bit >= ctx_size][:1]
        rest = [bit for bit in bits if bit not in near]
        self.bits = bits
        self.orders = (near + rest, near + rest[1:] + rest[:1])

    def partner(self, bit):
        other = flip(self.me, bit)
        return {"dp": lax.div(other, self.ctx_size), "ctx": lax.rem(other, self.ctx_size)}

    def partners(self):
        return [self.partner(bit) for bit in self.bits]


class Scatter:
    SLOTS = (2, 4, 4, 4)
    KEPT = (1, 3, 3, 3)
    RESULTS = 2
    LAGS = (0, 1, 4, 7, 10, 13)

    def __init__(self, plane, refs, groups, share, tile):
        self.plane = plane
        self.groups = groups
        self.share, self.tile = share, tile
        self.stages = len(plane.bits)
        self.units = sum(group[4] for group in groups)
        self.refs = [refs[6 * k : 6 * k + 6] for k in range(self.stages)]
        self.made, self.out_sem, self.load_sem = refs[6 * self.stages :]
        self.steps = self.units + self.LAGS[self.stages]

    @classmethod
    def scratch(cls, count, share, tile):
        found = []
        blocks = count // 2
        for k in range(count.bit_length() - 1):
            slots = cls.SLOTS[k]
            found += [
                pltpu.VMEM((depth, blocks, share, tile), BF) for depth in (slots, cls.KEPT[k], slots)
            ]
            found += [
                pltpu.SemaphoreType.DMA((slots,)),
                pltpu.SemaphoreType.DMA((slots,)),
                pltpu.SemaphoreType.REGULAR((slots,)),
            ]
            blocks //= 2
        return found + [
            pltpu.VMEM((cls.RESULTS, share, tile), BF),
            pltpu.SemaphoreType.DMA((cls.RESULTS,)),
            pltpu.SemaphoreType.DMA((2,)),
        ]

    def partner(self, stage, u):
        odd = lax.rem(u, 2) == 1
        even_one, odd_one = (self.plane.partner(order[stage]) for order in self.plane.orders)
        return {axis: jnp.where(odd, odd_one[axis], even_one[axis]) for axis in even_one}

    def copy(self, stage, u):
        send, unused, land, s_sem, r_sem, unused_credit = self.refs[stage]
        slot = lax.rem(u, self.SLOTS[stage])
        return pltpu.make_async_remote_copy(
            src_ref=send.at[slot],
            dst_ref=land.at[slot],
            send_sem=s_sem.at[slot],
            recv_sem=r_sem.at[slot],
            device_id=self.partner(stage, u),
            device_id_type=MESH,
        )

    def ready(self, stage, u):
        @pl.when(u >= self.SLOTS[stage])
        def _():
            self.copy(stage, u - self.SLOTS[stage]).wait_send()

    def push(self, stage, u):
        @pl.when(u >= self.SLOTS[stage])
        def _():
            pl.semaphore_wait(self.refs[stage][5].at[lax.rem(u, self.SLOTS[stage])], 1)

        self.copy(stage, u).start()

    def product(self, u):
        send, keep = self.refs[0][:2]
        slot, spot = lax.rem(u, self.SLOTS[0]), lax.rem(u, self.KEPT[0])
        odd = lax.rem(u, 2)
        orders = self.plane.orders
        blocks = self.plane.count // 2
        first = 0
        for whole, parts, by_rows, unused, count, loads in self.groups:

            @pl.when((u >= first) & (u < first + count))
            def _(whole=whole, parts=parts, by_rows=by_rows, first=first, loads=loads):
                if loads:

                    @pl.when(u == first)
                    def _():
                        wait_all(load_all(loads, self.load_sem))

                col = columns(u - first, self.tile)

                def one(i):
                    far = lax.rem(i, 2)
                    j = lax.div(i, 2)
                    owner = flip(self.plane.me, orders[0][0]) * far + self.plane.me * (1 - far)
                    rest = j
                    for bits in reversed(tuple(zip(*orders))[1:]):
                        low = lax.rem(rest, 2)
                        rest = lax.div(rest, 2)
                        turned = flip(owner, bits[0]) * (1 - odd) + flip(owner, bits[1]) * odd
                        owner = turned * low + owner * (1 - low)
                    at = columns(owner, self.share)
                    if by_rows:
                        made = weight_product(whole[:, at], parts[:, col])
                    else:
                        made = weight_product(parts[:, col], whole[:, at])
                    made = made.astype(BF)

                    @pl.when(far == 1)
                    def _():
                        send[slot, j] = made

                    @pl.when(far == 0)
                    def _():
                        keep[spot, j] = made

                loop(2 * blocks, one)

            first += count

    def merge(self, stage, u):
        unused, keep, land = self.refs[stage][:3]
        slots = self.SLOTS[stage]
        slot, spot = lax.rem(u, slots), lax.rem(u, self.KEPT[stage])
        self.copy(stage, u).wait_recv()
        half = (self.plane.count // 2) >> (stage + 1)
        last = stage == self.stages - 1
        if not last:
            self.ready(stage + 1, u)
            send_on, keep_on = self.refs[stage + 1][:2]
            slot_on = lax.rem(u, self.SLOTS[stage + 1])
            spot_on = lax.rem(u, self.KEPT[stage + 1])

            def one(j):
                far = keep[spot, half + j].astype(F32) + land[slot, half + j].astype(F32)
                send_on[slot_on, j] = far.astype(BF)
                near = keep[spot, j].astype(F32) + land[slot, j].astype(F32)
                keep_on[spot_on, j] = near.astype(BF)

            loop(half, one)
            self.push(stage + 1, u)
        else:
            place = lax.rem(u, self.RESULTS)

            @pl.when(u >= self.RESULTS)
            def _():
                self.results(u - self.RESULTS, lambda copy: copy.wait())

            total = keep[spot, 0].astype(F32) + land[slot, 0].astype(F32)
            self.made[place] = total.astype(BF)
            self.results(u, lambda copy: copy.start())

        @pl.when(u + slots < self.units)
        def _():
            pl.semaphore_signal(
                self.refs[stage][5].at[slot],
                inc=1,
                device_id=self.partner(stage, u),
                device_id_type=MESH,
            )

    def results(self, u, act):
        place = lax.rem(u, self.RESULTS)
        first = 0
        for unused, unused_parts, by_rows, out, count, unused_loads in self.groups:

            @pl.when((u >= first) & (u < first + count))
            def _(by_rows=by_rows, out=out, first=first):
                if by_rows:
                    at = (slice(None), columns(u - first, self.tile))
                else:
                    at = (rows_of(u - first, self.tile), slice(None))
                act(pltpu.make_async_copy(self.made.at[place], out.at[at], self.out_sem.at[place]))

            first += count

    def tick(self, i):
        for stage in reversed(range(self.stages)):
            u = i - self.LAGS[stage + 1]

            @pl.when((u >= 0) & (u < self.units))
            def _(stage=stage, u=u):
                self.merge(stage, u)

        @pl.when(i < self.units)
        def _():
            self.ready(0, i)
            self.product(i)
            self.push(0, i)

    def close(self):
        for stage in range(self.stages):
            for k in range(max(0, self.units - self.SLOTS[stage]), self.units):
                self.copy(stage, jnp.int32(k)).wait_send()
        for k in range(max(0, self.units - self.RESULTS), self.units):
            self.results(jnp.int32(k), lambda copy: copy.wait())


class Total:
    def __init__(self, plane, size, refs, own):
        self.plane, self.own = plane, own
        self.value, self.land, self.s_sem, self.r_sem = refs
        spot = lax.axis_index("tensor")
        bits = [1 << k for k in range(size.bit_length() - 1)]
        self.targets = [plane.partner(bit) for bit in plane.bits]
        self.across = [{"tensor": flip(spot, bit)} for bit in bits]
        self.stages = len(self.targets) + len(bits)

    @staticmethod
    def scratch(rows, width, stages):
        return [
            pltpu.VMEM((stages, rows, width), F32),
            pltpu.VMEM((stages, rows, width), F32),
            pltpu.SemaphoreType.DMA((stages,)),
            pltpu.SemaphoreType.DMA((stages,)),
        ]

    def copy(self, k):
        count = len(self.targets)
        rows = slice(None) if k < count else pl.ds(0, self.own)
        return pltpu.make_async_remote_copy(
            src_ref=self.value.at[k, rows],
            dst_ref=self.land.at[k, rows],
            send_sem=self.s_sem.at[k],
            recv_sem=self.r_sem.at[k],
            device_id=(self.targets + self.across)[k],
            device_id_type=MESH,
        )

    def start(self, k):
        if k > 0:
            self.copy(k - 1).wait_recv()
            rows = slice(None) if k - 1 < len(self.targets) else pl.ds(0, self.own)
            if k - 1 >= len(self.targets):
                self.value[k] = self.value[k - 1]
            self.value[k, rows] = self.value[k - 1, rows] + self.land[k - 1, rows]
        self.copy(k).start()

    def finish(self, target):
        last = self.stages - 1
        self.copy(last).wait_recv()
        rows = pl.ds(0, self.own)
        target[...] = self.value[last]
        target[rows] = self.value[last, rows] + self.land[last, rows]
        for k in range(self.stages):
            self.copy(k).wait_send()


def forward_kernel(
    size, depth, rows, width,
    mixed, stream, wo, feed_gain, wg, wu, wd, next_gain, wq, wk, wv, gh,
    middle_o, two_o, slope_o, silu_o, hidden_o, x_o, normed_o, q_o, k_o, v_o, logit_o,
    *scratch,
):
    (wo_v, wg_v, wu_v, wd_v, wq_v, wk_v, wv_v, x_v, middle_v, slope_v, silu_v, hidden_v, q_v, k_v,
     v_v, logit_v, load_sem, out_sem) = scratch[:18]
    chain = Chain(size)
    one = Sum(chain, scratch[18:25], rows, width)
    two = Sum(chain, scratch[25:32], rows, width)
    span = one.block * GROUP
    loads = load_all(
        [(wo.at[depth], wo_v), (stream, x_v), (wg.at[depth], wg_v), (wu.at[depth], wu_v),
         (wd.at[depth], wd_v), (wq.at[depth + 1], wq_v), (wk.at[depth + 1], wk_v),
         (wv.at[depth + 1], wv_v)],
        load_sem,
    )
    chain.greet()
    tile = wg_v.shape[1] // (PARTS - 1)
    gain_one = feed_gain[depth : depth + 1, :]
    gain_two = next_gain[depth + 1 : depth + 2, :]

    def out(k, g, src, dst):
        at = rows_of(g, span)
        return pltpu.make_async_copy(src.at[at], dst.at[at], out_sem.at[k, g])

    loads[0].wait()

    def start(g):
        at = rows_of(g, span)
        fill(one.part, at, lambda col: matmul(mixed[at, :], wo_v[:, col]))
        one.offer(g)

    loop(GROUPS, start)
    wait_all(loads[1:5])

    def made_one(at, total):
        value = x_v[at, :].astype(F32) + total
        middle_v[at, :] = value
        return rms_scale(value, gain_one).astype(BF)

    def between(g, part):
        at = rows_of(g, span)

        @pl.when(part == 0)
        def _():
            out(1, g, one.spread, two_o).start()

            @pl.when(chain.mid)
            def _():
                out(0, g, middle_v, middle_o).start()

        @pl.when(part < PARTS - 1)
        def _():
            col = columns(part, tile)
            gate = matmul(one.spread[at, :], wg_v[:, col])
            up = matmul(one.spread[at, :], wu_v[:, col])
            sig = jax.nn.sigmoid(gate)
            act = gate * sig
            hidden_v[at, col] = (act * up).astype(BF)
            silu_v[at, col] = act.astype(BF)
            slope_v[at, col] = (up * (sig * (1.0 + gate * (1.0 - sig)))).astype(BF)

        @pl.when(part == PARTS - 1)
        def _():
            fill(two.part, at, lambda col: matmul(hidden_v[at, :], wd_v[:, col]))
            two.offer(g)
            out(2, g, slope_v, slope_o).start()
            out(3, g, silu_v, silu_o).start()
            out(4, g, hidden_v, hidden_o).start()

    def ahead(g):
        @pl.when(g == 0)
        def _():
            wait_all(loads[5:])

        @pl.when(chain.mid)
        def _():
            out(0, g, middle_v, middle_o).wait()

    def made_two(at, total):
        value = middle_v[at, :] + total
        middle_v[at, :] = value
        return rms_scale(value, gain_two).astype(BF)

    def after(g):
        at = rows_of(g, span)

        @pl.when(chain.mid)
        def _():
            out(5, g, middle_v, x_o).start()

        q_v[at, :] = matmul(two.spread[at, :], wq_v[...])
        out(7, g, q_v, q_o).start()
        k_v[at, :] = matmul(two.spread[at, :], wk_v[...])
        out(8, g, k_v, k_o).start()
        v_v[at, :] = matmul(two.spread[at, :], wv_v[...]).astype(BF)
        out(9, g, v_v, v_o).start()
        logit_v[at, :] = matmul(two.spread[at, :], gh[...])
        out(10, g, logit_v, logit_o).start()
        out(6, g, two.spread, normed_o).start()

    loop(STEPS, lambda s: two_sums(s, one, two, made_one, between, ahead, made_two, after))
    one.close()
    two.close()

    def drain(g):
        @pl.when(chain.mid)
        def _():
            out(5, g, middle_v, x_o).wait()

        for k, src, dst in (
            (1, one.spread, two_o), (2, slope_v, slope_o), (3, silu_v, silu_o),
            (4, hidden_v, hidden_o), (6, two.spread, normed_o), (7, q_v, q_o),
            (8, k_v, k_o), (9, v_v, v_o), (10, logit_v, logit_o),
        ):
            out(k, g, src, dst).wait()

    loop(GROUPS, drain)


def turn_kernel(
    size, depth, rows, width,
    mixed, x_in, cot, wo, feed_gain, wg, wu, wd,
    two_o, hidden_o, down_o, gate_o, up_o, grad_o, low_o, mixed_o, gain_o,
    *scratch,
):
    (wo_v, wg_v, wu_v, wd_v, middle_v, cot_v, hidden_v, gate_v, up_v, mixed_v, down_v, gain_v,
     load_sem, out_sem) = scratch[:14]
    chain = Chain(size)
    one = Sum(chain, scratch[14:21], rows, width)
    two = Sum(chain, scratch[21:28], rows, width)
    span = one.block * GROUP
    loads = load_all(
        [(wo.at[depth], wo_v), (x_in, middle_v), (cot, cot_v), (wg.at[depth], wg_v),
         (wu.at[depth], wu_v), (wd.at[depth], wd_v)],
        load_sem,
    )
    chain.greet()
    tile = wg_v.shape[1] // (PARTS - 1)
    gain_one = feed_gain[depth : depth + 1, :]

    def out(k, g, src, dst):
        at = rows_of(g, span)
        return pltpu.make_async_copy(src.at[at], dst.at[at], out_sem.at[k, g])

    loads[0].wait()

    def start(g):
        at = rows_of(g, span)
        fill(one.part, at, lambda col: matmul(mixed[at, :], wo_v[:, col]))
        one.offer(g)

    loop(GROUPS, start)
    gain_v[...] = jnp.zeros_like(gain_v)
    wait_all(loads[1:])

    def made_one(at, total):
        value = middle_v[at, :] + total
        middle_v[at, :] = value
        return rms_scale(value, gain_one).astype(BF)

    def between(g, part):
        at = rows_of(g, span)

        @pl.when(part == 0)
        def _():
            out(0, g, one.spread, two_o).start()

        @pl.when(part < PARTS - 1)
        def _():
            col = columns(part, tile)
            gate = matmul(one.spread[at, :], wg_v[:, col])
            sig = jax.nn.sigmoid(gate)
            act = gate * sig
            slope = sig * (1.0 + gate * (1.0 - sig))
            up = matmul(one.spread[at, :], wu_v[:, col])
            hidden_v[at, col] = (act * up).astype(BF)
            pulled = back_product(cot_v[at, :], wd_v[col, :])
            gate_v[at, col] = (pulled * up * slope).astype(BF)
            up_v[at, col] = (pulled * act).astype(BF)

        @pl.when(part == PARTS - 1)
        def _():
            fill(
                two.part,
                at,
                lambda col: back_product(gate_v[at, :], wg_v[col, :])
                + back_product(up_v[at, :], wu_v[col, :]),
            )
            two.offer(g)
            out(1, g, hidden_v, hidden_o).start()
            out(2, g, gate_v, gate_o).start()
            out(3, g, up_v, up_o).start()

    def ahead(g):
        at = rows_of(g, span)
        share = jnp.where(chain.first_mid, 1.0, 0.0)

        @pl.when(chain.first_mid)
        def _():
            fill(down_v, at, lambda col: matmul(hidden_v[at, :], wd_v[:, col]) + middle_v[at, col])

        @pl.when(jnp.logical_not(chain.first_mid))
        def _():
            fill(down_v, at, lambda col: matmul(hidden_v[at, :], wd_v[:, col]))

        out(4, g, down_v, down_o).start()

    def made_two(at, total):
        pulled, terms = back_norm(middle_v[at, :], gain_one, total)
        gain_v[...] += fold(terms)
        value = cot_v[at, :].astype(F32) + pulled
        middle_v[at, :] = value
        return value.astype(BF)

    def after(g):
        at = rows_of(g, span)

        @pl.when(chain.mid)
        def _():
            out(5, g, middle_v, grad_o).start()

        out(6, g, two.spread, low_o).start()
        mixed_v[at, :] = back_product(two.spread[at, :], wo_v[...])
        out(7, g, mixed_v, mixed_o).start()

    loop(STEPS, lambda s: two_sums(s, one, two, made_one, between, ahead, made_two, after))

    @pl.when(jnp.logical_not(chain.first_mid))
    def _():
        gain_v[...] = jnp.zeros_like(gain_v)

    gain_out = pltpu.make_async_copy(gain_v, gain_o, out_sem.at[8, 0])
    gain_out.start()
    one.close()
    two.close()

    def drain(g):
        @pl.when(chain.mid)
        def _():
            out(5, g, middle_v, grad_o).wait()

        for k, src, dst in (
            (0, one.spread, two_o), (1, hidden_v, hidden_o), (2, gate_v, gate_o),
            (3, up_v, up_o), (4, down_v, down_o), (6, two.spread, low_o), (7, mixed_v, mixed_o),
        ):
            out(k, g, src, dst).wait()

    loop(GROUPS, drain)
    gain_out.wait()


def back_kernel(
    size, plane_sizes, depth, rows, width,
    q_low, k_low, v_low, l_low, gh, x_in, grad_in, attention_gain, wq, wk, wv,
    wd, wg, wu, slope_in, silu_in, middle_in, feed_gain, wo,
    two_in, gate_in, up_in, cot_in, hidden_in, normed_in, low_in, mixed_in,
    gate_o, up_o, first_o, grad_o, low_o, mixed_o, gain_o, feed_gain_o,
    *rest,
):
    made, scratch = rest[:7], rest[7:]
    (wq_v, wk_v, wv_v, wd_v, wg_v, wu_v, wo_v, x_v, grad_v, slope_v, silu_v, gate_v, up_v, mixed_v,
     gain_v, feed_v, whole_v, parts_v, load_sem, row_sem, tile_sem, out_sem) = scratch[:22]
    chain = Chain(size)
    one = Sum(chain, scratch[22:29], rows, width)
    two = Sum(chain, scratch[29:36], rows, width)
    plane = Plane(*plane_sizes)
    share = width // plane.count
    unit = min(256, wk_v.shape[1])
    units_wide, heads_wide, keys_wide = wg_v.shape[1], wq_v.shape[1], wk_v.shape[1]
    parts_heads = parts_v.at[:, pl.ds(0, heads_wide)]
    scatter = Scatter(
        plane, scratch[36:],
        [
            (whole_v, parts_v, True, made[0], units_wide // unit, [(two_in, whole_v), (gate_in, parts_v)]),
            (whole_v, parts_v, True, made[1], units_wide // unit, [(up_in, parts_v)]),
            (whole_v, parts_v, False, made[2], units_wide // unit, [(cot_in, whole_v), (hidden_in, parts_v)]),
            (whole_v, q_low, True, made[3], heads_wide // unit, [(normed_in, whole_v)]),
            (whole_v, k_low, True, made[4], keys_wide // unit, []),
            (whole_v, v_low, True, made[5], keys_wide // unit, []),
            (whole_v, parts_v, False, made[6], heads_wide // unit, [(low_in, whole_v), (mixed_in, parts_heads)]),
        ],
        share, unit,
    )
    span = one.block * GROUP
    below = depth - 1
    loads = load_all(
        [(wq.at[depth], wq_v), (wk.at[depth], wk_v), (wv.at[depth], wv_v), (grad_in, grad_v),
         (wd.at[below], wd_v), (wg.at[below], wg_v), (wu.at[below], wu_v), (wo.at[below], wo_v)],
        load_sem,
    )

    def row_load(src, g, k):
        return pltpu.make_async_copy(src.at[rows_of(g, span)], x_v, row_sem.at[k])

    tile = wg_v.shape[1] // (PARTS - 1)

    def tile_load(src, dst, g, part, k):
        col = columns(part, tile)
        return pltpu.make_async_copy(
            src.at[rows_of(g, span), col], dst.at[:, col], tile_sem.at[k, part]
        )

    row_load(x_in, 0, 0).start()

    def first_tiles(part):
        tile_load(slope_in, slope_v, 0, part, 0).start()
        tile_load(silu_in, silu_v, 0, part, 1).start()

    loop(PARTS - 1, first_tiles)
    chain.greet(plane.partners())
    wait_all(loads[:3])
    gain_one = attention_gain[depth : depth + 1, :]
    gain_two = feed_gain[below : below + 1, :]

    def out(k, g, src, dst, whole=True):
        at = rows_of(g, span)
        return pltpu.make_async_copy(src.at[at] if whole else src, dst.at[at], out_sem.at[k, g])

    def start(g):
        at = rows_of(g, span)
        fill(
            one.part,
            at,
            lambda col: back_product(q_low[at, :], wq_v[col, :])
            + back_product(k_low[at, :], wk_v[col, :])
            + back_product(v_low[at, :], wv_v[col, :])
            + back_product(l_low[at, :], gh[col, :]),
        )
        one.offer(g)

    loop(GROUPS, start)
    gain_v[...] = jnp.zeros_like(gain_v)
    feed_v[...] = jnp.zeros_like(feed_v)
    wait_all(loads[3:])
    row_load(x_in, 0, 0).wait()

    def local(at):
        return pl.ds(pl.multiple_of(lax.rem(at.start, span), STRIP), STRIP)

    def made_one(at, total):
        pulled, terms = back_norm(x_v[local(at), :], gain_one, total)
        gain_v[...] += fold(terms)
        value = grad_v[at, :] + pulled
        grad_v[at, :] = value
        return value.astype(BF)

    def between(g, part):
        at = rows_of(g, span)

        @pl.when(part == 0)
        def _():
            out(0, g, one.spread, first_o).start()

            @pl.when(g < GROUPS - 1)
            def _():
                copy = row_load(x_in, g + 1, 1)
                copy.start()
                copy.wait()

            @pl.when(g > 0)
            def _():
                out(1, g - 1, gate_v, gate_o, False).wait()
                out(2, g - 1, up_v, up_o, False).wait()

        @pl.when(part < PARTS - 1)
        def _():
            col = columns(part, tile)
            tile_load(slope_in, slope_v, g, part, 0).wait()
            tile_load(silu_in, silu_v, g, part, 1).wait()
            pulled = back_product(one.spread[at, :], wd_v[col, :])
            gate_v[:, col] = (pulled * slope_v[:, col].astype(F32)).astype(BF)
            up_v[:, col] = (pulled * silu_v[:, col].astype(F32)).astype(BF)

            @pl.when(g < GROUPS - 1)
            def _():
                tile_load(slope_in, slope_v, g + 1, part, 0).start()
                tile_load(silu_in, silu_v, g + 1, part, 1).start()

        @pl.when(part == PARTS - 1)
        def _():
            fill(
                two.part,
                at,
                lambda col: back_product(gate_v[...], wg_v[col, :])
                + back_product(up_v[...], wu_v[col, :]),
            )
            two.offer(g)
            out(1, g, gate_v, gate_o, False).start()
            out(2, g, up_v, up_o, False).start()

    def ahead(g):
        copy = row_load(middle_in, g, 2)
        copy.start()
        copy.wait()

    def made_two(at, total):
        pulled, terms = back_norm(x_v[local(at), :], gain_two, total)
        feed_v[...] += fold(terms)
        value = grad_v[at, :] + pulled
        grad_v[at, :] = value
        return value.astype(BF)

    def after(g):
        at = rows_of(g, span)

        @pl.when(chain.mid)
        def _():
            out(5, g, grad_v, grad_o).start()

        out(3, g, two.spread, low_o).start()

        @pl.when(g > 0)
        def _():
            out(4, g - 1, mixed_v, mixed_o, False).wait()

        mixed_v[...] = back_product(two.spread[at, :], wo_v[...])
        out(4, g, mixed_v, mixed_o, False).start()

    pace = 3

    def step(s):
        two_sums(s, one, two, made_one, between, ahead, made_two, after)
        begin = lax.div(s * pace, 2)
        stop = lax.div((s + 1) * pace, 2)
        lax.fori_loop(begin, stop, lambda i, carry: (scatter.tick(i), carry)[1], 0)

    loop(max(STEPS, (2 * scatter.steps + pace - 1) // pace), step)

    @pl.when(jnp.logical_not(chain.first_mid))
    def _():
        gain_v[...] = jnp.zeros_like(gain_v)
        feed_v[...] = jnp.zeros_like(feed_v)

    gain_out = pltpu.make_async_copy(gain_v, gain_o, out_sem.at[6, 0])
    feed_out = pltpu.make_async_copy(feed_v, feed_gain_o, out_sem.at[7, 0])
    gain_out.start()
    feed_out.start()
    one.close()
    two.close()
    scatter.close()

    def drain(g):
        out(0, g, one.spread, first_o).wait()
        out(3, g, two.spread, low_o).wait()

        @pl.when(chain.mid)
        def _():
            out(5, g, grad_v, grad_o).wait()

    loop(GROUPS, drain)
    out(1, GROUPS - 1, gate_v, gate_o, False).wait()
    out(2, GROUPS - 1, up_v, up_o, False).wait()
    out(4, GROUPS - 1, mixed_v, mixed_o, False).wait()
    gain_out.wait()
    feed_out.wait()


def last_kernel(
    size, plane_sizes, depth, rows, width,
    q_low, k_low, v_low, l_low, gh, smalls, x_in, grad_in, attention_gain, wq, wk, wv,
    two_in, gate_in, up_in, first_in, hidden_in, normed_in, low_in, mixed_in,
    grad_o, total_o,
    *rest,
):
    made, scratch = rest[:7], rest[7:]
    (wq_v, wk_v, wv_v, x_v, grad_v, gain_v, whole_v, parts_v, total_v, load_sem, out_sem) = scratch[:11]
    chain = Chain(size)
    one = Sum(chain, scratch[11:18], rows, width)
    plane = Plane(*plane_sizes)
    total = Total(plane, size, scratch[18:22], 8)
    share = width // plane.count
    units_wide, heads_wide, keys_wide = parts_v.shape[1], wq_v.shape[1], wk_v.shape[1]
    unit = min(256, keys_wide)
    parts_heads = parts_v.at[:, pl.ds(0, heads_wide)]
    scatter = Scatter(
        plane, scratch[22:],
        [
            (whole_v, parts_v, True, made[0], units_wide // unit, [(two_in, whole_v), (gate_in, parts_v)]),
            (whole_v, parts_v, True, made[1], units_wide // unit, [(up_in, parts_v)]),
            (whole_v, parts_v, False, made[2], units_wide // unit, [(first_in, whole_v), (hidden_in, parts_v)]),
            (whole_v, q_low, True, made[3], heads_wide // unit, [(normed_in, whole_v)]),
            (whole_v, k_low, True, made[4], keys_wide // unit, []),
            (whole_v, v_low, True, made[5], keys_wide // unit, []),
            (whole_v, parts_v, False, made[6], heads_wide // unit, [(low_in, whole_v), (mixed_in, parts_heads)]),
        ],
        share, unit,
    )
    span = one.block * GROUP
    loads = load_all(
        [(wq.at[depth], wq_v), (wk.at[depth], wk_v), (wv.at[depth], wv_v), (x_in, x_v),
         (grad_in, grad_v)],
        load_sem,
    )
    chain.greet([*plane.partners(), *total.across])
    wait_all(loads[:3])
    gain_one = attention_gain[depth : depth + 1, :]

    def out(g):
        at = rows_of(g, span)
        return pltpu.make_async_copy(one.spread.at[at], grad_o.at[at], out_sem.at[g])

    def start(g):
        at = rows_of(g, span)
        fill(
            one.part,
            at,
            lambda col: back_product(q_low[at, :], wq_v[col, :])
            + back_product(k_low[at, :], wk_v[col, :])
            + back_product(v_low[at, :], wv_v[col, :])
            + back_product(l_low[at, :], gh[col, :]),
        )
        one.offer(g)

    loop(GROUPS, start)
    gain_v[...] = jnp.zeros_like(gain_v)
    wait_all(loads[3:])

    def made_one(at, total_sum):
        pulled, terms = back_norm(x_v[at, :].astype(F32), gain_one, total_sum)
        gain_v[...] += fold(terms)
        return (grad_v[at, :] + pulled).astype(BF)

    first_total = 2 * BLOCKS + 1

    def step(i):
        scatter.tick(i)
        s = lax.div(i, 2)

        @pl.when(lax.rem(i, 2) == 1)
        def _():
            @pl.when(s < BLOCKS)
            def _():
                one.relay(s)

            @pl.when((s >= 1) & (s <= BLOCKS))
            def _():
                one.finish(s - 1, made_one)

                @pl.when(lax.rem(s, GROUP) == 0)
                def _():
                    group = lax.div(s, GROUP) - 1
                    one.receive(group)
                    out(group).start()

        @pl.when(i == first_total)
        def _():
            total.value[0] = smalls[...]

            @pl.when(chain.first_mid)
            def _():
                total.value[0, pl.ds(0, 1)] = jnp.sum(gain_v[...], axis=0, keepdims=True)

        for k in range(total.stages):

            @pl.when(i == first_total + 1 + k)
            def _(k=k):
                total.start(k)

    loop(max(scatter.steps, first_total + 2 + total.stages), step)
    total.finish(total_v)
    total_out = pltpu.make_async_copy(total_v, total_o, out_sem.at[GROUPS])
    total_out.start()
    one.close()
    scatter.close()
    loop(GROUPS, lambda g: out(g).wait())
    total_out.wait()


def call(kernel, collective_id, in_specs, outs, scratch, flops):
    return pl.pallas_call(
        kernel,
        out_shape=tuple(jax.ShapeDtypeStruct(shape, kind) for shape, kind in outs),
        in_specs=in_specs,
        out_specs=tuple(ANY for _ in outs),
        scratch_shapes=scratch,
        cost_estimate=pl.CostEstimate(flops=flops, bytes_accessed=40_000_000, transcendentals=0),
        compiler_params=pltpu.CompilerParams(
            collective_id=collective_id, has_side_effects=True, vmem_limit_bytes=VMEM_LIMIT
        ),
    )


def dma(*shape):
    return pltpu.SemaphoreType.DMA(shape)


def shards(
    size,
    stream,
    cotangent,
    prefixes,
    attention_gain,
    query_weight,
    key_weight,
    value_weight,
    gate_heads,
    query_gain,
    key_gain,
    output_weight,
    feed_gain,
    gate_weight,
    up_weight,
    down_weight,
):
    seq_count, row_count, width = stream.shape
    rows = seq_count * row_count
    span = rows // GROUPS
    dp_size = lax.axis_size("dp")
    plane_sizes = (dp_size, lax.axis_size("ctx"))
    plane_count = plane_sizes[0] * plane_sizes[1]
    heads_wide = query_weight.shape[2]
    keys_wide = key_weight.shape[2]
    units = gate_weight.shape[2]
    gates = gate_heads.shape[2]
    share = width // plane_count
    unit = min(256, keys_wide)
    halves = lax.axis_size("ctx")
    offset = lax.axis_index("ctx") * row_count
    query_pos = offset + jnp.arange(row_count, dtype=jnp.int32)
    key_pos = jnp.arange(row_count * halves, dtype=jnp.int32)
    cos_table, sin_table = rotary_tables(query_pos, HD)
    stream_flat = stream.reshape(rows, width)
    cot_flat = cotangent.reshape(rows, width)
    heads_padded = [
        jnp.pad(gate_heads[depth], ((0, 0), (0, LANES - gates))) for depth in range(LAYERS)
    ]
    sum_scratch = Sum.scratch(rows, width)

    def attention(depth, q_raw, k_raw, values, logits):
        q_raw = q_raw.reshape(seq_count, row_count, -1, HD)
        k_raw = k_raw.reshape(seq_count, row_count, -1, HD)
        values = values.reshape(seq_count, row_count, -1, HD)
        query_rot = rotated_norm(q_raw, query_gain[depth], cos_table, sin_table).astype(BF)
        key_rot = rotated_norm(k_raw, key_gain[depth], cos_table, sin_table).astype(BF)
        key_full = lax.all_gather(key_rot, "ctx", axis=1, tiled=True)
        value_full = lax.all_gather(values, "ctx", axis=1, tiled=True)
        key_heads = key_rot.shape[2]
        grouped = query_rot.reshape(seq_count, row_count, key_heads, -1, HD)
        attended, logsum = lax.map(
            partial(attend_forward, query_pos=query_pos, key_pos=key_pos),
            (grouped, key_full, value_full, prefixes),
        )
        attended = attended.reshape(rows, -1, HD)
        mixed = gated(attended, logits).reshape(rows, -1).astype(BF)
        return mixed, (q_raw, k_raw, logits, grouped, key_full, value_full, logsum, attended)

    def attention_back(depth, mixed_grad, saved):
        q_raw, k_raw, logits, grouped, key_full, value_full, logsum, attended = saved
        unused, gate_pull = jax.vjp(gated, attended, logits)
        attended_grad, logits_grad = gate_pull(mixed_grad.reshape(attended.shape))
        attended_low = attended_grad.astype(BF).reshape(grouped.shape)
        logits_low = logits_grad.astype(BF)
        query_grad, key_grad, value_grad = lax.map(
            partial(attend_backward, query_pos=query_pos, key_pos=key_pos),
            (grouped, key_full, value_full, prefixes, logsum, attended_low),
        )
        key_grad = lax.psum_scatter(
            key_grad.astype(BF), "ctx", scatter_dimension=1, tiled=True
        ).astype(F32)
        value_grad = lax.psum_scatter(
            value_grad.astype(BF), "ctx", scatter_dimension=1, tiled=True
        ).astype(F32)
        rotation = partial(rotated_norm, cos_table=cos_table, sin_table=sin_table)
        unused, query_pull = jax.vjp(rotation, q_raw, query_gain[depth])
        query_raw_grad, grad_query_gain = query_pull(query_grad.reshape(q_raw.shape))
        unused, key_pull = jax.vjp(rotation, k_raw, key_gain[depth])
        key_raw_grad, grad_key_gain = key_pull(key_grad)
        query_low = query_raw_grad.astype(BF).reshape(rows, -1)
        key_low = key_raw_grad.astype(BF).reshape(rows, -1)
        value_low = value_grad.astype(BF).reshape(rows, -1)
        return query_low, key_low, value_low, logits_low, grad_query_gain, grad_key_gain

    made_shapes = [
        ((share, units), BF), ((share, units), BF), ((units, share), BF),
        ((share, heads_wide), BF), ((share, keys_wide), BF), ((share, keys_wide), BF),
        ((heads_wide, share), BF),
    ]
    scatter_scratch = Scatter.scratch(plane_count, share, unit)

    def padded(l):
        return jnp.pad(l, ((0, 0), (0, LANES - gates)))

    normed_zero = rms_scale(stream_flat.astype(F32), attention_gain[0]).astype(BF)
    mixed_zero, saved_zero = attention(
        0,
        matmul(normed_zero, query_weight[0]),
        matmul(normed_zero, key_weight[0]),
        matmul(normed_zero, value_weight[0]).astype(BF),
        matmul(normed_zero, gate_heads[0]),
    )
    middle_zero, two_zero, slope, silu, hidden_zero, x_one, normed_one, q_raw, k_raw, values, logits = call(
        partial(forward_kernel, size, 0, rows, width),
        0,
        [WHOLE, ANY, ANY, WHOLE, ANY, ANY, ANY, WHOLE, ANY, ANY, ANY, WHOLE],
        [
            ((rows, width), F32), ((rows, width), BF), ((rows, units), BF), ((rows, units), BF),
            ((rows, units), BF), ((rows, width), F32), ((rows, width), BF),
            ((rows, heads_wide), F32), ((rows, keys_wide), F32), ((rows, keys_wide), BF),
            ((rows, LANES), F32),
        ],
        [
            pltpu.VMEM((heads_wide, width), BF), pltpu.VMEM((width, units), BF),
            pltpu.VMEM((width, units), BF), pltpu.VMEM((units, width), BF),
            pltpu.VMEM((width, heads_wide), BF), pltpu.VMEM((width, keys_wide), BF),
            pltpu.VMEM((width, keys_wide), BF), pltpu.VMEM((rows, width), BF),
            pltpu.VMEM((rows, width), F32), pltpu.VMEM((rows, units), BF),
            pltpu.VMEM((rows, units), BF), pltpu.VMEM((rows, units), BF),
            pltpu.VMEM((rows, heads_wide), F32), pltpu.VMEM((rows, keys_wide), F32),
            pltpu.VMEM((rows, keys_wide), BF), pltpu.VMEM((rows, LANES), F32),
            dma(8), dma(11, GROUPS),
        ]
        + sum_scratch + sum_scratch,
        13_000_000_000,
    )(
        mixed_zero, stream_flat, output_weight, feed_gain, gate_weight, up_weight, down_weight,
        attention_gain, query_weight, key_weight, value_weight, heads_padded[1],
    )
    mixed_one, saved_one = attention(1, q_raw, k_raw, values, logits[:, :gates])
    two_one, hidden_one, down_part, gate_low, up_low, grad, low, mixed_grad, feed_one = call(
        partial(turn_kernel, size, 1, rows, width),
        1,
        [WHOLE, ANY, ANY, ANY, WHOLE, ANY, ANY, ANY],
        [
            ((rows, width), BF), ((rows, units), BF), ((rows, width), BF), ((rows, units), BF),
            ((rows, units), BF), ((rows, width), F32), ((rows, width), BF),
            ((rows, heads_wide), F32), ((8, width), F32),
        ],
        [
            pltpu.VMEM((heads_wide, width), BF), pltpu.VMEM((width, units), BF),
            pltpu.VMEM((width, units), BF), pltpu.VMEM((units, width), BF),
            pltpu.VMEM((rows, width), F32), pltpu.VMEM((rows, width), BF),
            pltpu.VMEM((rows, units), BF), pltpu.VMEM((rows, units), BF),
            pltpu.VMEM((rows, units), BF), pltpu.VMEM((rows, heads_wide), F32),
            pltpu.VMEM((rows, width), BF), pltpu.VMEM((8, width), F32),
            dma(6), dma(9, GROUPS),
        ]
        + sum_scratch + sum_scratch,
        24_000_000_000,
    )(mixed_one, x_one, cot_flat, output_weight, feed_gain, gate_weight, up_weight, down_weight)
    result = lax.psum(down_part, "tensor")
    q_low, k_low, v_low, l_low, q_gain_one, k_gain_one = attention_back(1, mixed_grad, saved_one)
    heads_one = weight_product(l_low, normed_one)
    gate_low, up_low, first_low, grad, low, mixed_grad, gain_one, feed_zero, *made_one = call(
        partial(back_kernel, size, plane_sizes, 1, rows, width),
        2,
        [WHOLE] * 5 + [ANY, ANY, WHOLE] + [ANY] * 9 + [WHOLE] + [ANY] * 9,
        [
            ((rows, units), BF), ((rows, units), BF), ((rows, width), BF), ((rows, width), F32),
            ((rows, width), BF), ((rows, heads_wide), F32), ((8, width), F32), ((8, width), F32),
            *made_shapes,
        ],
        [
            pltpu.VMEM((width, heads_wide), BF), pltpu.VMEM((width, keys_wide), BF),
            pltpu.VMEM((width, keys_wide), BF), pltpu.VMEM((units, width), BF),
            pltpu.VMEM((width, units), BF), pltpu.VMEM((width, units), BF),
            pltpu.VMEM((heads_wide, width), BF), pltpu.VMEM((span, width), F32),
            pltpu.VMEM((rows, width), F32), pltpu.VMEM((span, units), BF),
            pltpu.VMEM((span, units), BF), pltpu.VMEM((span, units), BF),
            pltpu.VMEM((span, units), BF), pltpu.VMEM((span, heads_wide), F32),
            pltpu.VMEM((8, width), F32), pltpu.VMEM((8, width), F32),
            pltpu.VMEM((rows, width), BF), pltpu.VMEM((rows, units), BF),
            dma(8), dma(3), dma(2, PARTS - 1), dma(8, GROUPS),
        ]
        + sum_scratch + sum_scratch + scatter_scratch,
        26_000_000_000,
    )(
        q_low, k_low, v_low, padded(l_low), heads_padded[1], x_one, grad, attention_gain,
        query_weight, key_weight, value_weight, down_weight, gate_weight, up_weight, slope, silu,
        middle_zero, feed_gain, output_weight,
        two_one, gate_low, up_low, cot_flat, hidden_one, normed_one, low, mixed_one,
    )
    q_low, k_low, v_low, l_low, q_gain_zero, k_gain_zero = attention_back(0, mixed_grad, saved_zero)
    heads_zero = weight_product(l_low, normed_zero)
    head_gains = jnp.concatenate([q_gain_zero, k_gain_zero, q_gain_one, k_gain_one])
    below_rows = -(-LAYERS * gates // 8) * 8
    smalls = jnp.concatenate(
        [
            jnp.zeros((1, width), F32),
            gain_one.sum(0, keepdims=True),
            feed_zero.sum(0, keepdims=True),
            feed_one.sum(0, keepdims=True),
            jnp.pad(head_gains, (0, width - head_gains.shape[0]))[None],
            jnp.zeros((3, width), F32),
            heads_zero,
            heads_one,
            jnp.zeros((below_rows - LAYERS * gates, width), F32),
        ]
    )
    stages = plane_count.bit_length() - 1 + size.bit_length() - 1
    stream_low, totals, *made_zero = call(
        partial(last_kernel, size, plane_sizes, 0, rows, width),
        3,
        [WHOLE] * 6 + [ANY, ANY, WHOLE] + [ANY] * 11,
        [((rows, width), BF), ((8 + below_rows, width), F32), *made_shapes],
        [
            pltpu.VMEM((width, heads_wide), BF), pltpu.VMEM((width, keys_wide), BF),
            pltpu.VMEM((width, keys_wide), BF), pltpu.VMEM((rows, width), BF),
            pltpu.VMEM((rows, width), F32), pltpu.VMEM((8, width), F32),
            pltpu.VMEM((rows, width), BF), pltpu.VMEM((rows, units), BF),
            pltpu.VMEM((8 + below_rows, width), F32), dma(5), dma(GROUPS + 1),
        ]
        + sum_scratch + Total.scratch(8 + below_rows, width, stages) + scatter_scratch,
        16_000_000_000,
    )(
        q_low, k_low, v_low, padded(l_low), heads_padded[0], smalls, stream_flat, grad,
        attention_gain, query_weight, key_weight, value_weight,
        two_zero, gate_low, up_low, first_low, hidden_zero, normed_zero, low, mixed_zero,
    )
    here = lax.axis_index("dp") * halves + lax.axis_index("ctx")

    def own(array, wide_share):
        return lax.dynamic_slice_in_dim(array, here * wide_share, wide_share, array.ndim - 1)

    gains = own(totals[:4], share)
    head_gains = own(totals[4, : 4 * HD].reshape(2, 2, HD), HD // plane_count)
    heads = own(totals[8 : 8 + LAYERS * gates].reshape(LAYERS, gates, width), share)
    weights = [
        jnp.stack([made_zero[entry], made_one[entry]]).astype(F32) for entry in range(7)
    ]
    return (
        result.reshape(seq_count, row_count, width),
        stream_low.astype(F32).reshape(seq_count, row_count, width),
        gains[0:2],
        weights[3],
        weights[4],
        weights[5],
        heads.transpose(0, 2, 1),
        head_gains[:, 0],
        head_gains[:, 1],
        weights[6],
        gains[2:4],
        weights[0],
        weights[1],
        weights[2],
    )


def solution(mesh):
    return jax.shard_map(
        partial(shards, mesh.shape["tensor"]),
        mesh=mesh,
        in_specs=(
            P("dp", "ctx", None),
            P("dp", "ctx", None),
            P("dp"),
            P(),
            P(None, None, "tensor"),
            P(None, None, "tensor"),
            P(None, None, "tensor"),
            P(None, None, "tensor"),
            P(),
            P(),
            P(None, "tensor", None),
            P(),
            P(None, None, "tensor"),
            P(None, None, "tensor"),
            P(None, "tensor", None),
        ),
        out_specs=(
            P("dp", "ctx", None),
            P("dp", "ctx", None),
            P(None, ("dp", "ctx")),
            P(None, ("dp", "ctx"), "tensor"),
            P(None, ("dp", "ctx"), "tensor"),
            P(None, ("dp", "ctx"), "tensor"),
            P(None, ("dp", "ctx"), "tensor"),
            P(None, ("dp", "ctx")),
            P(None, ("dp", "ctx")),
            P(None, "tensor", ("dp", "ctx")),
            P(None, ("dp", "ctx")),
            P(None, ("dp", "ctx"), "tensor"),
            P(None, ("dp", "ctx"), "tensor"),
            P(None, "tensor", ("dp", "ctx")),
        ),
        check_vma=False,
    )
```

time: 1570 us -> 808 us (0.51)
  waiting for transfers between devices: 707 us -> 0.38 us
  matrix products: 127 us -> 60.4 us
  Pallas kernels: 512 us -> 569 us
  local copies, waits for them, and re-layouts: 74.5 us -> 52.1 us
    reduce_scatter x14 -> x0, waiting for transfers between devices: 706 us -> none  [scatter(): lax.psum_scatter(value.astype(BF), ('dp', 'ctx'), scatter_dimension=dimen...]
    pallas_call x2, Pallas kernels: 249 us -> 347 us  [the longest x1 181 us: shards(): call(partial(back_kernel, size, plane_sizes, 1, rows, width), 2, [WHOLE]...]
    dot_general x16 -> x2, matrix products: 72.6 us -> 4.26 us  [weight_product(): lax.dot_general(left, right, (((0,), (0,)), ((), ())), preferred_element_...]
    pallas_call x1, Pallas kernels: 135 us -> 109 us  [shards(): call(partial(turn_kernel, size, 1, rows, width), 1, [WHOLE, ANY, ANY, ANY...]
    unnamed x181 -> x173, local copies, waits for them, and re-layouts: 42 us -> 23.5 us
    another operation x16 -> x4, other arithmetic: 20.4 us -> 3.04 us  [the longest x12 18.3 us: shards(): jnp.stack([grads[depth][entry] for depth in range(LAYERS)])]
  transfers between devices with their start and end apart: 25 -> 5, of which waited for: 14 -> 0; matrix products, arithmetic and copies ran while one was open for 11% -> 11% of each run, Pallas kernels for 8% -> 21%
where the time goes in v2:
time: 808 us; the launch traced here: 799 us
  Pallas kernels  569 us (70%)
  other arithmetic  65.3 us (8%)
  matrix products  60.4 us (7%)
  local copies, waits for them, and re-layouts  52.1 us (6%)
  blocking collectives  33 us (4%)
  between operations  17.8 us (2%)
    pallas_call x1, Pallas kernels, shards(): call(partial(back_kernel, size, plane_sizes, 1, rows, width), 2, [WHOLE]...  181 us
    pallas_call x1, Pallas kernels, shards(): call(partial(last_kernel, size, plane_sizes, 0, rows, width), 3, [WHOLE]...  166 us
    pallas_call x1, Pallas kernels, shards(): call(partial(forward_kernel, size, 0, rows, width), 0, [WHOLE, ANY, ANY,...  113 us
    pallas_call x1, Pallas kernels, shards(): call(partial(turn_kernel, size, 1, rows, width), 1, [WHOLE, ANY, ANY, ANY...  109 us
    unnamed x173, local copies, waits for them, and re-layouts  23.5 us
    all_gather x2, blocking collectives, attention(): key_full = lax.all_gather(key_rot, 'ctx', axis=1, tiled=True)  17.2 us
  transfers between devices with their start and end apart: 5, of which 0 were waited for; matrix products, arithmetic and copies ran while one was open for 11% of the time, Pallas kernels for 21%

profile of v2, /device:TPU:0, one launch (start us, length us, event | category | flops | bytes accessed | tf_op | source)
XLA Modules:
  0.0 798.8 jit_solution(12432532874170342324)
XLA Ops:
  8.8 2.1 fusion.10
  10.9 2.9 fusion.37
  14.1 3.1 fusion.14
  18.4 2.5 copy.317
  24.2 10.0 %all_gather.13 = bf16[1,1024,2,128]{3,1,2,0:T(8,128)(2,1)} all-gather(bf16[1,512,2,128]{3,1,2,0:T(8,128)(2,1)S(1)} %pad_maximum_fusion.2), channel_id=1, replica_groups=mesh['dp'=4,'ctx'=2,'tensor'=4] {'ctx'}, dimensions={1}, use_global_device_ids=true | all-gather | bytes 786432 | tf_op jit(solution)/shard_map/all_gather | solution.py:1253
  34.4 1.8 multiply_multiply_fusion.1
  38.4 2.2 fusion.8
  40.7 1.9 exponential_reduce_fusion.1
  44.8 8.4 %all_gather.12 = bf16[1,1024,2,128]{1,3,2,0:T(8,128)(2,1)S(1)} all-gather(bf16[1,512,2,128]{1,3,2,0:T(8,128)(2,1)S(1)} %bitcast.334), channel_id=1, replica_groups=mesh['dp'=4,'ctx'=2,'tensor'=4] {'ctx'}, dimensions={1}, use_global_device_ids=true | all-gather | bytes 786432 | tf_op jit(solution)/shard_map/all_gather | solution.py:1254
  53.2 2.5 fusion.56
  59.5 113.5 %shard_map.254 = (f32[512,2048]{1,0:T(8,128)}, bf16[512,2048]{1,0:T(8,128)(2,1)}, bf16[512,1536]{1,0:T(8,128)(2,1)}, bf16[512,1536]{1,0:T(8,128)(2,1)}, bf16[512...) custom-call(bf16[512,512]{1,0:T(8,128)(2,1)} %fusion.34.mixed.mixed_, ...), custom_call_target="tpu_custom_call" | custom-call | flops 12999999488 | bytes 40000000 | tf_op jit(solution)/shard_map/pallas_call | solution.py:1309
  176.7 7.2 all_gather.15
  188.5 2.2 fusion.9
  190.8 1.9 exponential_reduce_fusion
  194.2 7.5 all_gather.14
  201.7 5.9 fusion.49
  210.7 108.9 %shard_map.255 = (bf16[512,2048]{1,0:T(8,128)(2,1)}, bf16[512,1536]{1,0:T(8,128)(2,1)}, bf16[512,2048]{1,0:T(8,128)(2,1)}, bf16[512,1536]{1,0:T(8,128)(2,1)}, bf...) custom-call(bf16[512,512]{1,0:T(8,128)(2,1)} %fusion.33.mixed.mixed_, ...), custom_call_target="tpu_custom_call" | custom-call | flops 24000000000 | bytes 40000000 | tf_op jit(solution)/shard_map/pallas_call | solution.py:1337
  321.2 6.6 fusion.27
  328.1 5.2 fusion.3
  333.3 4.8 fusion.5
  338.1 2.0 copy-done.3
  340.1 2.1 fusion.25
  342.6 3.1 convolution_multiply_fusion.1
  350.5 2.2 multiply_add_fusion.3
  353.6 3.7 multiply_reduce_fusion
  359.3 3.7 fusion.31
  369.0 180.9 %shard_map.256 = (bf16[512,1536]{1,0:T(8,128)(2,1)}, bf16[512,1536]{1,0:T(8,128)(2,1)}, bf16[512,2048]{1,0:T(8,128)(2,1)}, f32[512,2048]{1,0:T(8,128)}, bf16[512...) custom-call(bf16[512,512]{1,0:T(8,128)(2,1)} %bitcast.333, ...), custom_call_target="tpu_custom_call" | custom-call | flops 25999998976 | bytes 40000000 | tf_op jit(solution)/shard_map/pallas_call | solution.py:1361
  551.4 5.7 fusion
  557.9 2.6 fusion.2
  560.5 2.0 copy-done.2
  562.5 2.1 fusion.24
  564.8 6.6 fusion.26
  572.0 2.0 fusion.86
  574.0 1.9 fusion.12.normed_in
  577.1 3.3 convolution_multiply_fusion
  584.3 2.2 fusion.85
  586.6 2.2 multiply_add_fusion.1
  589.8 2.1 multiply_reduce_fusion.1
  592.9 3.5 fusion.32
  598.6 1.8 copy.422.v_low
  603.9 165.9 %shard_map.257 = (bf16[512,2048]{1,0:T(8,128)(2,1)}, f32[16,2048]{1,0:T(8,128)}, bf16[256,1536]{1,0:T(8,128)(2,1)}, bf16[256,1536]{1,0:T(8,128)(2,1)}, bf16[1536...) custom-call(bf16[512,512]{1,0:T(8,128)(2,1)} %bitcast.332, ...), custom_call_target="tpu_custom_call" | custom-call | flops 16000000000 | bytes 40000000 | tf_op jit(solution)/shard_map/pallas_call | solution.py:1408
  774.3 2.0 maximum_convert_fusion.4
  776.3 2.1 maximum_convert_fusion.3
  778.4 2.0 maximum_convert_fusion.5
  780.4 1.9 maximum_convert_fusion.2
  782.3 3.1 maximum_convert_fusion
  785.4 2.5 bitcast_convert_fusion
  788.0 3.2 copy.457
  (290 shorter events, 61.5 us)
Async XLA Ops:
  8.0 355.9 %reduce-scatter.7.cloned.1.call-start = ((), (), s32[]{:S(2)}) async-start(), calls=%async_computation.6 | async-start | bytes 786432 | tf_op jit(solution)/shard_map/reduce_scatter | solution.py:1278
  13.9 8.6 %copy-start.67 = (f32[512,2]{0,1:T(2,128)}, f32[512,2]{0,1:T(2,128)S(1)}, u32[]{:S(2)}) copy-start(f32[512,2]{0,1:T(2,128)S(1)} %multiply_reduce_fusion.11) | copy-start | bytes 12292
  14.1 9.4 %copy-start.20 = (f32[1,512,2,128]{3,1,2,0:T(8,128)}, f32[1,512,2,128]{3,1,2,0:T(8,128)S(1)}, u32[]{:S(2)}) copy-start(f32[1,512,2,128]{3,1,2,0:T(8,128)S(1)} %copy.315) | copy-start | bytes 1572868
  14.1 6.8 copy-start.69
  18.4 15.8 %copy-start.60 = (f32[512,4]{0,1:T(4,128)}, f32[512,4]{0,1:T(4,128)S(1)}, u32[]{:S(2)}) copy-start(f32[512,4]{0,1:T(4,128)S(1)} %multiply_reduce_fusion.5) | copy-start | bytes 24580
  20.9 13.4 %copy-start.78 = (f32[2,128]{1,0:T(2,128)S(1)}, f32[2,128]{1,0:T(2,128)}, u32[]{:S(2)}) copy-start(f32[2,128]{1,0:T(2,128)} %param.23) | copy-start | bytes 3076
  22.5 14.6 %copy-start.62 = (f32[512,2]{0,1:T(2,128)}, f32[512,2]{0,1:T(2,128)S(1)}, u32[]{:S(2)}) copy-start(f32[512,2]{0,1:T(2,128)S(1)} %fusion.65) | copy-start | bytes 12292
  22.5 152.6 %copy-start.74 = (f32[128]{0:T(128)}, f32[128]{0:T(128)S(1)}, u32[]{:S(2)}) copy-start(f32[128]{0:T(128)S(1)} %get-tuple-element.266) | copy-start | bytes 1540
  23.5 13.6 %copy-start.6 = (f32[512,64]{1,0:T(8,128)}, f32[512,64]{1,0:T(8,128)S(1)}, u32[]{:S(2)}) copy-start(f32[512,64]{1,0:T(8,128)S(1)} %get-tuple-element.261) | copy-start | bytes 393220
  40.7 12.5 %copy-start = (f32[2,1024,512,2]{2,1,3,0:T(8,128)}, f32[2,1024,512,2]{2,1,3,0:T(8,128)S(1)}, u32[]{:S(2)}) copy-start(f32[2,1024,512,2]{2,1,3,0:T(8,128)S(1)} %get-tuple-element.269) | copy-start | bytes 25165828
  173.0 10.9 %copy-start.48 = (f32[512,512]{1,0:T(8,128)S(1)}, f32[512,512]{1,0:T(8,128)}, u32[]{:S(2)}) copy-start(f32[512,512]{1,0:T(8,128)} %get-tuple-element.186) | copy-start | bytes 3145732
  174.4 9.5 %copy-start.13 = (f32[1,512,2,128]{3,2,1,0:T(2,128)}, f32[1,512,2,128]{3,2,1,0:T(2,128)S(1)}, u32[]{:S(2)}) copy-start(f32[1,512,2,128]{3,2,1,0:T(2,128)S(1)} %reshape.718) | copy-start | bytes 1572868
  176.6 11.0 %copy-start.7 = (f32[512,64]{1,0:T(8,128)S(1)}, f32[512,64]{1,0:T(8,128)}, u32[]{:S(2)}) copy-start(f32[512,64]{1,0:T(8,128)} %copy-done.6) | copy-start | bytes 393220
  201.7 5.9 copy-start.35
  321.2 6.9 copy-start.36
  327.9 37.8 %reduce-scatter.5.cloned.1.call-start = ((), (), s32[]{:S(2)}) async-start(), calls=%async_computation.5 | async-start | bytes 786432 | tf_op jit(solution)/shard_map/reduce_scatter | solution.py:1275
  333.3 6.8 copy-start.45
  333.3 6.8 copy-start.47
  342.2 255.1 %reduce-scatter.9.cloned.1.call-start = ((), (), s32[]{:S(2)}) async-start(), calls=%async_computation.7 | async-start | bytes 786432 | tf_op jit(solution)/shard_map/reduce_scatter | solution.py:1275
  347.8 5.8 copy-start.5
  352.6 5.8 copy-start.17
  359.3 7.7 copy-start.14
  359.3 7.7 copy-start.75
  551.4 13.4 %copy-start.15 = (f32[512,512]{0,1:T(8,128)}, f32[512,512]{0,1:T(8,128)S(1)}, u32[]{:S(2)}) copy-start(f32[512,512]{0,1:T(8,128)S(1)} %copy.424) | copy-start | bytes 3145732
  551.4 5.8 slice-start
  551.4 6.4 slice-start.1
  564.7 33.9 %reduce-scatter.11.cloned.1.call-start = ((), (), s32[]{:S(2)}) async-start(), calls=%async_computation.8 | async-start | bytes 786432 | tf_op jit(solution)/shard_map/reduce_scatter | solution.py:1278
  571.4 216.6 %all-reduce.15.cloned.1.call-start = ((), (), s32[]{:S(2)}) async-start(), calls=%async_computation.4 | async-start | bytes 4194304 | tf_op jit(solution)/shard_map/psum | solution.py:1358
  580.7 5.9 copy-start.66
  580.7 5.9 copy-start.65
  580.7 5.9 copy-start.9
  583.4 6.4 copy-start.12
  583.4 6.4 copy-start.28
  583.4 6.4 copy-start.71
  586.6 5.4 copy-start.61
  592.9 7.5 copy-start.21
  592.9 7.5 copy-start.63
  592.9 7.5 copy-start.73
  603.9 170.4 %copy-start.57 = (bf16[512,256]{1,0:T(8,128)(2,1)S(1)}, bf16[512,256]{1,0:T(8,128)(2,1)}, u32[]{:S(2)}) copy-start(bf16[512,256]{1,0:T(8,128)(2,1)} %get-tuple-element.221) | copy-start | bytes 786436
  603.9 172.4 %copy-start.56 = (bf16[256,512]{1,0:T(8,128)(2,1)S(1)}, bf16[256,512]{1,0:T(8,128)(2,1)}, u32[]{:S(2)}) copy-start(bf16[256,512]{1,0:T(8,128)(2,1)} %get-tuple-element.215) | copy-start | bytes 786436
  603.9 174.5 %copy-start.58 = (bf16[256,256]{1,0:T(8,128)(2,1)S(1)}, bf16[256,256]{1,0:T(8,128)(2,1)}, u32[]{:S(2)}) copy-start(bf16[256,256]{1,0:T(8,128)(2,1)} %get-tuple-element.217) | copy-start | bytes 393220
  603.9 174.5 %copy-start.59 = (bf16[256,256]{1,0:T(8,128)(2,1)S(1)}, bf16[256,256]{1,0:T(8,128)(2,1)}, u32[]{:S(2)}) copy-start(bf16[256,256]{1,0:T(8,128)(2,1)} %get-tuple-element.219) | copy-start | bytes 393220
  769.8 10.6 %copy-start.51 = (bf16[1536,256]{1,0:T(8,128)(2,1)S(1)}, bf16[1536,256]{1,0:T(8,128)(2,1)}, u32[]{:S(2)}) copy-start(bf16[1536,256]{1,0:T(8,128)(2,1)} %get-tuple-element.227) | copy-start | bytes 2359300
  769.8 10.6 %copy-start.54 = (bf16[1536,256]{1,0:T(8,128)(2,1)S(1)}, bf16[1536,256]{1,0:T(8,128)(2,1)}, u32[]{:S(2)}) copy-start(bf16[1536,256]{1,0:T(8,128)(2,1)} %get-tuple-element.226) | copy-start | bytes 2359300
  776.2 6.0 copy-start.49
  776.2 6.0 copy-start.50
  776.2 6.0 copy-start.52
  776.3 6.0 copy-start.53
  (38 other events, 122.3 us)
Sparse Core Ops, SparseCore 0:
  328.0 14.4 reduce-scatter.6
  344.8 14.5 reduce-scatter.4
  564.8 12.4 reduce-scatter.8
  579.4 14.5 reduce-scatter.10
Sparse Core Ops, SparseCore 1:
  574.2 116.0 all-reduce.14

commit v3 on v2

--- a/solution.py
+++ b/solution.py
@@ -39,26 +39,6 @@
     return (jnp.cos(angles), jnp.sin(angles))
 
 
-def rotate(values, cos_table, sin_table):
-    width = values.shape[-1]
-    leading = values[..., : width // 2]
-    trailing = values[..., width // 2 :]
-    cos_part = cos_table[:, None, :]
-    sin_part = sin_table[:, None, :]
-    return jnp.concatenate(
-        [leading * cos_part - trailing * sin_part, trailing * cos_part + leading * sin_part],
-        axis=-1,
-    )
-
-
-def rotated_norm(raw, gain, cos_table, sin_table):
-    return rotate(rms_scale(raw, gain), cos_table, sin_table)
-
-
-def gated(attended, logits):
-    return attended * jax.nn.sigmoid(logits)[:, :, None]
-
-
 def matmul(left, right):
     return jnp.dot(left, right, preferred_element_type=F32)
 
@@ -69,38 +49,6 @@
 
 def back_product(gradient, weight):
     return lax.dot_general(gradient, weight, (((1,), (1,)), ((), ())), preferred_element_type=F32)
-
-
-def masked_scores(query, keys, prefix, query_pos, key_pos):
-    scale = query.shape[-1] ** (-0.5)
-    scores = jnp.einsum("qkgd,tkd->kgqt", query, keys, preferred_element_type=F32) * scale
-    visible = (key_pos[None, :] <= query_pos[:, None]) | (key_pos[None, :] < prefix)
-    return jnp.where(visible, scores, masked)
-
-
-def attend_forward(inputs, query_pos, key_pos):
-    query, keys, values, prefix = inputs
-    scores = masked_scores(query, keys, prefix, query_pos, key_pos)
-    highest = jnp.max(scores, axis=-1, keepdims=True)
-    logsum = highest + jnp.log(jnp.sum(jnp.exp(scores - highest), axis=-1, keepdims=True))
-    weights = jnp.exp(scores - logsum).astype(BF)
-    attended = jnp.einsum("kgqt,tkd->qkgd", weights, values, preferred_element_type=F32)
-    return (attended, logsum)
-
-
-def attend_backward(inputs, query_pos, key_pos):
-    query, keys, values, prefix, logsum, out_grad = inputs
-    scale = query.shape[-1] ** (-0.5)
-    weights = jnp.exp(masked_scores(query, keys, prefix, query_pos, key_pos) - logsum)
-    weight_grad = jnp.einsum("qkgd,tkd->kgqt", out_grad, values, preferred_element_type=F32)
-    score_grad = weights * (weight_grad - jnp.sum(weights * weight_grad, axis=-1, keepdims=True))
-    score_low = score_grad.astype(BF)
-    query_grad = jnp.einsum("kgqt,tkd->qkgd", score_low, keys, preferred_element_type=F32) * scale
-    key_grad = jnp.einsum("kgqt,qkgd->tkd", score_low, query, preferred_element_type=F32) * scale
-    value_grad = jnp.einsum(
-        "kgqt,qkgd->tkd", weights.astype(BF), out_grad, preferred_element_type=F32
-    )
-    return (query_grad, key_grad, value_grad)
 
 
 def loop(count, body):
@@ -153,9 +101,10 @@
 
 
 class Sum:
-    def __init__(self, chain, refs, rows, width):
+    def __init__(self, chain, refs, landed, rows, width):
         self.chain = chain
-        self.part, self.landed, self.spread, self.s_in, self.r_in, self.s_out, self.r_out = refs
+        self.part, self.spread, self.s_in, self.r_in, self.s_out, self.r_out, self.r_cross = refs
+        self.landed, self.cross = landed
         self.block = rows // BLOCKS
         self.piece = width // PIECES
 
@@ -163,21 +112,21 @@
     def scratch(rows, width):
         return [
             pltpu.VMEM((rows, width), BF),
-            pltpu.VMEM((2, rows, width), BF),
             pltpu.VMEM((rows, width), BF),
             pltpu.SemaphoreType.DMA((BLOCKS, PIECES)),
-            pltpu.SemaphoreType.DMA((2, BLOCKS, PIECES)),
+            pltpu.SemaphoreType.DMA((BLOCKS, PIECES)),
             pltpu.SemaphoreType.DMA((BLOCKS,)),
             pltpu.SemaphoreType.DMA((BLOCKS,)),
+            pltpu.SemaphoreType.DMA((BLOCKS, PIECES)),
         ]
 
-    def hop(self, r, p, slot):
+    def hop(self, r, p, across):
         where = (rows_of(r, self.block), columns(p, self.piece))
         return pltpu.make_async_remote_copy(
             src_ref=self.part.at[where],
-            dst_ref=self.landed.at[(slot,) + where],
+            dst_ref=self.landed.at[(self.cross if across else 0,) + where],
             send_sem=self.s_in.at[r, p],
-            recv_sem=self.r_in.at[slot, r, p],
+            recv_sem=(self.r_cross if across else self.r_in).at[r, p],
             device_id=self.chain.inward,
             device_id_type=MESH,
         )
@@ -198,7 +147,7 @@
         def _():
             def one(k):
                 for p in range(PIECES):
-                    self.hop(g * GROUP + k, p, 0).start()
+                    self.hop(g * GROUP + k, p, False).start()
 
             loop(GROUP, one)
 
@@ -206,7 +155,7 @@
         @pl.when(self.chain.inner)
         def _():
             for p in range(PIECES):
-                self.hop(r, p, 0).wait_recv()
+                self.hop(r, p, False).wait_recv()
                 col = columns(p, self.piece)
 
                 def strip(i, col=col):
@@ -218,21 +167,21 @@
 
                 @pl.when(self.chain.mid)
                 def _(p=p):
-                    self.hop(r, p, 1).start()
+                    self.hop(r, p, True).start()
 
                 @pl.when(self.chain.outer)
                 def _(p=p):
-                    self.hop(r, p, 0).start()
+                    self.hop(r, p, False).start()
 
     def finish(self, r, make):
         @pl.when(self.chain.mid)
         def _():
             for p in range(PIECES):
-                self.hop(r, p, 1).wait_recv()
+                self.hop(r, p, True).wait_recv()
 
             def strip(i):
                 at = pl.ds(pl.multiple_of(r * self.block + i * STRIP, STRIP), STRIP)
-                total = self.part[at, :].astype(F32) + self.landed[1, at, :].astype(F32)
+                total = self.part[at, :].astype(F32) + self.landed[self.cross, at, :].astype(F32)
                 self.spread[at, :] = make(at, total)
 
             loop(self.block // STRIP, strip)
@@ -253,7 +202,7 @@
     def close(self):
         def block(r):
             for p in range(PIECES):
-                self.hop(r, p, 0).wait_send()
+                self.hop(r, p, False).wait_send()
 
             @pl.when(self.chain.inner)
             def _():
@@ -373,7 +322,7 @@
 
 class Scatter:
     SLOTS = (2, 4, 4, 4)
-    KEPT = (1, 3, 3, 3)
+    KEPT = (2, 3, 3, 3)
     RESULTS = 2
     LAGS = (0, 1, 4, 7, 10, 13)
 
@@ -542,18 +491,18 @@
             first += count
 
     def tick(self, i):
+        @pl.when(i < self.units)
+        def _():
+            self.ready(0, i)
+            self.product(i)
+            self.push(0, i)
+
         for stage in reversed(range(self.stages)):
             u = i - self.LAGS[stage + 1]
 
             @pl.when((u >= 0) & (u < self.units))
             def _(stage=stage, u=u):
                 self.merge(stage, u)
-
-        @pl.when(i < self.units)
-        def _():
-            self.ready(0, i)
-            self.product(i)
-            self.push(0, i)
 
     def close(self):
         for stage in range(self.stages):
@@ -613,6 +562,310 @@
             self.copy(k).wait_send()
 
 
+def turned(value):
+    return pltpu.roll(value, HD // 2, 1)
+
+
+def head_at(h):
+    return pl.ds(h * HD, HD)
+
+
+def head_norm(raw, gain, cos, sin):
+    scaled = rms_scale(raw, gain)
+    return scaled * cos + turned(scaled) * sin
+
+
+def head_norm_back(raw, gain, cos, sin, grad):
+    return back_norm(raw, gain, grad * cos - turned(grad) * sin)
+
+
+def seen(rows, first_row, columns_wide, offset, prefix):
+    query = first_row + lax.broadcasted_iota(jnp.int32, (rows, columns_wide), 0)
+    key = lax.broadcasted_iota(jnp.int32, (rows, columns_wide), 1)
+    return (key <= query) | (key + offset < prefix)
+
+
+def attend(prefix, q_raw, k_raw, v, logits, query_gain, key_gain, cos, sin,
+           mixed_o, q_o, keys_o, values_o, norm_o, attended_o, scratch, half):
+    high, low, out, send_sem, land_sem = scratch
+    rows = q_raw.shape[0]
+    span = rows // GROUPS
+    key_heads = k_raw.shape[1] // HD
+    shared = q_raw.shape[1] // k_raw.shape[1]
+    scale = HD ** (-0.5)
+
+    def copy(j, which):
+        ref = (keys_o, values_o)[which]
+        return pltpu.make_async_remote_copy(
+            src_ref=ref.at[0, j],
+            dst_ref=ref.at[1, j],
+            send_sem=send_sem.at[j, which],
+            recv_sem=land_sem.at[j, which],
+            device_id={"ctx": 1 - half},
+            device_id_type=MESH,
+        )
+
+    for j in range(key_heads):
+
+        def key_rows(g, j=j):
+            at = rows_of(g, span)
+            made = head_norm(k_raw[at, head_at(j)], key_gain, cos[at, :], sin[at, :])
+            keys_o[0, j, at, :] = made.astype(BF)
+            values_o[0, j, at, :] = v[at, head_at(j)]
+
+        loop(GROUPS, key_rows)
+
+        @pl.when(half == 0)
+        def _(j=j):
+            copy(j, 0).start()
+            copy(j, 1).start()
+
+    def own(g):
+        at = rows_of(g, span)
+        mask = seen(span, g * span, rows, half * rows, prefix)
+        for h in range(key_heads * shared):
+            j = h // shared
+            query = head_norm(q_raw[at, head_at(h)], query_gain, cos[at, :], sin[at, :]).astype(BF)
+            q_o[at, head_at(h)] = query
+            scores = jnp.where(mask, back_product(query, keys_o[0, j]) * scale, masked)
+            top = jnp.max(scores, axis=1, keepdims=True)
+            weights = jnp.exp(scores - top)
+            high[h, at, :] = top
+            low[h, at, :] = jnp.sum(weights, axis=1, keepdims=True)
+            out[at, head_at(h)] = matmul(weights.astype(BF), values_o[0, j])
+
+    loop(GROUPS, own)
+
+    @pl.when(half == 1)
+    def _():
+        for h in range(key_heads * shared):
+            j = h // shared
+            if h % shared == 0:
+                copy(j, 0).wait_recv()
+                copy(j, 1).wait_recv()
+
+            def other(g, h=h, j=j):
+                at = rows_of(g, span)
+                scores = back_product(q_o[at, head_at(h)], keys_o[1, j]) * scale
+                before = high[h, at, :]
+                top = jnp.maximum(before, jnp.max(scores, axis=1, keepdims=True))
+                weights = jnp.exp(scores - top)
+                shrink = jnp.exp(before - top)
+                high[h, at, :] = top
+                low[h, at, :] = low[h, at, :] * shrink + jnp.sum(weights, axis=1, keepdims=True)
+                out[at, head_at(h)] = out[at, head_at(h)] * shrink + matmul(
+                    weights.astype(BF), values_o[1, j]
+                )
+
+            loop(GROUPS, other)
+
+    def close(g):
+        at = rows_of(g, span)
+        open_gate = jax.nn.sigmoid(logits[at, :])
+        for h in range(key_heads * shared):
+            total = low[h, at, :]
+            norm_o[h, at, :] = high[h, at, :] + jnp.log(total)
+            attended = out[at, head_at(h)] * (1.0 / total)
+            attended_o[at, head_at(h)] = attended
+            mixed_o[at, head_at(h)] = (attended * open_gate[:, h : h + 1]).astype(BF)
+
+    loop(GROUPS, close)
+
+    @pl.when(half == 0)
+    def _():
+        for j in range(key_heads):
+            copy(j, 0).wait_send()
+            copy(j, 1).wait_send()
+
+
+def attend_scratch(rows, heads_wide, keys_wide):
+    return [
+        pltpu.VMEM((heads_wide // HD, rows, 1), F32),
+        pltpu.VMEM((heads_wide // HD, rows, 1), F32),
+        pltpu.VMEM((rows, heads_wide), F32),
+        pltpu.SemaphoreType.DMA((keys_wide // HD, 2)),
+        pltpu.SemaphoreType.DMA((keys_wide // HD, 2)),
+    ]
+
+
+def greet_half(half):
+    greet([{"ctx": 1 - half}], {"ctx": 1 - half}, half < 0)
+
+
+def attend_kernel(
+    depth, prefix, q_raw, k_raw, v, logits, query_gain, key_gain, cos, sin,
+    mixed_o, q_o, keys_o, values_o, norm_o, attended_o, *scratch,
+):
+    half = lax.axis_index("ctx")
+    greet_half(half)
+    attend(prefix[0], q_raw, k_raw, v, logits, query_gain[depth : depth + 1, :],
+           key_gain[depth : depth + 1, :], cos, sin,
+           mixed_o, q_o, keys_o, values_o, norm_o, attended_o, scratch, half)
+
+
+def first_kernel(
+    depth, prefix, stream, gain, wq, wk, wv, gh, query_gain, key_gain, cos, sin,
+    mixed_o, q_o, keys_o, values_o, norm_o, attended_o, normed_o, q_raw, k_raw, logits,
+    v, wq_v, wk_v, wv_v, load_sem, *scratch,
+):
+    half = lax.axis_index("ctx")
+    loads = load_all([(wk.at[depth], wk_v), (wv.at[depth], wv_v), (wq.at[depth], wq_v)], load_sem)
+    greet_half(half)
+    rows = stream.shape[0]
+    span = rows // GROUPS
+
+    def strip(i):
+        at = rows_of(i, STRIP)
+        value = stream[at, :].astype(F32)
+        normed_o[at, :] = rms_scale(value, gain[depth : depth + 1, :]).astype(BF)
+
+    loop(rows // STRIP, strip)
+    wait_all(loads)
+
+    def project(g):
+        at = rows_of(g, span)
+        k_raw[at, :] = matmul(normed_o[at, :], wk_v[...])
+        v[at, :] = matmul(normed_o[at, :], wv_v[...]).astype(BF)
+        q_raw[at, :] = matmul(normed_o[at, :], wq_v[...])
+        logits[at, :] = matmul(normed_o[at, :], gh[depth])
+
+    loop(GROUPS, project)
+    attend(prefix[0], q_raw, k_raw, v, logits, query_gain[depth : depth + 1, :],
+           key_gain[depth : depth + 1, :], cos, sin,
+           mixed_o, q_o, keys_o, values_o, norm_o, attended_o, scratch, half)
+
+
+def attend_back_kernel(
+    depth, prefix, mixed_grad, logits, attended, q_rot, keys, values, norm, q_raw, k_raw,
+    query_gain, key_gain, cos, sin, normed,
+    q_o, k_o, v_o, l_o, heads_o, q_gain_o, k_gain_o,
+    grad_low, inner, q_grad, k_grad, v_grad, given, landed, send_sem, land_sem,
+):
+    half = lax.axis_index("ctx")
+    greet_half(half)
+    rows = q_raw.shape[0]
+    span = rows // GROUPS
+    key_heads = k_raw.shape[1] // HD
+    shared = q_raw.shape[1] // k_raw.shape[1]
+    heads = key_heads * shared
+    scale = HD ** (-0.5)
+    query_gain_here = query_gain[depth : depth + 1, :]
+    key_gain_here = key_gain[depth : depth + 1, :]
+
+    def copy(j):
+        return pltpu.make_async_remote_copy(
+            src_ref=given.at[j],
+            dst_ref=landed.at[j],
+            send_sem=send_sem.at[j],
+            recv_sem=land_sem.at[j],
+            device_id={"ctx": 1 - half},
+            device_id_type=MESH,
+        )
+
+    def gate_back(g):
+        at = rows_of(g, span)
+        open_gate = jax.nn.sigmoid(logits[at, :])
+        lane = lax.broadcasted_iota(jnp.int32, (span, LANES), 1)
+        pulled = jnp.zeros((span, LANES), F32)
+        for h in range(heads):
+            grad = mixed_grad[at, head_at(h)]
+            here = attended[at, head_at(h)]
+            low_grad = (grad * open_gate[:, h : h + 1]).astype(BF)
+            grad_low[at, head_at(h)] = low_grad
+            inner[h, at, :] = jnp.sum(low_grad.astype(F32) * here, axis=1, keepdims=True)
+            pulled = jnp.where(lane == h, jnp.sum(grad * here, axis=1, keepdims=True), pulled)
+        l_o[at, :] = (pulled * (open_gate * (1.0 - open_gate))).astype(BF)
+
+    loop(GROUPS, gate_back)
+    heads_o[...] = weight_product(l_o[...], normed[...])[: heads_o.shape[0], :]
+
+    def back(j, side, mask_of, first):
+        k_grad[j] = jnp.zeros((rows, HD), F32)
+        v_grad[j] = jnp.zeros((rows, HD), F32)
+
+        def block(g):
+            at = rows_of(g, span)
+            for h in range(j * shared, (j + 1) * shared):
+                query = q_rot[at, head_at(h)]
+                pulled = grad_low[at, head_at(h)]
+                scores = back_product(query, keys[side, j]) * scale
+                if mask_of is not None:
+                    scores = jnp.where(mask_of(g), scores, masked)
+                weights = jnp.exp(scores - norm[h, at, :])
+                slope = back_product(pulled, values[side, j])
+                score_low = (weights * (slope - inner[h, at, :])).astype(BF)
+                moved = matmul(score_low, keys[side, j])
+                if first:
+                    q_grad[at, head_at(h)] = moved
+                else:
+                    q_grad[at, head_at(h)] += moved
+                k_grad[j] += weight_product(score_low, query)
+                v_grad[j] += weight_product(weights.astype(BF), pulled)
+
+        loop(GROUPS, block)
+
+    @pl.when(half == 1)
+    def _():
+        for j in range(key_heads):
+            back(j, 1, None, True)
+            given[j, 0] = (k_grad[j] * scale).astype(BF)
+            given[j, 1] = v_grad[j].astype(BF)
+            copy(j).start()
+
+    @pl.when(half == 0)
+    def _():
+        q_grad[...] = jnp.zeros_like(q_grad)
+
+    for j in range(key_heads):
+        back(j, 0, lambda g: seen(span, g * span, rows, half * rows, prefix[0]), False)
+
+    q_gain_o[...] = jnp.zeros_like(q_gain_o)
+    k_gain_o[...] = jnp.zeros_like(k_gain_o)
+
+    def query_rows(g):
+        at = rows_of(g, span)
+        for h in range(heads):
+            pulled, terms = head_norm_back(
+                q_raw[at, head_at(h)], query_gain_here, cos[at, :], sin[at, :],
+                q_grad[at, head_at(h)] * scale,
+            )
+            q_o[at, head_at(h)] = pulled.astype(BF)
+            q_gain_o[...] += jnp.sum(terms.reshape(span // 8, 8, HD), axis=0)
+
+    loop(GROUPS, query_rows)
+
+    for j in range(key_heads):
+
+        @pl.when(half == 0)
+        def _(j=j):
+            copy(j).wait_recv()
+
+        def key_rows(g, j=j):
+            at = rows_of(g, span)
+            k_total = k_grad[j, at, :] * scale
+            v_total = v_grad[j, at, :]
+            k_grad[j, at, :] = k_total
+            v_o[at, head_at(j)] = v_total.astype(BF)
+
+            @pl.when(half == 0)
+            def _():
+                k_grad[j, at, :] = k_total + landed[j, 0, at, :].astype(F32)
+                v_o[at, head_at(j)] = (v_total + landed[j, 1, at, :].astype(F32)).astype(BF)
+
+            pulled, terms = head_norm_back(
+                k_raw[at, head_at(j)], key_gain_here, cos[at, :], sin[at, :], k_grad[j, at, :]
+            )
+            k_o[at, head_at(j)] = pulled.astype(BF)
+            k_gain_o[...] += jnp.sum(terms.reshape(span // 8, 8, HD), axis=0)
+
+        loop(GROUPS, key_rows)
+
+    @pl.when(half == 1)
+    def _():
+        for j in range(key_heads):
+            copy(j).wait_send()
+
+
 def forward_kernel(
     size, depth, rows, width,
     mixed, stream, wo, feed_gain, wg, wu, wd, next_gain, wq, wk, wv, gh,
@@ -622,8 +875,9 @@
     (wo_v, wg_v, wu_v, wd_v, wq_v, wk_v, wv_v, x_v, middle_v, slope_v, silu_v, hidden_v, q_v, k_v,
      v_v, logit_v, load_sem, out_sem) = scratch[:18]
     chain = Chain(size)
-    one = Sum(chain, scratch[18:25], rows, width)
-    two = Sum(chain, scratch[25:32], rows, width)
+    landed = scratch[18]
+    one = Sum(chain, scratch[19:26], (landed, 1), rows, width)
+    two = Sum(chain, scratch[26:33], (landed, 2), rows, width)
     span = one.block * GROUP
     loads = load_all(
         [(wo.at[depth], wo_v), (stream, x_v), (wg.at[depth], wg_v), (wu.at[depth], wu_v),
@@ -712,7 +966,7 @@
         out(8, g, k_v, k_o).start()
         v_v[at, :] = matmul(two.spread[at, :], wv_v[...]).astype(BF)
         out(9, g, v_v, v_o).start()
-        logit_v[at, :] = matmul(two.spread[at, :], gh[...])
+        logit_v[at, :] = matmul(two.spread[at, :], gh[depth + 1])
         out(10, g, logit_v, logit_o).start()
         out(6, g, two.spread, normed_o).start()
 
@@ -744,8 +998,9 @@
     (wo_v, wg_v, wu_v, wd_v, middle_v, cot_v, hidden_v, gate_v, up_v, mixed_v, down_v, gain_v,
      load_sem, out_sem) = scratch[:14]
     chain = Chain(size)
-    one = Sum(chain, scratch[14:21], rows, width)
-    two = Sum(chain, scratch[21:28], rows, width)
+    landed = scratch[14]
+    one = Sum(chain, scratch[15:22], (landed, 1), rows, width)
+    two = Sum(chain, scratch[22:29], (landed, 2), rows, width)
     span = one.block * GROUP
     loads = load_all(
         [(wo.at[depth], wo_v), (x_in, middle_v), (cot, cot_v), (wg.at[depth], wg_v),
@@ -877,17 +1132,18 @@
 ):
     made, scratch = rest[:7], rest[7:]
     (wq_v, wk_v, wv_v, wd_v, wg_v, wu_v, wo_v, x_v, grad_v, slope_v, silu_v, gate_v, up_v, mixed_v,
-     gain_v, feed_v, whole_v, parts_v, load_sem, row_sem, tile_sem, out_sem) = scratch[:22]
+     gain_v, feed_v, whole_v, parts_v, gh_v, load_sem, row_sem, tile_sem, out_sem) = scratch[:23]
     chain = Chain(size)
-    one = Sum(chain, scratch[22:29], rows, width)
-    two = Sum(chain, scratch[29:36], rows, width)
+    landed = scratch[23]
+    one = Sum(chain, scratch[24:31], (landed, 1), rows, width)
+    two = Sum(chain, scratch[31:38], (landed, 2), rows, width)
     plane = Plane(*plane_sizes)
     share = width // plane.count
     unit = min(256, wk_v.shape[1])
     units_wide, heads_wide, keys_wide = wg_v.shape[1], wq_v.shape[1], wk_v.shape[1]
     parts_heads = parts_v.at[:, pl.ds(0, heads_wide)]
     scatter = Scatter(
-        plane, scratch[36:],
+        plane, scratch[38:],
         [
             (whole_v, parts_v, True, made[0], units_wide // unit, [(two_in, whole_v), (gate_in, parts_v)]),
             (whole_v, parts_v, True, made[1], units_wide // unit, [(up_in, parts_v)]),
@@ -902,7 +1158,8 @@
     span = one.block * GROUP
     below = depth - 1
     loads = load_all(
-        [(wq.at[depth], wq_v), (wk.at[depth], wk_v), (wv.at[depth], wv_v), (grad_in, grad_v),
+        [(wq.at[depth], wq_v), (wk.at[depth], wk_v), (wv.at[depth], wv_v), (gh.at[depth], gh_v),
+         (grad_in, grad_v),
          (wd.at[below], wd_v), (wg.at[below], wg_v), (wu.at[below], wu_v), (wo.at[below], wo_v)],
         load_sem,
     )
@@ -926,7 +1183,7 @@
 
     loop(PARTS - 1, first_tiles)
     chain.greet(plane.partners())
-    wait_all(loads[:3])
+    wait_all(loads[:4])
     gain_one = attention_gain[depth : depth + 1, :]
     gain_two = feed_gain[below : below + 1, :]
 
@@ -942,14 +1199,14 @@
             lambda col: back_product(q_low[at, :], wq_v[col, :])
             + back_product(k_low[at, :], wk_v[col, :])
             + back_product(v_low[at, :], wv_v[col, :])
-            + back_product(l_low[at, :], gh[col, :]),
+            + back_product(l_low[at, :], gh_v[col, :]),
         )
         one.offer(g)
 
     loop(GROUPS, start)
     gain_v[...] = jnp.zeros_like(gain_v)
     feed_v[...] = jnp.zeros_like(feed_v)
-    wait_all(loads[3:])
+    wait_all(loads[4:])
     row_load(x_in, 0, 0).wait()
 
     def local(at):
@@ -1075,23 +1332,25 @@
 
 def last_kernel(
     size, plane_sizes, depth, rows, width,
-    q_low, k_low, v_low, l_low, gh, smalls, x_in, grad_in, attention_gain, wq, wk, wv,
+    q_low, k_low, v_low, l_low, gh, gain_rows, head_gains, heads_below, x_in, grad_in,
+    attention_gain, wq, wk, wv, down_in,
     two_in, gate_in, up_in, first_in, hidden_in, normed_in, low_in, mixed_in,
-    grad_o, total_o,
+    grad_o, result_o, total_o,
     *rest,
 ):
     made, scratch = rest[:7], rest[7:]
     (wq_v, wk_v, wv_v, x_v, grad_v, gain_v, whole_v, parts_v, total_v, load_sem, out_sem) = scratch[:11]
     chain = Chain(size)
-    one = Sum(chain, scratch[11:18], rows, width)
+    one = Sum(chain, scratch[12:19], (scratch[11], 1), rows, width)
+    two = Sum(chain, scratch[20:27], (scratch[19], 1), rows, width)
     plane = Plane(*plane_sizes)
-    total = Total(plane, size, scratch[18:22], 8)
+    total = Total(plane, size, scratch[27:31], 8)
     share = width // plane.count
     units_wide, heads_wide, keys_wide = parts_v.shape[1], wq_v.shape[1], wk_v.shape[1]
     unit = min(256, keys_wide)
     parts_heads = parts_v.at[:, pl.ds(0, heads_wide)]
     scatter = Scatter(
-        plane, scratch[22:],
+        plane, scratch[31:],
         [
             (whole_v, parts_v, True, made[0], units_wide // unit, [(two_in, whole_v), (gate_in, parts_v)]),
             (whole_v, parts_v, True, made[1], units_wide // unit, [(up_in, parts_v)]),
@@ -1106,16 +1365,16 @@
     span = one.block * GROUP
     loads = load_all(
         [(wq.at[depth], wq_v), (wk.at[depth], wk_v), (wv.at[depth], wv_v), (x_in, x_v),
-         (grad_in, grad_v)],
+         (grad_in, grad_v), (down_in, two.part)],
         load_sem,
     )
     chain.greet([*plane.partners(), *total.across])
-    wait_all(loads[:3])
     gain_one = attention_gain[depth : depth + 1, :]
 
-    def out(g):
-        at = rows_of(g, span)
-        return pltpu.make_async_copy(one.spread.at[at], grad_o.at[at], out_sem.at[g])
+    def out(k, g):
+        at = rows_of(g, span)
+        src, dst = ((one.spread, grad_o), (two.spread, result_o))[k]
+        return pltpu.make_async_copy(src.at[at], dst.at[at], out_sem.at[k, g])
 
     def start(g):
         at = rows_of(g, span)
@@ -1125,71 +1384,104 @@
             lambda col: back_product(q_low[at, :], wq_v[col, :])
             + back_product(k_low[at, :], wk_v[col, :])
             + back_product(v_low[at, :], wv_v[col, :])
-            + back_product(l_low[at, :], gh[col, :]),
+            + back_product(l_low[at, :], gh[depth, col, :]),
         )
         one.offer(g)
 
-    loop(GROUPS, start)
     gain_v[...] = jnp.zeros_like(gain_v)
-    wait_all(loads[3:])
 
     def made_one(at, total_sum):
         pulled, terms = back_norm(x_v[at, :].astype(F32), gain_one, total_sum)
         gain_v[...] += fold(terms)
         return (grad_v[at, :] + pulled).astype(BF)
 
-    first_total = 2 * BLOCKS + 1
-
-    def step(i):
-        scatter.tick(i)
-        s = lax.div(i, 2)
-
-        @pl.when(lax.rem(i, 2) == 1)
-        def _():
-            @pl.when(s < BLOCKS)
+    def made_two(at, total_sum):
+        return total_sum.astype(BF)
+
+    first_step, first_total = 4, 2 * BLOCKS + 8
+
+    def sums(i):
+        @pl.when(i == 1)
+        def _():
+            wait_all(loads)
+            loop(GROUPS, start)
+            loop(GROUPS, two.offer)
+
+        def one_step(k, sum_here, make, s):
+            @pl.when((s >= 0) & (s < BLOCKS))
             def _():
-                one.relay(s)
+                sum_here.relay(s)
 
             @pl.when((s >= 1) & (s <= BLOCKS))
             def _():
-                one.finish(s - 1, made_one)
+                sum_here.finish(s - 1, make)
 
                 @pl.when(lax.rem(s, GROUP) == 0)
                 def _():
                     group = lax.div(s, GROUP) - 1
-                    one.receive(group)
-                    out(group).start()
-
+                    sum_here.receive(group)
+                    out(k, group).start()
+
+        @pl.when((i >= first_step) & (lax.rem(i - first_step, 2) == 0))
+        def _():
+            one_step(0, one, made_one, lax.div(i - first_step, 2))
+
+        @pl.when((i >= first_step + 9) & (lax.rem(i - first_step, 2) == 1))
+        def _():
+            one_step(1, two, made_two, lax.div(i - first_step - 9, 2))
+
+    def totals(i):
         @pl.when(i == first_total)
         def _():
-            total.value[0] = smalls[...]
+            total.value[0] = jnp.zeros(total_v.shape, F32)
 
             @pl.when(chain.first_mid)
             def _():
                 total.value[0, pl.ds(0, 1)] = jnp.sum(gain_v[...], axis=0, keepdims=True)
 
+            for k in range(3):
+                total.value[0, pl.ds(k + 1, 1)] = jnp.sum(gain_rows[k], axis=0, keepdims=True)
+            for k in range(4):
+                total.value[0, pl.ds(4, 1), pl.ds(k * HD, HD)] = jnp.sum(
+                    head_gains[k], axis=0, keepdims=True
+                )
+            for k in range(LAYERS):
+                total.value[0, pl.ds(8 + 8 * k, 8)] = heads_below[k]
+
         for k in range(total.stages):
 
             @pl.when(i == first_total + 1 + k)
             def _(k=k):
                 total.start(k)
 
-    loop(max(scatter.steps, first_total + 2 + total.stages), step)
+    def step(i):
+        scatter.tick(i)
+        sums(i)
+        totals(i)
+
+    last_sum = first_step + 9 + 2 * BLOCKS + 1
+    loop(max(scatter.steps, last_sum, first_total + 2 + total.stages), step)
     total.finish(total_v)
-    total_out = pltpu.make_async_copy(total_v, total_o, out_sem.at[GROUPS])
+    total_out = pltpu.make_async_copy(total_v, total_o, out_sem.at[2, 0])
     total_out.start()
     one.close()
+    two.close()
     scatter.close()
-    loop(GROUPS, lambda g: out(g).wait())
+
+    def drain(g):
+        out(0, g).wait()
+        out(1, g).wait()
+
+    loop(GROUPS, drain)
     total_out.wait()
 
 
-def call(kernel, collective_id, in_specs, outs, scratch, flops):
+def call(kernel, collective_id, in_specs, outs, scratch, flops, out_spec=ANY):
     return pl.pallas_call(
         kernel,
         out_shape=tuple(jax.ShapeDtypeStruct(shape, kind) for shape, kind in outs),
         in_specs=in_specs,
-        out_specs=tuple(ANY for _ in outs),
+        out_specs=tuple(out_spec for _ in outs),
         scratch_shapes=scratch,
         cost_estimate=pl.CostEstimate(flops=flops, bytes_accessed=40_000_000, transcendentals=0),
         compiler_params=pltpu.CompilerParams(
@@ -1232,61 +1524,47 @@
     gates = gate_heads.shape[2]
     share = width // plane_count
     unit = min(256, keys_wide)
-    halves = lax.axis_size("ctx")
-    offset = lax.axis_index("ctx") * row_count
-    query_pos = offset + jnp.arange(row_count, dtype=jnp.int32)
-    key_pos = jnp.arange(row_count * halves, dtype=jnp.int32)
-    cos_table, sin_table = rotary_tables(query_pos, HD)
+    here = lax.axis_index("dp") * plane_sizes[1] + lax.axis_index("ctx")
+    positions = lax.axis_index("ctx") * row_count + jnp.arange(row_count, dtype=jnp.int32)
+    cos_table, sin_table = rotary_tables(positions, HD)
+    cos = jnp.concatenate([cos_table, cos_table], axis=1)
+    sin = jnp.concatenate([-sin_table, sin_table], axis=1)
     stream_flat = stream.reshape(rows, width)
     cot_flat = cotangent.reshape(rows, width)
-    heads_padded = [
-        jnp.pad(gate_heads[depth], ((0, 0), (0, LANES - gates))) for depth in range(LAYERS)
+    heads_padded = jnp.pad(gate_heads, ((0, 0), (0, 0), (0, LANES - gates)))
+    sum_scratch = Sum.scratch(rows, width)
+    landed = [pltpu.VMEM((2, rows, width), BF)]
+    pair_scratch = [pltpu.VMEM((3, rows, width), BF)] + sum_scratch + sum_scratch
+
+    key_heads = keys_wide // HD
+    attend_outs = [
+        ((rows, heads_wide), BF), ((rows, heads_wide), BF), ((2, key_heads, rows, HD), BF),
+        ((2, key_heads, rows, HD), BF), ((heads_wide // HD, rows, 1), F32), ((rows, heads_wide), F32),
     ]
-    sum_scratch = Sum.scratch(rows, width)
-
-    def attention(depth, q_raw, k_raw, values, logits):
-        q_raw = q_raw.reshape(seq_count, row_count, -1, HD)
-        k_raw = k_raw.reshape(seq_count, row_count, -1, HD)
-        values = values.reshape(seq_count, row_count, -1, HD)
-        query_rot = rotated_norm(q_raw, query_gain[depth], cos_table, sin_table).astype(BF)
-        key_rot = rotated_norm(k_raw, key_gain[depth], cos_table, sin_table).astype(BF)
-        key_full = lax.all_gather(key_rot, "ctx", axis=1, tiled=True)
-        value_full = lax.all_gather(values, "ctx", axis=1, tiled=True)
-        key_heads = key_rot.shape[2]
-        grouped = query_rot.reshape(seq_count, row_count, key_heads, -1, HD)
-        attended, logsum = lax.map(
-            partial(attend_forward, query_pos=query_pos, key_pos=key_pos),
-            (grouped, key_full, value_full, prefixes),
+    smem = pl.BlockSpec(memory_space=pltpu.SMEM)
+
+    def attention_back(depth, collective_id, mixed_grad, logits, saved, q_raw, k_raw, normed):
+        mixed, q_rot, keys, values, norm, attended = saved
+        return call(
+            partial(attend_back_kernel, depth),
+            collective_id,
+            [smem] + [WHOLE] * 14,
+            [
+                ((rows, heads_wide), BF), ((rows, keys_wide), BF), ((rows, keys_wide), BF),
+                ((rows, LANES), BF), ((8, width), F32), ((8, HD), F32), ((8, HD), F32),
+            ],
+            [
+                pltpu.VMEM((rows, heads_wide), BF), pltpu.VMEM((heads_wide // HD, rows, 1), F32),
+                pltpu.VMEM((rows, heads_wide), F32), pltpu.VMEM((key_heads, rows, HD), F32),
+                pltpu.VMEM((key_heads, rows, HD), F32), pltpu.VMEM((key_heads, 2, rows, HD), BF),
+                pltpu.VMEM((key_heads, 2, rows, HD), BF), dma(key_heads), dma(key_heads),
+            ],
+            3_000_000_000,
+            WHOLE,
+        )(
+            prefixes, mixed_grad, logits, attended, q_rot, keys, values, norm, q_raw, k_raw,
+            query_gain, key_gain, cos, sin, normed,
         )
-        attended = attended.reshape(rows, -1, HD)
-        mixed = gated(attended, logits).reshape(rows, -1).astype(BF)
-        return mixed, (q_raw, k_raw, logits, grouped, key_full, value_full, logsum, attended)
-
-    def attention_back(depth, mixed_grad, saved):
-        q_raw, k_raw, logits, grouped, key_full, value_full, logsum, attended = saved
-        unused, gate_pull = jax.vjp(gated, attended, logits)
-        attended_grad, logits_grad = gate_pull(mixed_grad.reshape(attended.shape))
-        attended_low = attended_grad.astype(BF).reshape(grouped.shape)
-        logits_low = logits_grad.astype(BF)
-        query_grad, key_grad, value_grad = lax.map(
-            partial(attend_backward, query_pos=query_pos, key_pos=key_pos),
-            (grouped, key_full, value_full, prefixes, logsum, attended_low),
-        )
-        key_grad = lax.psum_scatter(
-            key_grad.astype(BF), "ctx", scatter_dimension=1, tiled=True
-        ).astype(F32)
-        value_grad = lax.psum_scatter(
-            value_grad.astype(BF), "ctx", scatter_dimension=1, tiled=True
-        ).astype(F32)
-        rotation = partial(rotated_norm, cos_table=cos_table, sin_table=sin_table)
-        unused, query_pull = jax.vjp(rotation, q_raw, query_gain[depth])
-        query_raw_grad, grad_query_gain = query_pull(query_grad.reshape(q_raw.shape))
-        unused, key_pull = jax.vjp(rotation, k_raw, key_gain[depth])
-        key_raw_grad, grad_key_gain = key_pull(key_grad)
-        query_low = query_raw_grad.astype(BF).reshape(rows, -1)
-        key_low = key_raw_grad.astype(BF).reshape(rows, -1)
-        value_low = value_grad.astype(BF).reshape(rows, -1)
-        return query_low, key_low, value_low, logits_low, grad_query_gain, grad_key_gain
 
     made_shapes = [
         ((share, units), BF), ((share, units), BF), ((units, share), BF),
@@ -1295,17 +1573,27 @@
     ]
     scatter_scratch = Scatter.scratch(plane_count, share, unit)
 
-    def padded(l):
-        return jnp.pad(l, ((0, 0), (0, LANES - gates)))
-
-    normed_zero = rms_scale(stream_flat.astype(F32), attention_gain[0]).astype(BF)
-    mixed_zero, saved_zero = attention(
-        0,
-        matmul(normed_zero, query_weight[0]),
-        matmul(normed_zero, key_weight[0]),
-        matmul(normed_zero, value_weight[0]).astype(BF),
-        matmul(normed_zero, gate_heads[0]),
+    *saved_zero, normed_zero, q_raw_zero, k_raw_zero, logits_zero = call(
+        partial(first_kernel, 0),
+        4,
+        [smem, WHOLE, WHOLE, ANY, ANY, ANY] + [WHOLE] * 5,
+        attend_outs
+        + [
+            ((rows, width), BF), ((rows, heads_wide), F32), ((rows, keys_wide), F32),
+            ((rows, LANES), F32),
+        ],
+        [
+            pltpu.VMEM((rows, keys_wide), BF), pltpu.VMEM((width, heads_wide), BF),
+            pltpu.VMEM((width, keys_wide), BF), pltpu.VMEM((width, keys_wide), BF), dma(3),
+        ]
+        + attend_scratch(rows, heads_wide, keys_wide),
+        3_500_000_000,
+        WHOLE,
+    )(
+        prefixes, stream_flat, attention_gain, query_weight, key_weight, value_weight, heads_padded,
+        query_gain, key_gain, cos, sin,
     )
+    mixed_zero = saved_zero[0]
     middle_zero, two_zero, slope, silu, hidden_zero, x_one, normed_one, q_raw, k_raw, values, logits = call(
         partial(forward_kernel, size, 0, rows, width),
         0,
@@ -1327,13 +1615,22 @@
             pltpu.VMEM((rows, keys_wide), BF), pltpu.VMEM((rows, LANES), F32),
             dma(8), dma(11, GROUPS),
         ]
-        + sum_scratch + sum_scratch,
+        + pair_scratch,
         13_000_000_000,
     )(
         mixed_zero, stream_flat, output_weight, feed_gain, gate_weight, up_weight, down_weight,
-        attention_gain, query_weight, key_weight, value_weight, heads_padded[1],
+        attention_gain, query_weight, key_weight, value_weight, heads_padded,
     )
-    mixed_one, saved_one = attention(1, q_raw, k_raw, values, logits[:, :gates])
+    saved_one = call(
+        partial(attend_kernel, 1),
+        5,
+        [smem] + [WHOLE] * 8,
+        attend_outs,
+        attend_scratch(rows, heads_wide, keys_wide),
+        1_000_000_000,
+        WHOLE,
+    )(prefixes, q_raw, k_raw, values, logits, query_gain, key_gain, cos, sin)
+    mixed_one = saved_one[0]
     two_one, hidden_one, down_part, gate_low, up_low, grad, low, mixed_grad, feed_one = call(
         partial(turn_kernel, size, 1, rows, width),
         1,
@@ -1352,16 +1649,16 @@
             pltpu.VMEM((rows, width), BF), pltpu.VMEM((8, width), F32),
             dma(6), dma(9, GROUPS),
         ]
-        + sum_scratch + sum_scratch,
+        + pair_scratch,
         24_000_000_000,
     )(mixed_one, x_one, cot_flat, output_weight, feed_gain, gate_weight, up_weight, down_weight)
-    result = lax.psum(down_part, "tensor")
-    q_low, k_low, v_low, l_low, q_gain_one, k_gain_one = attention_back(1, mixed_grad, saved_one)
-    heads_one = weight_product(l_low, normed_one)
+    q_low, k_low, v_low, l_low, heads_one, q_gain_one, k_gain_one = attention_back(
+        1, 6, mixed_grad, logits, saved_one, q_raw, k_raw, normed_one
+    )
     gate_low, up_low, first_low, grad, low, mixed_grad, gain_one, feed_zero, *made_one = call(
         partial(back_kernel, size, plane_sizes, 1, rows, width),
         2,
-        [WHOLE] * 5 + [ANY, ANY, WHOLE] + [ANY] * 9 + [WHOLE] + [ANY] * 9,
+        [WHOLE] * 4 + [ANY, ANY, ANY, WHOLE] + [ANY] * 9 + [WHOLE] + [ANY] * 9,
         [
             ((rows, units), BF), ((rows, units), BF), ((rows, width), BF), ((rows, width), F32),
             ((rows, width), BF), ((rows, heads_wide), F32), ((8, width), F32), ((8, width), F32),
@@ -1377,61 +1674,52 @@
             pltpu.VMEM((span, units), BF), pltpu.VMEM((span, heads_wide), F32),
             pltpu.VMEM((8, width), F32), pltpu.VMEM((8, width), F32),
             pltpu.VMEM((rows, width), BF), pltpu.VMEM((rows, units), BF),
-            dma(8), dma(3), dma(2, PARTS - 1), dma(8, GROUPS),
+            pltpu.VMEM((width, LANES), BF),
+            dma(9), dma(3), dma(2, PARTS - 1), dma(8, GROUPS),
         ]
-        + sum_scratch + sum_scratch + scatter_scratch,
+        + pair_scratch + scatter_scratch,
         26_000_000_000,
     )(
-        q_low, k_low, v_low, padded(l_low), heads_padded[1], x_one, grad, attention_gain,
+        q_low, k_low, v_low, l_low, heads_padded, x_one, grad, attention_gain,
         query_weight, key_weight, value_weight, down_weight, gate_weight, up_weight, slope, silu,
         middle_zero, feed_gain, output_weight,
         two_one, gate_low, up_low, cot_flat, hidden_one, normed_one, low, mixed_one,
     )
-    q_low, k_low, v_low, l_low, q_gain_zero, k_gain_zero = attention_back(0, mixed_grad, saved_zero)
-    heads_zero = weight_product(l_low, normed_zero)
-    head_gains = jnp.concatenate([q_gain_zero, k_gain_zero, q_gain_one, k_gain_one])
-    below_rows = -(-LAYERS * gates // 8) * 8
-    smalls = jnp.concatenate(
-        [
-            jnp.zeros((1, width), F32),
-            gain_one.sum(0, keepdims=True),
-            feed_zero.sum(0, keepdims=True),
-            feed_one.sum(0, keepdims=True),
-            jnp.pad(head_gains, (0, width - head_gains.shape[0]))[None],
-            jnp.zeros((3, width), F32),
-            heads_zero,
-            heads_one,
-            jnp.zeros((below_rows - LAYERS * gates, width), F32),
-        ]
+    q_low, k_low, v_low, l_low, heads_zero, q_gain_zero, k_gain_zero = attention_back(
+        0, 7, mixed_grad, logits_zero, saved_zero, q_raw_zero, k_raw_zero, normed_zero
     )
+    gain_rows = jnp.stack([gain_one, feed_zero, feed_one])
+    head_gains = jnp.stack([q_gain_zero, k_gain_zero, q_gain_one, k_gain_one])
+    heads_below = jnp.stack([heads_zero, heads_one])
+    below_rows = 8 * LAYERS
     stages = plane_count.bit_length() - 1 + size.bit_length() - 1
-    stream_low, totals, *made_zero = call(
+    stream_low, result, totals, *made_zero = call(
         partial(last_kernel, size, plane_sizes, 0, rows, width),
         3,
-        [WHOLE] * 6 + [ANY, ANY, WHOLE] + [ANY] * 11,
-        [((rows, width), BF), ((8 + below_rows, width), F32), *made_shapes],
+        [WHOLE] * 8 + [ANY, ANY, WHOLE] + [ANY] * 12,
+        [
+            ((rows, width), BF), ((rows, width), BF), ((8 + below_rows, width), F32), *made_shapes,
+        ],
         [
             pltpu.VMEM((width, heads_wide), BF), pltpu.VMEM((width, keys_wide), BF),
             pltpu.VMEM((width, keys_wide), BF), pltpu.VMEM((rows, width), BF),
             pltpu.VMEM((rows, width), F32), pltpu.VMEM((8, width), F32),
             pltpu.VMEM((rows, width), BF), pltpu.VMEM((rows, units), BF),
-            pltpu.VMEM((8 + below_rows, width), F32), dma(5), dma(GROUPS + 1),
+            pltpu.VMEM((8 + below_rows, width), F32), dma(6), dma(3, GROUPS),
         ]
-        + sum_scratch + Total.scratch(8 + below_rows, width, stages) + scatter_scratch,
+        + landed + sum_scratch + landed + sum_scratch + Total.scratch(8 + below_rows, width, stages) + scatter_scratch,
         16_000_000_000,
     )(
-        q_low, k_low, v_low, padded(l_low), heads_padded[0], smalls, stream_flat, grad,
-        attention_gain, query_weight, key_weight, value_weight,
+        q_low, k_low, v_low, l_low, heads_padded, gain_rows, head_gains, heads_below, stream_flat,
+        grad, attention_gain, query_weight, key_weight, value_weight, down_part,
         two_zero, gate_low, up_low, first_low, hidden_zero, normed_zero, low, mixed_zero,
     )
-    here = lax.axis_index("dp") * halves + lax.axis_index("ctx")
-
     def own(array, wide_share):
         return lax.dynamic_slice_in_dim(array, here * wide_share, wide_share, array.ndim - 1)
 
     gains = own(totals[:4], share)
     head_gains = own(totals[4, : 4 * HD].reshape(2, 2, HD), HD // plane_count)
-    heads = own(totals[8 : 8 + LAYERS * gates].reshape(LAYERS, gates, width), share)
+    heads = own(totals[8:].reshape(LAYERS, 8, width)[:, :gates], share)
     weights = [
         jnp.stack([made_zero[entry], made_one[entry]]).astype(F32) for entry in range(7)
     ]

time: 808 us -> 672 us (0.83)
  Pallas kernels: 569 us -> 638 us
  matrix products: 60.4 us -> 0 us
  local copies, waits for them, and re-layouts: 52.1 us -> 5.14 us
  other arithmetic: 65.3 us -> 18.6 us
  blocking collectives: 33 us -> 0 us
  between operations: 17.8 us -> 1.99 us
    pallas_call x0 -> x4, Pallas kernels: none -> 86.2 us  [the longest x2 41.4 us: attention_back(): call(partial(attend_back_kernel, depth), collective_id, [smem] + [WHOLE]...]
    dot_general x18 -> x0, matrix products: 60.4 us -> none  [the longest x2 13.2 us: attend_backward(): jnp.einsum('kgqt,qkgd->tkd', weights.astype(BF), out_grad, preferred_elem...]
    all_gather x4 -> x0, blocking collectives: 33 us -> none  [the longest x2 17.2 us: attention(): key_full = lax.all_gather(key_rot, 'ctx', axis=1, tiled=True)]
    convert_element_type x13 -> x0, other arithmetic: 22.4 us -> none  [the longest x2 7.4 us: attend_backward(): score_low = score_grad.astype(BF)]
    unnamed x173 -> x48, local copies, waits for them, and re-layouts: 23.5 us -> 2.03 us
    reduce_sum x16 -> x0, other arithmetic: 14.6 us -> none  [the longest x4 6.85 us: rms_scale(): values * lax.rsqrt(jnp.mean(values * values, axis=-1, keepdims=True) + ep...]
    pallas_call x1, Pallas kernels: 181 us -> 168 us  [shards(): call(partial(back_kernel, size, plane_sizes, 1, rows, width), 2, [WHOLE]...]
    reshape x12 -> x1, local copies, waits for them, and re-layouts: 12 us -> 0.01 us  [shards(): heads = own(totals[8:].reshape(LAYERS, 8, width)[:, :gates], share)]
  transfers between devices with their start and end apart: 5 -> 0, of which waited for: 0 -> 0; matrix products, arithmetic and copies ran while one was open for 11% -> 0% of each run, Pallas kernels for 21% -> 0%
where the time goes in v3:
time: 672 us; the launch traced here: 664 us
  Pallas kernels  638 us (95%)
  other arithmetic  18.6 us (3%)
    pallas_call x1, Pallas kernels, shards(): call(partial(back_kernel, size, plane_sizes, 1, rows, width), 2, [WHOLE]...  168 us
    pallas_call x1, Pallas kernels, shards(): call(partial(last_kernel, size, plane_sizes, 0, rows, width), 3, [WHOLE]...  157 us
    pallas_call x1, Pallas kernels, shards(): call(partial(forward_kernel, size, 0, rows, width), 0, [WHOLE, ANY, ANY,...  115 us
    pallas_call x1, Pallas kernels, shards(): call(partial(turn_kernel, size, 1, rows, width), 1, [WHOLE, ANY, ANY, ANY...  112 us
    pallas_call x2, Pallas kernels, attention_back(): call(partial(attend_back_kernel, depth), collective_id, [smem] + [WHOLE]...  41.4 us
    pallas_call x1, Pallas kernels, shards(): call(partial(first_kernel, 0), 4, [smem, WHOLE, WHOLE, ANY, ANY, ANY] + [...  26.6 us
    pallas_call x1, Pallas kernels, shards(): call(partial(attend_kernel, 1), 5, [smem] + [WHOLE] * 8, attend_outs, att...  18.2 us

profile of v3, /device:TPU:0, one launch (start us, length us, event | category | flops | bytes accessed | tf_op | source)
XLA Modules:
  0.0 663.8 jit_solution(8274717468197708325)
XLA Ops:
  0.6 0.0 copy-start.20
  0.7 1.0 fusion
  1.7 1.0 pad_maximum_fusion
  2.7 0.0 copy-done.20
  2.7 0.5 copy.29
  3.2 1.2 pad.4.gh
  5.0 26.6 %shard_map.254 = (bf16[512,512]{1,0:T(8,128)(2,1)}, bf16[512,512]{1,0:T(8,128)(2,1)}, bf16[2,2,512,128]{3,2,1,0:T(8,128)(2,1)}, bf16[2,2,512,128]{3,2,1,0:T(8,12...) custom-call(s32[1]{0:T(128)S(6)} %copy.35.prefix, ...), custom_call_target="tpu_custom_call" | custom-call | flops 3500000000 | bytes 40000000 | tf_op jit(solution)/shard_map/pallas_call | solution.py:1576
  31.7 114.6 %shard_map.255 = (f32[512,2048]{1,0:T(8,128)}, bf16[512,2048]{1,0:T(8,128)(2,1)}, bf16[512,1536]{1,0:T(8,128)(2,1)}, bf16[512,1536]{1,0:T(8,128)(2,1)}, bf16[512...) custom-call(bf16[512,512]{1,0:T(8,128)(2,1)} %get-tuple-element.89.m, ...), custom_call_target="tpu_custom_call" | custom-call | flops 12999999488 | bytes 40000000 | tf_op jit(solution)/shard_map/pallas_call | solution.py:1597
  146.3 18.2 %shard_map.256 = (bf16[512,512]{1,0:T(8,128)(2,1)}, bf16[512,512]{1,0:T(8,128)(2,1)}, bf16[2,2,512,128]{3,2,1,0:T(8,128)(2,1)}, bf16[2,2,512,128]{3,2,1,0:T(8,12...) custom-call(s32[1]{0:T(128)S(6)} %copy.35.prefix, f32[512,512]{1,0:T(8,128)} %get-tuple-element.90.q_raw, ...), custom_call_target="tpu_custom_call" | custom-call | flops 1000000000 | bytes 40000000 | tf_op jit(solution)/shard_map/pallas_call | solution.py:1624
  164.5 111.9 %shard_map.257 = (bf16[512,2048]{1,0:T(8,128)(2,1)}, bf16[512,1536]{1,0:T(8,128)(2,1)}, bf16[512,2048]{1,0:T(8,128)(2,1)}, bf16[512,1536]{1,0:T(8,128)(2,1)}, bf...) custom-call(bf16[512,512]{1,0:T(8,128)(2,1)} %get-tuple-element.94.m, ...), custom_call_target="tpu_custom_call" | custom-call | flops 24000000000 | bytes 40000000 | tf_op jit(solution)/shard_map/pallas_call | solution.py:1634
  276.4 22.3 %shard_map.258 = (bf16[512,512]{1,0:T(8,128)(2,1)}, bf16[512,256]{1,0:T(8,128)(2,1)}, bf16[512,256]{1,0:T(8,128)(2,1)}, bf16[512,128]{1,0:T(8,128)(2,1)}, f32[8,...) custom-call(s32[1]{0:T(128)S(6)} %copy.35.prefix, f32[512,512]{1,0:T(8,128)} %get-tuple-element.96.mixed_grad, ...), custom_call_target="tpu_custom_call" | custom-call | flops 3000000000 | bytes 40000000 | tf_op jit(solution)/shard_map/pallas_call | solution.py:1548
  298.7 168.0 %shard_map.259 = (bf16[512,1536]{1,0:T(8,128)(2,1)}, bf16[512,1536]{1,0:T(8,128)(2,1)}, bf16[512,2048]{1,0:T(8,128)(2,1)}, f32[512,2048]{1,0:T(8,128)}, bf16[512...) custom-call(bf16[512,512]{1,0:T(8,128)(2,1)} %get-tuple-element.103., ...), custom_call_target="tpu_custom_call" | custom-call | flops 25999998976 | bytes 40000000 | tf_op jit(solution)/shard_map/pallas_call | solution.py:1658
  466.6 0.0 copy-start.17
  466.7 0.0 copy-start.21
  466.7 0.0 copy-start.22
  466.7 0.0 copy-start.16
  466.7 0.0 copy-start.18
  466.7 0.0 copy-start.19
  466.7 19.1 %shard_map.260 = (bf16[512,512]{1,0:T(8,128)(2,1)}, bf16[512,256]{1,0:T(8,128)(2,1)}, bf16[512,256]{1,0:T(8,128)(2,1)}, bf16[512,128]{1,0:T(8,128)(2,1)}, f32[8,...) custom-call(s32[1]{0:T(128)S(6)} %copy.35.prefix, f32[512,512]{1,0:T(8,128)} %get-tuple-element.116.mixed_grad, ...), custom_call_target="tpu_custom_call" | custom-call | flops 3000000000 | bytes 40000000 | tf_op jit(solution)/shard_map/pallas_call | solution.py:1548
  485.8 0.0 copy-done.17
  485.8 1.5 pad_maximum_fusion.3.heads_below
  487.3 0.0 copy-done.21
  487.3 0.0 copy-done.22
  487.3 1.3 pad_maximum_fusion.4.head_gains
  488.6 0.0 copy-done.16
  488.6 0.0 copy-done.18
  488.6 0.0 copy-done.19
  488.7 0.7 pad_maximum_fusion.2.gain_rows
  489.3 157.4 %shard_map.261 = (bf16[512,2048]{1,0:T(8,128)(2,1)}, bf16[512,2048]{1,0:T(8,128)(2,1)}, f32[24,2048]{1,0:T(8,128)}, bf16[256,1536]{1,0:T(8,128)(2,1)}, bf16[256,...) custom-call(bf16[512,512]{1,0:T(8,128)(2,1)} %get-tuple-element.126., ...), custom_call_target="tpu_custom_call" | custom-call | flops 16000000000 | bytes 40000000 | tf_op jit(solution)/shard_map/pallas_call | solution.py:1696
  646.7 0.0 copy-done.4
  646.7 0.0 copy-start.3
  646.8 0.0 copy-start.6
  646.8 3.1 maximum_convert_fusion.2
  649.9 1.9 maximum_convert_fusion.1
  651.8 0.1 copy-done.5
  651.9 1.9 maximum_convert_fusion
  653.8 1.0 maximum_convert_fusion.4
  654.8 0.0 copy-done.15
  654.8 0.8 maximum_convert_fusion.6
  655.7 0.8 maximum_convert_fusion.5
  656.5 0.0 copy-done.9
  656.5 1.0 maximum_convert_fusion.3
  657.6 0.0 copy-done
  657.6 2.5 bitcast_convert_fusion
  660.1 0.6 dynamic-slice_bitcast_fusion
  660.8 0.7 fusion.1
  661.4 0.6 constant_dynamic-slice_fusion.2
  662.1 1.3 copy.36
  (31 shorter events, 0.1 us)
Async XLA Ops:
  0.6 2.0 copy-start.20
  466.6 19.2 %copy-start.17 = (f32[8,2048]{1,0:T(8,128)S(1)}, f32[8,2048]{1,0:T(8,128)}, u32[]{:S(2)}) copy-start(f32[8,2048]{1,0:T(8,128)} %get-tuple-element.138) | copy-start | bytes 196612
  466.7 20.7 %copy-start.21 = (f32[8,128]{1,0:T(8,128)S(1)}, f32[8,128]{1,0:T(8,128)}, u32[]{:S(2)}) copy-start(f32[8,128]{1,0:T(8,128)} %get-tuple-element.135) | copy-start | bytes 12292
  466.7 20.7 %copy-start.22 = (f32[8,128]{1,0:T(8,128)S(1)}, f32[8,128]{1,0:T(8,128)}, u32[]{:S(2)}) copy-start(f32[8,128]{1,0:T(8,128)} %get-tuple-element.136) | copy-start | bytes 12292
  466.7 22.0 %copy-start.16 = (f32[8,2048]{1,0:T(8,128)S(1)}, f32[8,2048]{1,0:T(8,128)}, u32[]{:S(2)}) copy-start(f32[8,2048]{1,0:T(8,128)} %get-tuple-element.132) | copy-start | bytes 196612
  466.7 22.0 %copy-start.18 = (f32[8,2048]{1,0:T(8,128)S(1)}, f32[8,2048]{1,0:T(8,128)}, u32[]{:S(2)}) copy-start(f32[8,2048]{1,0:T(8,128)} %get-tuple-element.130) | copy-start | bytes 196612
  466.7 22.0 %copy-start.19 = (f32[8,2048]{1,0:T(8,128)S(1)}, f32[8,2048]{1,0:T(8,128)}, u32[]{:S(2)}) copy-start(f32[8,2048]{1,0:T(8,128)} %get-tuple-element.131) | copy-start | bytes 196612
  489.3 157.4 %copy-start.4 = (bf16[1536,256]{1,0:T(8,128)(2,1)S(1)}, bf16[1536,256]{1,0:T(8,128)(2,1)}, u32[]{:S(2)}) copy-start(bf16[1536,256]{1,0:T(8,128)(2,1)} %get-tuple-element.163) | copy-start | bytes 2359300
  646.7 3.1 copy-start.3
  646.8 3.1 copy-start.6
  649.9 1.9 copy-start.2
  649.9 2.0 copy-start.5
  651.9 1.9 copy-start.8
  651.9 1.9 copy-start.10
  651.9 3.0 copy-start.13
  651.9 3.0 copy-start.15
  653.8 1.9 copy-start.12
  653.8 1.9 copy-start.14
  653.8 2.8 copy-start.7
  653.8 2.8 copy-start.9
  653.8 3.8 copy-start
  657.6 2.5 copy-start.11
  657.6 4.5 copy-start.1

commit v4 on v3

--- a/solution.py
+++ b/solution.py
@@ -326,12 +326,13 @@
     RESULTS = 2
     LAGS = (0, 1, 4, 7, 10, 13)
 
-    def __init__(self, plane, refs, groups, share, tile):
+    def __init__(self, plane, refs, whole, parts, groups, share, tile):
         self.plane = plane
+        self.whole, self.parts = whole, parts
         self.groups = groups
         self.share, self.tile = share, tile
         self.stages = len(plane.bits)
-        self.units = sum(group[4] for group in groups)
+        self.units = sum(group[2] for group in groups)
         self.refs = [refs[6 * k : 6 * k + 6] for k in range(self.stages)]
         self.made, self.out_sem, self.load_sem = refs[6 * self.stages :]
         self.steps = self.units + self.LAGS[self.stages]
@@ -354,7 +355,7 @@
         return found + [
             pltpu.VMEM((cls.RESULTS, share, tile), BF),
             pltpu.SemaphoreType.DMA((cls.RESULTS,)),
-            pltpu.SemaphoreType.DMA((2,)),
+            pltpu.SemaphoreType.DMA((4,)),
         ]
 
     def partner(self, stage, u):
@@ -391,48 +392,42 @@
         slot, spot = lax.rem(u, self.SLOTS[0]), lax.rem(u, self.KEPT[0])
         odd = lax.rem(u, 2)
         orders = self.plane.orders
-        blocks = self.plane.count // 2
         first = 0
-        for whole, parts, by_rows, unused, count, loads in self.groups:
-
-            @pl.when((u >= first) & (u < first + count))
-            def _(whole=whole, parts=parts, by_rows=by_rows, first=first, loads=loads):
-                if loads:
-
-                    @pl.when(u == first)
-                    def _():
-                        wait_all(load_all(loads, self.load_sem))
-
-                col = columns(u - first, self.tile)
-
-                def one(i):
-                    far = lax.rem(i, 2)
-                    j = lax.div(i, 2)
-                    owner = flip(self.plane.me, orders[0][0]) * far + self.plane.me * (1 - far)
-                    rest = j
-                    for bits in reversed(tuple(zip(*orders))[1:]):
-                        low = lax.rem(rest, 2)
-                        rest = lax.div(rest, 2)
-                        turned = flip(owner, bits[0]) * (1 - odd) + flip(owner, bits[1]) * odd
-                        owner = turned * low + owner * (1 - low)
-                    at = columns(owner, self.share)
-                    if by_rows:
-                        made = weight_product(whole[:, at], parts[:, col])
-                    else:
-                        made = weight_product(parts[:, col], whole[:, at])
-                    made = made.astype(BF)
-
-                    @pl.when(far == 1)
-                    def _():
-                        send[slot, j] = made
-
-                    @pl.when(far == 0)
-                    def _():
-                        keep[spot, j] = made
-
-                loop(2 * blocks, one)
+        place = u
+        by_rows_here = u < 0
+        for unused, by_rows, count, loads in self.groups:
+            here = (u >= first) & (u < first + count)
+            place = jnp.where(here, u - first, place)
+            if by_rows:
+                by_rows_here = by_rows_here | here
+
+            @pl.when(u == first)
+            def _(loads=loads):
+                wait_all(load_all(loads, self.load_sem))
 
             first += count
+        parts = self.parts[:, columns(place, self.tile)]
+
+        def block(far, j):
+            owner = flip(self.plane.me, orders[0][0]) if far else self.plane.me
+            for bits in reversed(tuple(zip(*orders))[1:]):
+                if j % 2:
+                    owner = flip(owner, bits[0]) * (1 - odd) + flip(owner, bits[1]) * odd
+                j //= 2
+            return self.whole[:, columns(owner, self.share)]
+
+        def all_blocks(make):
+            for j in range(self.plane.count // 2):
+                send[slot, j] = make(block(True, j)).astype(BF)
+                keep[spot, j] = make(block(False, j)).astype(BF)
+
+        @pl.when(by_rows_here)
+        def _():
+            all_blocks(lambda whole: weight_product(whole, parts))
+
+        @pl.when(jnp.logical_not(by_rows_here))
+        def _():
+            all_blocks(lambda whole: weight_product(parts, whole))
 
     def merge(self, stage, u):
         unused, keep, land = self.refs[stage][:3]
@@ -478,7 +473,7 @@
     def results(self, u, act):
         place = lax.rem(u, self.RESULTS)
         first = 0
-        for unused, unused_parts, by_rows, out, count, unused_loads in self.groups:
+        for out, by_rows, count, unused_loads in self.groups:
 
             @pl.when((u >= first) & (u < first + count))
             def _(by_rows=by_rows, out=out, first=first):
@@ -735,14 +730,12 @@
            mixed_o, q_o, keys_o, values_o, norm_o, attended_o, scratch, half)
 
 
-def attend_back_kernel(
-    depth, prefix, mixed_grad, logits, attended, q_rot, keys, values, norm, q_raw, k_raw,
+def attend_back(
+    half, depth, prefix, mixed_grad, logits, attended, q_rot, keys, values, norm, q_raw, k_raw,
     query_gain, key_gain, cos, sin, normed,
     q_o, k_o, v_o, l_o, heads_o, q_gain_o, k_gain_o,
     grad_low, inner, q_grad, k_grad, v_grad, given, landed, send_sem, land_sem,
 ):
-    half = lax.axis_index("ctx")
-    greet_half(half)
     rows = q_raw.shape[0]
     span = rows // GROUPS
     key_heads = k_raw.shape[1] // HD
@@ -776,8 +769,9 @@
             pulled = jnp.where(lane == h, jnp.sum(grad * here, axis=1, keepdims=True), pulled)
         l_o[at, :] = (pulled * (open_gate * (1.0 - open_gate))).astype(BF)
 
-    loop(GROUPS, gate_back)
-    heads_o[...] = weight_product(l_o[...], normed[...])[: heads_o.shape[0], :]
+    def gates():
+        loop(GROUPS, gate_back)
+        heads_o[...] = weight_product(l_o[...], normed[...])[: heads_o.shape[0], :]
 
     def back(j, side, mask_of, first):
         k_grad[j] = jnp.zeros((rows, HD), F32)
@@ -804,23 +798,21 @@
 
         loop(GROUPS, block)
 
-    @pl.when(half == 1)
-    def _():
-        for j in range(key_heads):
+    def other(j):
+        @pl.when(half == 1)
+        def _():
             back(j, 1, None, True)
             given[j, 0] = (k_grad[j] * scale).astype(BF)
             given[j, 1] = v_grad[j].astype(BF)
             copy(j).start()
 
-    @pl.when(half == 0)
-    def _():
-        q_grad[...] = jnp.zeros_like(q_grad)
-
-    for j in range(key_heads):
+        @pl.when(half == 0)
+        def _():
+            wide_head = pl.ds(j * shared * HD, shared * HD)
+            q_grad[:, wide_head] = jnp.zeros((rows, shared * HD), F32)
+
+    def own(j):
         back(j, 0, lambda g: seen(span, g * span, rows, half * rows, prefix[0]), False)
-
-    q_gain_o[...] = jnp.zeros_like(q_gain_o)
-    k_gain_o[...] = jnp.zeros_like(k_gain_o)
 
     def query_rows(g):
         at = rows_of(g, span)
@@ -832,9 +824,13 @@
             q_o[at, head_at(h)] = pulled.astype(BF)
             q_gain_o[...] += jnp.sum(terms.reshape(span // 8, 8, HD), axis=0)
 
-    loop(GROUPS, query_rows)
-
-    for j in range(key_heads):
+    def queries():
+        q_gain_o[...] = jnp.zeros_like(q_gain_o)
+        loop(GROUPS, query_rows)
+
+    def keys_of(j):
+        if j == 0:
+            k_gain_o[...] = jnp.zeros_like(k_gain_o)
 
         @pl.when(half == 0)
         def _(j=j):
@@ -860,10 +856,30 @@
 
         loop(GROUPS, key_rows)
 
-    @pl.when(half == 1)
-    def _():
-        for j in range(key_heads):
-            copy(j).wait_send()
+    def close():
+        @pl.when(half == 1)
+        def _():
+            for j in range(key_heads):
+                copy(j).wait_send()
+
+    heads_each = range(key_heads)
+    return (
+        [gates]
+        + [partial(other, j) for j in heads_each]
+        + [partial(own, j) for j in heads_each]
+        + [queries]
+        + [partial(keys_of, j) for j in heads_each],
+        close,
+    )
+
+
+def attend_back_kernel(depth, *refs):
+    half = lax.axis_index("ctx")
+    greet_half(half)
+    pieces, close = attend_back(half, depth, *refs)
+    for piece in pieces:
+        piece()
+    close()
 
 
 def forward_kernel(
@@ -1130,7 +1146,7 @@
     gate_o, up_o, first_o, grad_o, low_o, mixed_o, gain_o, feed_gain_o,
     *rest,
 ):
-    made, scratch = rest[:7], rest[7:]
+    made, scratch = rest[:5], rest[5:]
     (wq_v, wk_v, wv_v, wd_v, wg_v, wu_v, wo_v, x_v, grad_v, slope_v, silu_v, gate_v, up_v, mixed_v,
      gain_v, feed_v, whole_v, parts_v, gh_v, load_sem, row_sem, tile_sem, out_sem) = scratch[:23]
     chain = Chain(size)
@@ -1142,16 +1158,19 @@
     unit = min(256, wk_v.shape[1])
     units_wide, heads_wide, keys_wide = wg_v.shape[1], wq_v.shape[1], wk_v.shape[1]
     parts_heads = parts_v.at[:, pl.ds(0, heads_wide)]
+    heads_parts = [
+        (q_low, parts_heads),
+        (k_low, parts_v.at[:, pl.ds(heads_wide, keys_wide)]),
+        (v_low, parts_v.at[:, pl.ds(heads_wide + keys_wide, keys_wide)]),
+    ]
     scatter = Scatter(
-        plane, scratch[38:],
+        plane, scratch[38:], whole_v, parts_v,
         [
-            (whole_v, parts_v, True, made[0], units_wide // unit, [(two_in, whole_v), (gate_in, parts_v)]),
-            (whole_v, parts_v, True, made[1], units_wide // unit, [(up_in, parts_v)]),
-            (whole_v, parts_v, False, made[2], units_wide // unit, [(cot_in, whole_v), (hidden_in, parts_v)]),
-            (whole_v, q_low, True, made[3], heads_wide // unit, [(normed_in, whole_v)]),
-            (whole_v, k_low, True, made[4], keys_wide // unit, []),
-            (whole_v, v_low, True, made[5], keys_wide // unit, []),
-            (whole_v, parts_v, False, made[6], heads_wide // unit, [(low_in, whole_v), (mixed_in, parts_heads)]),
+            (made[0], True, units_wide // unit, [(two_in, whole_v), (gate_in, parts_v)]),
+            (made[1], True, units_wide // unit, [(up_in, parts_v)]),
+            (made[2], False, units_wide // unit, [(cot_in, whole_v), (hidden_in, parts_v)]),
+            (made[3], True, (heads_wide + 2 * keys_wide) // unit, [(normed_in, whole_v), *heads_parts]),
+            (made[4], False, heads_wide // unit, [(low_in, whole_v), (mixed_in, parts_heads)]),
         ],
         share, unit,
     )
@@ -1332,13 +1351,18 @@
 
 def last_kernel(
     size, plane_sizes, depth, rows, width,
-    q_low, k_low, v_low, l_low, gh, gain_rows, head_gains, heads_below, x_in, grad_in,
-    attention_gain, wq, wk, wv, down_in,
-    two_in, gate_in, up_in, first_in, hidden_in, normed_in, low_in, mixed_in,
-    grad_o, result_o, total_o,
-    *rest,
+    *refs,
 ):
-    made, scratch = rest[:7], rest[7:]
+    attend_in, refs = refs[:15], refs[15:]
+    (gh, gain_one_in, feed_zero_in, feed_one_in, q_gain_one, k_gain_one, heads_one, x_in, grad_in,
+     attention_gain, wq, wk, wv, down_in, two_in, gate_in, up_in, first_in, hidden_in, low_in, mixed_in,
+     grad_o, result_o, total_o, *rest) = refs
+    normed_in = attend_in[14]
+    made, rest = rest[:5], rest[5:]
+    attend_made, attend_scratch, scratch = rest[:7], rest[7:16], rest[16:]
+    q_low, k_low, v_low, l_low, heads_zero, q_gain_zero, k_gain_zero = attend_made
+    half = lax.axis_index("ctx")
+    pieces, close_attend = attend_back(half, depth, *attend_in, *attend_made, *attend_scratch)
     (wq_v, wk_v, wv_v, x_v, grad_v, gain_v, whole_v, parts_v, total_v, load_sem, out_sem) = scratch[:11]
     chain = Chain(size)
     one = Sum(chain, scratch[12:19], (scratch[11], 1), rows, width)
@@ -1349,16 +1373,19 @@
     units_wide, heads_wide, keys_wide = parts_v.shape[1], wq_v.shape[1], wk_v.shape[1]
     unit = min(256, keys_wide)
     parts_heads = parts_v.at[:, pl.ds(0, heads_wide)]
+    heads_parts = [
+        (q_low, parts_heads),
+        (k_low, parts_v.at[:, pl.ds(heads_wide, keys_wide)]),
+        (v_low, parts_v.at[:, pl.ds(heads_wide + keys_wide, keys_wide)]),
+    ]
     scatter = Scatter(
-        plane, scratch[31:],
+        plane, scratch[31:], whole_v, parts_v,
         [
-            (whole_v, parts_v, True, made[0], units_wide // unit, [(two_in, whole_v), (gate_in, parts_v)]),
-            (whole_v, parts_v, True, made[1], units_wide // unit, [(up_in, parts_v)]),
-            (whole_v, parts_v, False, made[2], units_wide // unit, [(first_in, whole_v), (hidden_in, parts_v)]),
-            (whole_v, q_low, True, made[3], heads_wide // unit, [(normed_in, whole_v)]),
-            (whole_v, k_low, True, made[4], keys_wide // unit, []),
-            (whole_v, v_low, True, made[5], keys_wide // unit, []),
-            (whole_v, parts_v, False, made[6], heads_wide // unit, [(low_in, whole_v), (mixed_in, parts_heads)]),
+            (made[0], True, units_wide // unit, [(two_in, whole_v), (gate_in, parts_v)]),
+            (made[1], True, units_wide // unit, [(up_in, parts_v)]),
+            (made[2], False, units_wide // unit, [(first_in, whole_v), (hidden_in, parts_v)]),
+            (made[3], True, (heads_wide + 2 * keys_wide) // unit, [(normed_in, whole_v), *heads_parts]),
+            (made[4], False, heads_wide // unit, [(low_in, whole_v), (mixed_in, parts_heads)]),
         ],
         share, unit,
     )
@@ -1368,7 +1395,7 @@
          (grad_in, grad_v), (down_in, two.part)],
         load_sem,
     )
-    chain.greet([*plane.partners(), *total.across])
+    chain.greet([*plane.partners(), *total.across, {"ctx": 1 - half}])
     gain_one = attention_gain[depth : depth + 1, :]
 
     def out(k, g):
@@ -1398,14 +1425,24 @@
     def made_two(at, total_sum):
         return total_sum.astype(BF)
 
-    first_step, first_total = 4, 2 * BLOCKS + 8
+    begin = len(pieces)
+    first_two, first_one = 3, begin + 2
+    sum_ticks = 4 * -(-(BLOCKS + 1) // 3)
+    first_total = first_one + sum_ticks
 
     def sums(i):
-        @pl.when(i == 1)
-        def _():
-            wait_all(loads)
+        @pl.when(i == 0)
+        def _():
+            loads[5].wait()
+            loop(GROUPS, two.offer)
+
+        for place, piece in enumerate(pieces):
+            pl.when(i == place)(piece)
+
+        @pl.when(i == begin)
+        def _():
+            wait_all(loads[:5])
             loop(GROUPS, start)
-            loop(GROUPS, two.offer)
 
         def one_step(k, sum_here, make, s):
             @pl.when((s >= 0) & (s < BLOCKS))
@@ -1422,13 +1459,16 @@
                     sum_here.receive(group)
                     out(k, group).start()
 
-        @pl.when((i >= first_step) & (lax.rem(i - first_step, 2) == 0))
-        def _():
-            one_step(0, one, made_one, lax.div(i - first_step, 2))
-
-        @pl.when((i >= first_step + 9) & (lax.rem(i - first_step, 2) == 1))
-        def _():
-            one_step(1, two, made_two, lax.div(i - first_step - 9, 2))
+        def paced(k, sum_here, make, first):
+            since = i - first
+            take = lax.rem(since, 4)
+
+            @pl.when((since >= 0) & (take < 3))
+            def _():
+                one_step(k, sum_here, make, lax.div(since, 4) * 3 + take)
+
+        paced(1, two, made_two, first_two)
+        paced(0, one, made_one, first_one)
 
     def totals(i):
         @pl.when(i == first_total)
@@ -1439,14 +1479,14 @@
             def _():
                 total.value[0, pl.ds(0, 1)] = jnp.sum(gain_v[...], axis=0, keepdims=True)
 
-            for k in range(3):
-                total.value[0, pl.ds(k + 1, 1)] = jnp.sum(gain_rows[k], axis=0, keepdims=True)
-            for k in range(4):
+            for k, gains in enumerate((gain_one_in, feed_zero_in, feed_one_in)):
+                total.value[0, pl.ds(k + 1, 1)] = jnp.sum(gains[...], axis=0, keepdims=True)
+            for k, gains in enumerate((q_gain_zero, k_gain_zero, q_gain_one, k_gain_one)):
                 total.value[0, pl.ds(4, 1), pl.ds(k * HD, HD)] = jnp.sum(
-                    head_gains[k], axis=0, keepdims=True
+                    gains[...], axis=0, keepdims=True
                 )
-            for k in range(LAYERS):
-                total.value[0, pl.ds(8 + 8 * k, 8)] = heads_below[k]
+            for k, heads in enumerate((heads_zero, heads_one)):
+                total.value[0, pl.ds(8 + 8 * k, 8)] = heads[...]
 
         for k in range(total.stages):
 
@@ -1459,8 +1499,8 @@
         sums(i)
         totals(i)
 
-    last_sum = first_step + 9 + 2 * BLOCKS + 1
-    loop(max(scatter.steps, last_sum, first_total + 2 + total.stages), step)
+    loop(max(scatter.steps, first_total + 1 + total.stages), step)
+    close_attend()
     total.finish(total_v)
     total_out = pltpu.make_async_copy(total_v, total_o, out_sem.at[2, 0])
     total_out.start()
@@ -1474,6 +1514,48 @@
 
     loop(GROUPS, drain)
     total_out.wait()
+
+
+def widen_kernel(heads_wide, keys_wide, low_in, *refs):
+    below, above = refs[0:5], refs[5:10]
+    stream_o, gate_o, up_o, down_o, q_o, k_o, v_o, out_o = refs[10:]
+    stream_o[...] = low_in[...].astype(F32)
+    for depth, made in enumerate((below, above)):
+        gate_o[depth] = made[0][...].astype(F32)
+        up_o[depth] = made[1][...].astype(F32)
+        down_o[depth] = made[2][...].astype(F32)
+        q_o[depth] = made[3][:, :heads_wide].astype(F32)
+        k_o[depth] = made[3][:, heads_wide : heads_wide + keys_wide].astype(F32)
+        v_o[depth] = made[3][:, heads_wide + keys_wide :].astype(F32)
+        out_o[depth] = made[4][...].astype(F32)
+
+
+def widen(stream_low, below, above, heads_wide, keys_wide):
+    cuts = 4
+
+    def cut(shape):
+        return pl.BlockSpec((shape[0] // cuts, shape[1]), lambda i: (i, 0))
+
+    def pair(shape):
+        return pl.BlockSpec((2, shape[0] // cuts, shape[1]), lambda i: (0, i, 0))
+
+    share = below[0].shape[0]
+    shapes = [
+        below[0].shape, below[1].shape, below[2].shape, (share, heads_wide), (share, keys_wide),
+        (share, keys_wide), below[4].shape,
+    ]
+    inputs = [stream_low, *below, *above]
+    return pl.pallas_call(
+        partial(widen_kernel, heads_wide, keys_wide),
+        grid=(cuts,),
+        out_shape=(
+            jax.ShapeDtypeStruct(stream_low.shape, F32),
+            *(jax.ShapeDtypeStruct((2, *shape), F32) for shape in shapes),
+        ),
+        in_specs=[cut(array.shape) for array in inputs],
+        out_specs=(cut(stream_low.shape), *(pair(shape) for shape in shapes)),
+        compiler_params=pltpu.CompilerParams(vmem_limit_bytes=VMEM_LIMIT),
+    )(*inputs)
 
 
 def call(kernel, collective_id, in_specs, outs, scratch, flops, out_spec=ANY):
@@ -1543,33 +1625,27 @@
     ]
     smem = pl.BlockSpec(memory_space=pltpu.SMEM)
 
-    def attention_back(depth, collective_id, mixed_grad, logits, saved, q_raw, k_raw, normed):
+    attend_back_outs = [
+        ((rows, heads_wide), BF), ((rows, keys_wide), BF), ((rows, keys_wide), BF),
+        ((rows, LANES), BF), ((8, width), F32), ((8, HD), F32), ((8, HD), F32),
+    ]
+    attend_back_scratch = [
+        pltpu.VMEM((rows, heads_wide), BF), pltpu.VMEM((heads_wide // HD, rows, 1), F32),
+        pltpu.VMEM((rows, heads_wide), F32), pltpu.VMEM((key_heads, rows, HD), F32),
+        pltpu.VMEM((key_heads, rows, HD), F32), pltpu.VMEM((key_heads, 2, rows, HD), BF),
+        pltpu.VMEM((key_heads, 2, rows, HD), BF), dma(key_heads), dma(key_heads),
+    ]
+
+    def attend_back_in(mixed_grad, logits, saved, q_raw, k_raw, normed):
         mixed, q_rot, keys, values, norm, attended = saved
-        return call(
-            partial(attend_back_kernel, depth),
-            collective_id,
-            [smem] + [WHOLE] * 14,
-            [
-                ((rows, heads_wide), BF), ((rows, keys_wide), BF), ((rows, keys_wide), BF),
-                ((rows, LANES), BF), ((8, width), F32), ((8, HD), F32), ((8, HD), F32),
-            ],
-            [
-                pltpu.VMEM((rows, heads_wide), BF), pltpu.VMEM((heads_wide // HD, rows, 1), F32),
-                pltpu.VMEM((rows, heads_wide), F32), pltpu.VMEM((key_heads, rows, HD), F32),
-                pltpu.VMEM((key_heads, rows, HD), F32), pltpu.VMEM((key_heads, 2, rows, HD), BF),
-                pltpu.VMEM((key_heads, 2, rows, HD), BF), dma(key_heads), dma(key_heads),
-            ],
-            3_000_000_000,
-            WHOLE,
-        )(
+        return (
             prefixes, mixed_grad, logits, attended, q_rot, keys, values, norm, q_raw, k_raw,
             query_gain, key_gain, cos, sin, normed,
         )
 
     made_shapes = [
         ((share, units), BF), ((share, units), BF), ((units, share), BF),
-        ((share, heads_wide), BF), ((share, keys_wide), BF), ((share, keys_wide), BF),
-        ((heads_wide, share), BF),
+        ((share, heads_wide + 2 * keys_wide), BF), ((heads_wide, share), BF),
     ]
     scatter_scratch = Scatter.scratch(plane_count, share, unit)
 
@@ -1652,9 +1728,15 @@
         + pair_scratch,
         24_000_000_000,
     )(mixed_one, x_one, cot_flat, output_weight, feed_gain, gate_weight, up_weight, down_weight)
-    q_low, k_low, v_low, l_low, heads_one, q_gain_one, k_gain_one = attention_back(
-        1, 6, mixed_grad, logits, saved_one, q_raw, k_raw, normed_one
-    )
+    q_low, k_low, v_low, l_low, heads_one, q_gain_one, k_gain_one = call(
+        partial(attend_back_kernel, 1),
+        6,
+        [smem] + [WHOLE] * 14,
+        attend_back_outs,
+        attend_back_scratch,
+        3_000_000_000,
+        WHOLE,
+    )(*attend_back_in(mixed_grad, logits, saved_one, q_raw, k_raw, normed_one))
     gate_low, up_low, first_low, grad, low, mixed_grad, gain_one, feed_zero, *made_one = call(
         partial(back_kernel, size, plane_sizes, 1, rows, width),
         2,
@@ -1685,47 +1767,44 @@
         middle_zero, feed_gain, output_weight,
         two_one, gate_low, up_low, cot_flat, hidden_one, normed_one, low, mixed_one,
     )
-    q_low, k_low, v_low, l_low, heads_zero, q_gain_zero, k_gain_zero = attention_back(
-        0, 7, mixed_grad, logits_zero, saved_zero, q_raw_zero, k_raw_zero, normed_zero
-    )
-    gain_rows = jnp.stack([gain_one, feed_zero, feed_one])
-    head_gains = jnp.stack([q_gain_zero, k_gain_zero, q_gain_one, k_gain_one])
-    heads_below = jnp.stack([heads_zero, heads_one])
     below_rows = 8 * LAYERS
     stages = plane_count.bit_length() - 1 + size.bit_length() - 1
     stream_low, result, totals, *made_zero = call(
         partial(last_kernel, size, plane_sizes, 0, rows, width),
         3,
-        [WHOLE] * 8 + [ANY, ANY, WHOLE] + [ANY] * 12,
+        [smem] + [WHOLE] * 14 + [WHOLE] * 7 + [ANY, ANY, WHOLE] + [ANY] * 11,
         [
             ((rows, width), BF), ((rows, width), BF), ((8 + below_rows, width), F32), *made_shapes,
         ],
-        [
+        [pltpu.VMEM(shape, kind) for shape, kind in attend_back_outs]
+        + attend_back_scratch
+        + [
             pltpu.VMEM((width, heads_wide), BF), pltpu.VMEM((width, keys_wide), BF),
             pltpu.VMEM((width, keys_wide), BF), pltpu.VMEM((rows, width), BF),
             pltpu.VMEM((rows, width), F32), pltpu.VMEM((8, width), F32),
             pltpu.VMEM((rows, width), BF), pltpu.VMEM((rows, units), BF),
             pltpu.VMEM((8 + below_rows, width), F32), dma(6), dma(3, GROUPS),
         ]
-        + landed + sum_scratch + landed + sum_scratch + Total.scratch(8 + below_rows, width, stages) + scatter_scratch,
-        16_000_000_000,
+        + landed + sum_scratch + landed + sum_scratch
+        + Total.scratch(8 + below_rows, width, stages) + scatter_scratch,
+        19_000_000_000,
     )(
-        q_low, k_low, v_low, l_low, heads_padded, gain_rows, head_gains, heads_below, stream_flat,
+        *attend_back_in(mixed_grad, logits_zero, saved_zero, q_raw_zero, k_raw_zero, normed_zero),
+        heads_padded, gain_one, feed_zero, feed_one, q_gain_one, k_gain_one, heads_one, stream_flat,
         grad, attention_gain, query_weight, key_weight, value_weight, down_part,
-        two_zero, gate_low, up_low, first_low, hidden_zero, normed_zero, low, mixed_zero,
+        two_zero, gate_low, up_low, first_low, hidden_zero, low, mixed_zero,
     )
+    stream_grad, *weights = widen(stream_low, made_zero, made_one, heads_wide, keys_wide)
+
     def own(array, wide_share):
         return lax.dynamic_slice_in_dim(array, here * wide_share, wide_share, array.ndim - 1)
 
     gains = own(totals[:4], share)
     head_gains = own(totals[4, : 4 * HD].reshape(2, 2, HD), HD // plane_count)
     heads = own(totals[8:].reshape(LAYERS, 8, width)[:, :gates], share)
-    weights = [
-        jnp.stack([made_zero[entry], made_one[entry]]).astype(F32) for entry in range(7)
-    ]
     return (
         result.reshape(seq_count, row_count, width),
-        stream_low.astype(F32).reshape(seq_count, row_count, width),
+        stream_grad.reshape(seq_count, row_count, width),
         gains[0:2],
         weights[3],
         weights[4],

time: 672 us -> 639 us (0.951)
  Pallas kernels: 638 us -> 620 us
  other arithmetic: 18.6 us -> 2 us
    pallas_call x1, Pallas kernels: 168 us -> 153 us  [shards(): call(partial(back_kernel, size, plane_sizes, 1, rows, width), 2, [WHOLE]...]
    convert_element_type x7 -> x0, other arithmetic: 10.6 us -> none  [shards(): jnp.stack([made_zero[entry], made_one[entry]]).astype(F32)]
where the time goes in v4:
time: 639 us; the launch traced here: 631 us
  Pallas kernels  620 us (97%)
  local copies, waits for them, and re-layouts  6.79 us (1%)
    pallas_call x1, Pallas kernels, shards(): call(partial(last_kernel, size, plane_sizes, 0, rows, width), 3, [smem] +...  165 us
    pallas_call x1, Pallas kernels, shards(): call(partial(back_kernel, size, plane_sizes, 1, rows, width), 2, [WHOLE]...  153 us
    pallas_call x1, Pallas kernels, shards(): call(partial(forward_kernel, size, 0, rows, width), 0, [WHOLE, ANY, ANY,...  115 us
    pallas_call x1, Pallas kernels, shards(): call(partial(turn_kernel, size, 1, rows, width), 1, [WHOLE, ANY, ANY, ANY...  112 us
    pallas_call x1, Pallas kernels, shards(): call(partial(first_kernel, 0), 4, [smem, WHOLE, WHOLE, ANY, ANY, ANY] + [...  26.6 us
    pallas_call x1, Pallas kernels, shards(): call(partial(attend_back_kernel, 1), 6, [smem] + [WHOLE] * 14, attend_bac...  22.2 us
    pallas_call x1, Pallas kernels, shards(): call(partial(attend_kernel, 1), 5, [smem] + [WHOLE] * 8, attend_outs, att...  18.2 us

profile of v4, /device:TPU:0, one launch (start us, length us, event | category | flops | bytes accessed | tf_op | source)
XLA Modules:
  0.0 631.2 jit_solution(15116781642702880788)
XLA Ops:
  0.6 0.0 copy-start.1
  0.7 1.0 fusion
  1.7 1.0 pad_maximum_fusion
  2.7 0.0 copy-done.1
  2.7 0.5 copy.29
  3.2 1.2 pad.4.gh.refs_15_
  5.0 26.6 %shard_map.254 = (bf16[512,512]{1,0:T(8,128)(2,1)}, bf16[512,512]{1,0:T(8,128)(2,1)}, bf16[2,2,512,128]{3,2,1,0:T(8,128)(2,1)}, bf16[2,2,512,128]{3,2,1,0:T(8,12...) custom-call(s32[1]{0:T(128)S(6)} %copy.35.prefix.refs_0_, ...), custom_call_target="tpu_custom_call" | custom-call | flops 3500000000 | bytes 40000000 | tf_op jit(solution)/shard_map/pallas_call | solution.py:1652
  31.6 114.6 %shard_map.255 = (f32[512,2048]{1,0:T(8,128)}, bf16[512,2048]{1,0:T(8,128)(2,1)}, bf16[512,1536]{1,0:T(8,128)(2,1)}, bf16[512,1536]{1,0:T(8,128)(2,1)}, bf16[512...) custom-call(bf16[512,512]{1,0:T(8,128)(2,1)} %get-tuple-element.86.m, ...), custom_call_target="tpu_custom_call" | custom-call | flops 12999999488 | bytes 40000000 | tf_op jit(solution)/shard_map/pallas_call | solution.py:1673
  146.3 18.2 %shard_map.256 = (bf16[512,512]{1,0:T(8,128)(2,1)}, bf16[512,512]{1,0:T(8,128)(2,1)}, bf16[2,2,512,128]{3,2,1,0:T(8,128)(2,1)}, bf16[2,2,512,128]{3,2,1,0:T(8,12...) custom-call(s32[1]{0:T(128)S(6)} %copy.35.prefix.refs_0_, f32[512,512]{1,0:T(8,128)} %get-tuple-element.87.q_raw.refs_8_, ...), custom_call_target="tpu_custom_call" | custom-call | flops 1000000000 | bytes 40000000 | tf_op jit(solution)/shard_map/pallas_call | solution.py:1700
  164.5 111.9 %shard_map.257 = (bf16[512,2048]{1,0:T(8,128)(2,1)}, bf16[512,1536]{1,0:T(8,128)(2,1)}, bf16[512,2048]{1,0:T(8,128)(2,1)}, bf16[512,1536]{1,0:T(8,128)(2,1)}, bf...) custom-call(bf16[512,512]{1,0:T(8,128)(2,1)} %get-tuple-element.91.m, ...), custom_call_target="tpu_custom_call" | custom-call | flops 24000000000 | bytes 40000000 | tf_op jit(solution)/shard_map/pallas_call | solution.py:1710
  276.4 22.2 %shard_map.258 = (bf16[512,512]{1,0:T(8,128)(2,1)}, bf16[512,256]{1,0:T(8,128)(2,1)}, bf16[512,256]{1,0:T(8,128)(2,1)}, bf16[512,128]{1,0:T(8,128)(2,1)}, f32[8,...) custom-call(s32[1]{0:T(128)S(6)} %copy.35.prefix.refs_0_, f32[512,512]{1,0:T(8,128)} %get-tuple-element.93.refs_1_, ...), custom_call_target="tpu_custom_call" | custom-call | flops 3000000000 | bytes 40000000 | tf_op jit(solution)/shard_map/pallas_call | solution.py:1731
  298.6 153.0 %shard_map.259 = (bf16[512,1536]{1,0:T(8,128)(2,1)}, bf16[512,1536]{1,0:T(8,128)(2,1)}, bf16[512,2048]{1,0:T(8,128)(2,1)}, f32[512,2048]{1,0:T(8,128)}, bf16[512...) custom-call(bf16[512,512]{1,0:T(8,128)(2,1)} %get-tuple-element.100., ...), custom_call_target="tpu_custom_call" | custom-call | flops 25999998976 | bytes 40000000 | tf_op jit(solution)/shard_map/pallas_call | solution.py:1740
  451.7 164.6 %shard_map.260 = (bf16[512,2048]{1,0:T(8,128)(2,1)}, bf16[512,2048]{1,0:T(8,128)(2,1)}, f32[24,2048]{1,0:T(8,128)}, bf16[256,1536]{1,0:T(8,128)(2,1)}, bf16[256,...) custom-call(s32[1]{0:T(128)S(6)} %copy.35.prefix.refs_0_, ...), custom_call_target="tpu_custom_call" | custom-call | flops 19000000512 | bytes 40000000 | tf_op jit(solution)/shard_map/pallas_call | solution.py:1772
  616.3 0.0 copy-start
  616.3 9.3 %shard_map.261 = (f32[512,2048]{1,0:T(8,128)}, f32[2,256,1536]{2,1,0:T(8,128)}, f32[2,256,1536]{2,1,0:T(8,128)}, f32[2,1536,256]{2,1,0:T(8,128)}, f32[2,256,512]...) custom-call(bf16[512,2048]{1,0:T(8,128)(2,1)} %get-tuple-element.138.low_in, ...), custom_call_target="tpu_custom_call" | custom-call | tf_op jit(solution)/shard_map/pallas_call | solution.py:1548
  625.6 0.0 copy-done
  625.6 0.6 dynamic-slice_bitcast_fusion
  626.3 0.7 fusion.1
  626.9 0.6 constant_dynamic-slice_fusion.2
  627.6 3.2 copy.36
  (6 shorter events, 0.0 us)
Async XLA Ops:
  0.6 2.0 copy-start.1
  616.3 9.3 %copy-start = (f32[24,2048]{1,0:T(8,128)S(1)}, f32[24,2048]{1,0:T(8,128)}, u32[]{:S(2)}) copy-start(f32[24,2048]{1,0:T(8,128)} %get-tuple-element.150) | copy-start | bytes 589828

commit v5 on v4

--- a/solution.py
+++ b/solution.py
@@ -25,6 +25,7 @@
 PIECES = 2
 GROUP = 4
 STRIP = 16
+UNROLL = 2
 VMEM_LIMIT = 63 * 1024 * 1024
 
 
@@ -51,12 +52,12 @@
     return lax.dot_general(gradient, weight, (((1,), (1,)), ((), ())), preferred_element_type=F32)
 
 
-def loop(count, body):
+def loop(count, body, unroll=1):
     def step(i, carry):
         body(i)
         return carry
 
-    lax.fori_loop(0, count, step, 0)
+    lax.fori_loop(0, count, step, 0, unroll=unroll)
 
 
 def rows_of(r, block):
@@ -160,10 +161,9 @@
 
                 def strip(i, col=col):
                     at = pl.ds(pl.multiple_of(r * self.block + i * STRIP, STRIP), STRIP)
-                    total = self.part[at, col].astype(F32) + self.landed[0, at, col].astype(F32)
-                    self.part[at, col] = total.astype(BF)
-
-                loop(self.block // STRIP, strip)
+                    self.part[at, col] = self.part[at, col] + self.landed[0, at, col]
+
+                loop(self.block // STRIP, strip, True)
 
                 @pl.when(self.chain.mid)
                 def _(p=p):
@@ -184,7 +184,7 @@
                 total = self.part[at, :].astype(F32) + self.landed[self.cross, at, :].astype(F32)
                 self.spread[at, :] = make(at, total)
 
-            loop(self.block // STRIP, strip)
+            loop(self.block // STRIP, strip, UNROLL)
             self.out_hop(r).start()
 
     def receive(self, g):
@@ -211,13 +211,14 @@
         loop(BLOCKS, block)
 
 
-PARTS = GROUP
+PARTS = 4
+STRIDE = GROUP // PARTS
 GROUPS = BLOCKS // GROUP
 STEPS = 2 * BLOCKS + 1
 
 
 def two_sums(s, first, second, made_one, between, ahead, made_two, after):
-    @pl.when(s < BLOCKS)
+    @pl.when((s >= 0) & (s < BLOCKS))
     def _():
         first.relay(s)
 
@@ -227,14 +228,17 @@
 
     @pl.when((s >= GROUP) & (s < BLOCKS + GROUP))
     def _():
-        part = lax.rem(s - GROUP, PARTS)
-        group = lax.div(s - GROUP, PARTS)
-
-        @pl.when(part == 0)
+        place = lax.rem(s - GROUP, GROUP)
+        group = lax.div(s - GROUP, GROUP)
+
+        @pl.when(place == 0)
         def _():
             first.receive(group)
 
-        between(group, part)
+        outer = first.chain.outer
+        begin = jnp.where(outer, jnp.where(place == 0, 0, PARTS), lax.div(place + STRIDE - 1, STRIDE))
+        stop = jnp.where(outer, PARTS, lax.div(place, STRIDE) + 1)
+        lax.fori_loop(begin, stop, lambda part, carry: (between(group, part), carry)[1], 0)
 
     @pl.when((s >= BLOCKS) & (s < 2 * BLOCKS))
     def _():
@@ -320,11 +324,19 @@
         return [self.partner(bit) for bit in self.bits]
 
 
+BEFORE = 6
+PACE = 11
+ONE_AFTER = 3
+EARLY = BLOCKS + GROUP - 1
+TURN_PACE = 2
+OUTER_AHEAD = 4
+
+
 class Scatter:
-    SLOTS = (2, 4, 4, 4)
-    KEPT = (2, 3, 3, 3)
+    SLOTS = (2, 6, 6, 6)
+    KEPT = (2, 4, 4, 4)
     RESULTS = 2
-    LAGS = (0, 1, 4, 7, 10, 13)
+    LAGS = (0, 1, 5, 9, 13, 17)
 
     def __init__(self, plane, refs, whole, parts, groups, share, tile):
         self.plane = plane
@@ -443,10 +455,8 @@
             spot_on = lax.rem(u, self.KEPT[stage + 1])
 
             def one(j):
-                far = keep[spot, half + j].astype(F32) + land[slot, half + j].astype(F32)
-                send_on[slot_on, j] = far.astype(BF)
-                near = keep[spot, j].astype(F32) + land[slot, j].astype(F32)
-                keep_on[spot_on, j] = near.astype(BF)
+                send_on[slot_on, j] = keep[spot, half + j] + land[slot, half + j]
+                keep_on[spot_on, j] = keep[spot, j] + land[slot, j]
 
             loop(half, one)
             self.push(stage + 1, u)
@@ -457,8 +467,7 @@
             def _():
                 self.results(u - self.RESULTS, lambda copy: copy.wait())
 
-            total = keep[spot, 0].astype(F32) + land[slot, 0].astype(F32)
-            self.made[place] = total.astype(BF)
+            self.made[place] = keep[spot, 0] + land[slot, 0]
             self.results(u, lambda copy: copy.start())
 
         @pl.when(u + slots < self.units)
@@ -509,13 +518,19 @@
 
 class Total:
     def __init__(self, plane, size, refs, own):
-        self.plane, self.own = plane, own
         self.value, self.land, self.s_sem, self.r_sem = refs
         spot = lax.axis_index("tensor")
-        bits = [1 << k for k in range(size.bit_length() - 1)]
-        self.targets = [plane.partner(bit) for bit in plane.bits]
-        self.across = [{"tensor": flip(spot, bit)} for bit in bits]
-        self.stages = len(self.targets) + len(bits)
+        rows, first = pl.ds(0, self.value.shape[1]), pl.ds(0, own)
+        near, *rest = plane.orders[0]
+        across = [({"tensor": flip(spot, 1 << k)}, first) for k in range(size.bit_length() - 1)]
+        self.across = [target for target, unused in across]
+        self.stages = [(plane.partner(near), rows), *across]
+        self.stages += [(plane.partner(bit), rows) for bit in rest]
+        self.times = [0, 1]
+        for unused in across:
+            self.times.append(self.times[-1] + 2)
+        for unused in rest:
+            self.times.append(self.times[-1] + 3)
 
     @staticmethod
     def scratch(rows, width, stages):
@@ -527,33 +542,30 @@
         ]
 
     def copy(self, k):
-        count = len(self.targets)
-        rows = slice(None) if k < count else pl.ds(0, self.own)
+        target, rows = self.stages[k]
         return pltpu.make_async_remote_copy(
             src_ref=self.value.at[k, rows],
             dst_ref=self.land.at[k, rows],
             send_sem=self.s_sem.at[k],
             recv_sem=self.r_sem.at[k],
-            device_id=(self.targets + self.across)[k],
+            device_id=target,
             device_id_type=MESH,
         )
 
+    def take(self, k, target):
+        self.copy(k).wait_recv()
+        rows = self.stages[k][1]
+        target[...] = self.value[k]
+        target[rows] = self.value[k, rows] + self.land[k, rows]
+
     def start(self, k):
         if k > 0:
-            self.copy(k - 1).wait_recv()
-            rows = slice(None) if k - 1 < len(self.targets) else pl.ds(0, self.own)
-            if k - 1 >= len(self.targets):
-                self.value[k] = self.value[k - 1]
-            self.value[k, rows] = self.value[k - 1, rows] + self.land[k - 1, rows]
+            self.take(k - 1, self.value.at[k])
         self.copy(k).start()
 
     def finish(self, target):
-        last = self.stages - 1
-        self.copy(last).wait_recv()
-        rows = pl.ds(0, self.own)
-        target[...] = self.value[last]
-        target[rows] = self.value[last, rows] + self.land[last, rows]
-        for k in range(self.stages):
+        self.take(len(self.stages) - 1, target)
+        for k in range(len(self.stages)):
             self.copy(k).wait_send()
 
 
@@ -580,14 +592,99 @@
     return (key <= query) | (key + offset < prefix)
 
 
-def attend(prefix, q_raw, k_raw, v, logits, query_gain, key_gain, cos, sin,
-           mixed_o, q_o, keys_o, values_o, norm_o, attended_o, scratch, half):
-    high, low, out, send_sem, land_sem = scratch
+def key_strip(raw, v, keys, values, gain, cos, sin, j, at):
+    keys[j, at, :] = head_norm(raw[at, head_at(j)], gain, cos[at, :], sin[at, :]).astype(BF)
+    values[j, at, :] = v[at, head_at(j)]
+
+
+def attend(prefix, q_raw, logits, query_gain, cos, sin, keys, values,
+           mixed_o, q_o, norm_o, attended_o, scratch, half, arrived):
+    high, low, out = scratch
     rows = q_raw.shape[0]
     span = rows // GROUPS
+    key_heads = keys.shape[1]
+    shared = q_raw.shape[1] // HD // key_heads
+    scale = HD ** (-0.5)
+
+    def own(g):
+        at = rows_of(g, span)
+        mask = seen(span, g * span, rows, half * rows, prefix)
+        for h in range(key_heads * shared):
+            j = h // shared
+            query = head_norm(q_raw[at, head_at(h)], query_gain, cos[at, :], sin[at, :]).astype(BF)
+            q_o[at, head_at(h)] = query
+            scores = jnp.where(mask, back_product(query, keys[0, j]) * scale, masked)
+            top = jnp.max(scores, axis=1, keepdims=True)
+            weights = jnp.exp(scores - top)
+            high[h, at, :] = top
+            low[h, at, :] = jnp.sum(weights, axis=1, keepdims=True)
+            out[at, head_at(h)] = matmul(weights.astype(BF), values[0, j])
+
+    loop(GROUPS, own)
+
+    @pl.when(half == 1)
+    def _():
+        for h in range(key_heads * shared):
+            j = h // shared
+            if h % shared == 0:
+                arrived(j)
+
+            def other(g, h=h, j=j):
+                at = rows_of(g, span)
+                scores = back_product(q_o[at, head_at(h)], keys[1, j]) * scale
+                before = high[h, at, :]
+                top = jnp.maximum(before, jnp.max(scores, axis=1, keepdims=True))
+                weights = jnp.exp(scores - top)
+                shrink = jnp.exp(before - top)
+                high[h, at, :] = top
+                low[h, at, :] = low[h, at, :] * shrink + jnp.sum(weights, axis=1, keepdims=True)
+                out[at, head_at(h)] = out[at, head_at(h)] * shrink + matmul(
+                    weights.astype(BF), values[1, j]
+                )
+
+            loop(GROUPS, other)
+
+    def close(g):
+        at = rows_of(g, span)
+        open_gate = jax.nn.sigmoid(logits[at, :])
+        for h in range(key_heads * shared):
+            total = low[h, at, :]
+            norm_o[h, at, :] = high[h, at, :] + jnp.log(total)
+            attended = out[at, head_at(h)] * (1.0 / total)
+            attended_o[at, head_at(h)] = attended
+            mixed_o[at, head_at(h)] = (attended * open_gate[:, h : h + 1]).astype(BF)
+
+    loop(GROUPS, close)
+
+
+def attend_scratch(rows, heads_wide):
+    return [
+        pltpu.VMEM((heads_wide // HD, rows, 1), F32),
+        pltpu.VMEM((heads_wide // HD, rows, 1), F32),
+        pltpu.VMEM((rows, heads_wide), F32),
+    ]
+
+
+def attend_kernel(
+    depth, prefix, q_raw, logits, query_gain, cos, sin, keys, values,
+    mixed_o, q_o, norm_o, attended_o, *scratch,
+):
+    half = lax.axis_index("ctx")
+    attend(prefix[0], q_raw, logits, query_gain[depth : depth + 1, :], cos, sin, keys, values,
+           mixed_o, q_o, norm_o, attended_o, scratch, half, lambda j: None)
+
+
+def first_kernel(
+    depth, prefix, stream, gain, wq, wk, wv, gh, query_gain, key_gain, cos, sin,
+    mixed_o, q_o, norm_o, attended_o, keys_o, values_o, normed_o, q_raw, k_raw, logits,
+    v, wq_v, wk_v, wv_v, load_sem, send_sem, land_sem, *scratch,
+):
+    half = lax.axis_index("ctx")
+    loads = load_all([(wk.at[depth], wk_v), (wv.at[depth], wv_v), (wq.at[depth], wq_v)], load_sem)
+    greet([{"ctx": 1 - half}], {"ctx": 1 - half}, half < 0)
+    rows = stream.shape[0]
+    span = rows // GROUPS
     key_heads = k_raw.shape[1] // HD
-    shared = q_raw.shape[1] // k_raw.shape[1]
-    scale = HD ** (-0.5)
 
     def copy(j, which):
         ref = (keys_o, values_o)[which]
@@ -600,134 +697,50 @@
             device_id_type=MESH,
         )
 
-    for j in range(key_heads):
-
-        def key_rows(g, j=j):
-            at = rows_of(g, span)
-            made = head_norm(k_raw[at, head_at(j)], key_gain, cos[at, :], sin[at, :])
-            keys_o[0, j, at, :] = made.astype(BF)
-            values_o[0, j, at, :] = v[at, head_at(j)]
-
-        loop(GROUPS, key_rows)
-
-        @pl.when(half == 0)
-        def _(j=j):
+    def strip(i):
+        at = rows_of(i, STRIP)
+        value = stream[at, :].astype(F32)
+        normed_o[at, :] = rms_scale(value, gain[depth : depth + 1, :]).astype(BF)
+
+    loop(rows // STRIP, strip, UNROLL)
+    wait_all(loads[:2])
+
+    def project_keys(g):
+        at = rows_of(g, span)
+        k_raw[at, :] = matmul(normed_o[at, :], wk_v[...])
+        v[at, :] = matmul(normed_o[at, :], wv_v[...]).astype(BF)
+        for j in range(key_heads):
+            key_strip(k_raw, v, keys_o.at[0], values_o.at[0], key_gain[depth : depth + 1, :], cos, sin, j, at)
+
+    loop(GROUPS, project_keys)
+
+    @pl.when(half == 0)
+    def _():
+        for j in range(key_heads):
             copy(j, 0).start()
             copy(j, 1).start()
 
-    def own(g):
-        at = rows_of(g, span)
-        mask = seen(span, g * span, rows, half * rows, prefix)
-        for h in range(key_heads * shared):
-            j = h // shared
-            query = head_norm(q_raw[at, head_at(h)], query_gain, cos[at, :], sin[at, :]).astype(BF)
-            q_o[at, head_at(h)] = query
-            scores = jnp.where(mask, back_product(query, keys_o[0, j]) * scale, masked)
-            top = jnp.max(scores, axis=1, keepdims=True)
-            weights = jnp.exp(scores - top)
-            high[h, at, :] = top
-            low[h, at, :] = jnp.sum(weights, axis=1, keepdims=True)
-            out[at, head_at(h)] = matmul(weights.astype(BF), values_o[0, j])
-
-    loop(GROUPS, own)
-
-    @pl.when(half == 1)
-    def _():
-        for h in range(key_heads * shared):
-            j = h // shared
-            if h % shared == 0:
-                copy(j, 0).wait_recv()
-                copy(j, 1).wait_recv()
-
-            def other(g, h=h, j=j):
-                at = rows_of(g, span)
-                scores = back_product(q_o[at, head_at(h)], keys_o[1, j]) * scale
-                before = high[h, at, :]
-                top = jnp.maximum(before, jnp.max(scores, axis=1, keepdims=True))
-                weights = jnp.exp(scores - top)
-                shrink = jnp.exp(before - top)
-                high[h, at, :] = top
-                low[h, at, :] = low[h, at, :] * shrink + jnp.sum(weights, axis=1, keepdims=True)
-                out[at, head_at(h)] = out[at, head_at(h)] * shrink + matmul(
-                    weights.astype(BF), values_o[1, j]
-                )
-
-            loop(GROUPS, other)
-
-    def close(g):
-        at = rows_of(g, span)
-        open_gate = jax.nn.sigmoid(logits[at, :])
-        for h in range(key_heads * shared):
-            total = low[h, at, :]
-            norm_o[h, at, :] = high[h, at, :] + jnp.log(total)
-            attended = out[at, head_at(h)] * (1.0 / total)
-            attended_o[at, head_at(h)] = attended
-            mixed_o[at, head_at(h)] = (attended * open_gate[:, h : h + 1]).astype(BF)
-
-    loop(GROUPS, close)
+    loads[2].wait()
+
+    def project(g):
+        at = rows_of(g, span)
+        q_raw[at, :] = matmul(normed_o[at, :], wq_v[...])
+        logits[at, :] = matmul(normed_o[at, :], gh[depth])
+
+    loop(GROUPS, project)
+
+    def arrived(j):
+        copy(j, 0).wait_recv()
+        copy(j, 1).wait_recv()
+
+    attend(prefix[0], q_raw, logits, query_gain[depth : depth + 1, :], cos, sin, keys_o, values_o,
+           mixed_o, q_o, norm_o, attended_o, scratch, half, arrived)
 
     @pl.when(half == 0)
     def _():
         for j in range(key_heads):
             copy(j, 0).wait_send()
             copy(j, 1).wait_send()
-
-
-def attend_scratch(rows, heads_wide, keys_wide):
-    return [
-        pltpu.VMEM((heads_wide // HD, rows, 1), F32),
-        pltpu.VMEM((heads_wide // HD, rows, 1), F32),
-        pltpu.VMEM((rows, heads_wide), F32),
-        pltpu.SemaphoreType.DMA((keys_wide // HD, 2)),
-        pltpu.SemaphoreType.DMA((keys_wide // HD, 2)),
-    ]
-
-
-def greet_half(half):
-    greet([{"ctx": 1 - half}], {"ctx": 1 - half}, half < 0)
-
-
-def attend_kernel(
-    depth, prefix, q_raw, k_raw, v, logits, query_gain, key_gain, cos, sin,
-    mixed_o, q_o, keys_o, values_o, norm_o, attended_o, *scratch,
-):
-    half = lax.axis_index("ctx")
-    greet_half(half)
-    attend(prefix[0], q_raw, k_raw, v, logits, query_gain[depth : depth + 1, :],
-           key_gain[depth : depth + 1, :], cos, sin,
-           mixed_o, q_o, keys_o, values_o, norm_o, attended_o, scratch, half)
-
-
-def first_kernel(
-    depth, prefix, stream, gain, wq, wk, wv, gh, query_gain, key_gain, cos, sin,
-    mixed_o, q_o, keys_o, values_o, norm_o, attended_o, normed_o, q_raw, k_raw, logits,
-    v, wq_v, wk_v, wv_v, load_sem, *scratch,
-):
-    half = lax.axis_index("ctx")
-    loads = load_all([(wk.at[depth], wk_v), (wv.at[depth], wv_v), (wq.at[depth], wq_v)], load_sem)
-    greet_half(half)
-    rows = stream.shape[0]
-    span = rows // GROUPS
-
-    def strip(i):
-        at = rows_of(i, STRIP)
-        value = stream[at, :].astype(F32)
-        normed_o[at, :] = rms_scale(value, gain[depth : depth + 1, :]).astype(BF)
-
-    loop(rows // STRIP, strip)
-    wait_all(loads)
-
-    def project(g):
-        at = rows_of(g, span)
-        k_raw[at, :] = matmul(normed_o[at, :], wk_v[...])
-        v[at, :] = matmul(normed_o[at, :], wv_v[...]).astype(BF)
-        q_raw[at, :] = matmul(normed_o[at, :], wq_v[...])
-        logits[at, :] = matmul(normed_o[at, :], gh[depth])
-
-    loop(GROUPS, project)
-    attend(prefix[0], q_raw, k_raw, v, logits, query_gain[depth : depth + 1, :],
-           key_gain[depth : depth + 1, :], cos, sin,
-           mixed_o, q_o, keys_o, values_o, norm_o, attended_o, scratch, half)
 
 
 def attend_back(
@@ -873,27 +886,20 @@
     )
 
 
-def attend_back_kernel(depth, *refs):
-    half = lax.axis_index("ctx")
-    greet_half(half)
-    pieces, close = attend_back(half, depth, *refs)
-    for piece in pieces:
-        piece()
-    close()
-
-
 def forward_kernel(
     size, depth, rows, width,
-    mixed, stream, wo, feed_gain, wg, wu, wd, next_gain, wq, wk, wv, gh,
-    middle_o, two_o, slope_o, silu_o, hidden_o, x_o, normed_o, q_o, k_o, v_o, logit_o,
+    mixed, stream, wo, feed_gain, wg, wu, wd, next_gain, wq, wk, wv, gh, key_gain, cos, sin,
+    middle_o, two_o, slope_o, silu_o, hidden_o, x_o, normed_o, q_o, k_o, logit_o, keys_o, values_o,
     *scratch,
 ):
     (wo_v, wg_v, wu_v, wd_v, wq_v, wk_v, wv_v, x_v, middle_v, slope_v, silu_v, hidden_v, q_v, k_v,
-     v_v, logit_v, load_sem, out_sem) = scratch[:18]
+     v_v, logit_v, load_sem, out_sem, keys_v, values_v, keep_sem, send_sem, land_sem) = scratch[:23]
+    half = lax.axis_index("ctx")
+    key_heads = keys_v.shape[0]
     chain = Chain(size)
-    landed = scratch[18]
-    one = Sum(chain, scratch[19:26], (landed, 1), rows, width)
-    two = Sum(chain, scratch[26:33], (landed, 2), rows, width)
+    landed = scratch[23]
+    one = Sum(chain, scratch[24:31], (landed, 1), rows, width)
+    two = Sum(chain, scratch[31:38], (landed, 2), rows, width)
     span = one.block * GROUP
     loads = load_all(
         [(wo.at[depth], wo_v), (stream, x_v), (wg.at[depth], wg_v), (wu.at[depth], wu_v),
@@ -901,7 +907,7 @@
          (wv.at[depth + 1], wv_v)],
         load_sem,
     )
-    chain.greet()
+    chain.greet([{"ctx": 1 - half}])
     tile = wg_v.shape[1] // (PARTS - 1)
     gain_one = feed_gain[depth : depth + 1, :]
     gain_two = next_gain[depth + 1 : depth + 2, :]
@@ -909,6 +915,23 @@
     def out(k, g, src, dst):
         at = rows_of(g, span)
         return pltpu.make_async_copy(src.at[at], dst.at[at], out_sem.at[k, g])
+
+    def keep_keys(g, which):
+        at = rows_of(g, span)
+        src, dst = ((keys_v, keys_o), (values_v, values_o))[which]
+        return pltpu.make_async_copy(src.at[:, at], dst.at[0, :, at], keep_sem.at[which, g])
+
+    def give_keys(g, which):
+        at = rows_of(g, span)
+        src, dst = ((keys_v, keys_o), (values_v, values_o))[which]
+        return pltpu.make_async_remote_copy(
+            src_ref=src.at[:, at],
+            dst_ref=dst.at[1, :, at],
+            send_sem=send_sem.at[which, g],
+            recv_sem=land_sem.at[which, g],
+            device_id={"ctx": 1 - half},
+            device_id_type=MESH,
+        )
 
     loads[0].wait()
 
@@ -976,12 +999,21 @@
         def _():
             out(5, g, middle_v, x_o).start()
 
+        k_v[at, :] = matmul(two.spread[at, :], wk_v[...])
+        v_v[at, :] = matmul(two.spread[at, :], wv_v[...]).astype(BF)
+        for j in range(key_heads):
+            key_strip(k_v, v_v, keys_v, values_v, key_gain[depth + 1 : depth + 2, :], cos, sin, j, at)
+
+        @pl.when(half == 0)
+        def _():
+            give_keys(g, 0).start()
+            give_keys(g, 1).start()
+
+        keep_keys(g, 0).start()
+        keep_keys(g, 1).start()
+        out(8, g, k_v, k_o).start()
         q_v[at, :] = matmul(two.spread[at, :], wq_v[...])
         out(7, g, q_v, q_o).start()
-        k_v[at, :] = matmul(two.spread[at, :], wk_v[...])
-        out(8, g, k_v, k_o).start()
-        v_v[at, :] = matmul(two.spread[at, :], wv_v[...]).astype(BF)
-        out(9, g, v_v, v_o).start()
         logit_v[at, :] = matmul(two.spread[at, :], gh[depth + 1])
         out(10, g, logit_v, logit_o).start()
         out(6, g, two.spread, normed_o).start()
@@ -998,17 +1030,27 @@
         for k, src, dst in (
             (1, one.spread, two_o), (2, slope_v, slope_o), (3, silu_v, silu_o),
             (4, hidden_v, hidden_o), (6, two.spread, normed_o), (7, q_v, q_o),
-            (8, k_v, k_o), (9, v_v, v_o), (10, logit_v, logit_o),
+            (8, k_v, k_o), (10, logit_v, logit_o),
         ):
             out(k, g, src, dst).wait()
+        for which in range(2):
+            keep_keys(g, which).wait()
+
+            @pl.when(half == 0)
+            def _(which=which):
+                give_keys(g, which).wait_send()
+
+            @pl.when(half == 1)
+            def _(which=which):
+                give_keys(g, which).wait_recv()
 
     loop(GROUPS, drain)
 
 
 def turn_kernel(
-    size, depth, rows, width,
+    size, plane_sizes, depth, rows, width,
     mixed, x_in, cot, wo, feed_gain, wg, wu, wd,
-    two_o, hidden_o, down_o, gate_o, up_o, grad_o, low_o, mixed_o, gain_o,
+    two_o, down_o, gate_o, up_o, grad_o, low_o, mixed_o, gain_o, made_o,
     *scratch,
 ):
     (wo_v, wg_v, wu_v, wd_v, middle_v, cot_v, hidden_v, gate_v, up_v, mixed_v, down_v, gain_v,
@@ -1017,13 +1059,19 @@
     landed = scratch[14]
     one = Sum(chain, scratch[15:22], (landed, 1), rows, width)
     two = Sum(chain, scratch[22:29], (landed, 2), rows, width)
+    plane = Plane(*plane_sizes)
+    unit = made_o.shape[1] if made_o.shape[1] < 256 else 256
+    scatter = Scatter(
+        plane, scratch[29:], cot_v, hidden_v, [(made_o, False, hidden_v.shape[1] // unit, [])],
+        width // plane.count, unit,
+    )
     span = one.block * GROUP
     loads = load_all(
         [(wo.at[depth], wo_v), (x_in, middle_v), (cot, cot_v), (wg.at[depth], wg_v),
          (wu.at[depth], wu_v), (wd.at[depth], wd_v)],
         load_sem,
     )
-    chain.greet()
+    chain.greet(plane.partners())
     tile = wg_v.shape[1] // (PARTS - 1)
     gain_one = feed_gain[depth : depth + 1, :]
 
@@ -1076,7 +1124,6 @@
                 + back_product(up_v[at, :], wu_v[col, :]),
             )
             two.offer(g)
-            out(1, g, hidden_v, hidden_o).start()
             out(2, g, gate_v, gate_o).start()
             out(3, g, up_v, up_o).start()
 
@@ -1112,7 +1159,19 @@
         mixed_v[at, :] = back_product(two.spread[at, :], wo_v[...])
         out(7, g, mixed_v, mixed_o).start()
 
-    loop(STEPS, lambda s: two_sums(s, one, two, made_one, between, ahead, made_two, after))
+
+    def step(s):
+        two_sums(s, one, two, made_one, between, ahead, made_two, after)
+        ahead_ticks = jnp.where(chain.outer, OUTER_AHEAD, 0)
+
+        def ticks_before(s):
+            return jnp.where(s > EARLY, (s - EARLY) * TURN_PACE + ahead_ticks, 0)
+
+        lax.fori_loop(
+            ticks_before(s), ticks_before(s + 1), lambda t, carry: (scatter.tick(t), carry)[1], 0
+        )
+
+    loop(max(STEPS, EARLY + -(-scatter.steps // TURN_PACE)), step)
 
     @pl.when(jnp.logical_not(chain.first_mid))
     def _():
@@ -1122,6 +1181,7 @@
     gain_out.start()
     one.close()
     two.close()
+    scatter.close()
 
     def drain(g):
         @pl.when(chain.mid)
@@ -1129,8 +1189,8 @@
             out(5, g, middle_v, grad_o).wait()
 
         for k, src, dst in (
-            (0, one.spread, two_o), (1, hidden_v, hidden_o), (2, gate_v, gate_o),
-            (3, up_v, up_o), (4, down_v, down_o), (6, two.spread, low_o), (7, mixed_v, mixed_o),
+            (0, one.spread, two_o), (2, gate_v, gate_o), (3, up_v, up_o), (4, down_v, down_o),
+            (6, two.spread, low_o), (7, mixed_v, mixed_o),
         ):
             out(k, g, src, dst).wait()
 
@@ -1140,15 +1200,21 @@
 
 def back_kernel(
     size, plane_sizes, depth, rows, width,
-    q_low, k_low, v_low, l_low, gh, x_in, grad_in, attention_gain, wq, wk, wv,
-    wd, wg, wu, slope_in, silu_in, middle_in, feed_gain, wo,
-    two_in, gate_in, up_in, cot_in, hidden_in, normed_in, low_in, mixed_in,
-    gate_o, up_o, first_o, grad_o, low_o, mixed_o, gain_o, feed_gain_o,
-    *rest,
+    *refs,
 ):
-    made, scratch = rest[:5], rest[5:]
-    (wq_v, wk_v, wv_v, wd_v, wg_v, wu_v, wo_v, x_v, grad_v, slope_v, silu_v, gate_v, up_v, mixed_v,
-     gain_v, feed_v, whole_v, parts_v, gh_v, load_sem, row_sem, tile_sem, out_sem) = scratch[:23]
+    (prefix, mixed_grad, logits, attended, q_rot, keys, values, norm, q_raw, k_raw, query_gain, key_gain,
+     cos, sin, normed_in, gh, x_in, grad_in, attention_gain, wq, wk, wv,
+     wd, wg, wu, slope_in, silu_in, middle_in, feed_gain, wo,
+     two_in, gate_in, up_in, low_in, mixed_in,
+     gate_o, up_o, first_o, grad_o, low_o, mixed_o, gain_o, feed_gain_o, heads_o, q_gain_o, k_gain_o,
+     *rest) = refs
+    made, scratch = rest[:4], rest[4:]
+    attend_made, attend_scratch, scratch = scratch[:7], scratch[7:15], scratch[15:]
+    q_low, k_low, v_low, l_low, heads_v, q_gain_v, k_gain_v = attend_made
+    (wq_v, wk_v, wv_v, ring_v, wo_v, x_v, grad_v, slope_v, silu_v, gate_v, up_v, mixed_v,
+     gain_v, feed_v, whole_v, parts_v, gh_v, load_sem, row_sem, tile_sem, out_sem, ring_sem, attend_sem,
+     ) = scratch[:23]
+    half = lax.axis_index("ctx")
     chain = Chain(size)
     landed = scratch[23]
     one = Sum(chain, scratch[24:31], (landed, 1), rows, width)
@@ -1156,7 +1222,17 @@
     plane = Plane(*plane_sizes)
     share = width // plane.count
     unit = min(256, wk_v.shape[1])
-    units_wide, heads_wide, keys_wide = wg_v.shape[1], wq_v.shape[1], wk_v.shape[1]
+    units_wide, heads_wide, keys_wide = gate_v.shape[1], wq_v.shape[1], wk_v.shape[1]
+    mixed_grad_v, attended_v, q_raw_v, q_grad_v = (
+        grad_v.at[:, pl.ds(quarter * heads_wide, heads_wide)] for quarter in range(4)
+    )
+    normed_v = two.part
+    grad_low, inner, k_grad, v_grad, *given = attend_scratch
+    pieces, close_attend = attend_back(
+        half, depth, prefix, mixed_grad_v, logits, attended_v, q_rot, keys, values, norm, q_raw_v, k_raw,
+        query_gain, key_gain, cos, sin, normed_v, *attend_made,
+        grad_low, inner, q_grad_v, k_grad, v_grad, *given,
+    )
     parts_heads = parts_v.at[:, pl.ds(0, heads_wide)]
     heads_parts = [
         (q_low, parts_heads),
@@ -1168,25 +1244,59 @@
         [
             (made[0], True, units_wide // unit, [(two_in, whole_v), (gate_in, parts_v)]),
             (made[1], True, units_wide // unit, [(up_in, parts_v)]),
-            (made[2], False, units_wide // unit, [(cot_in, whole_v), (hidden_in, parts_v)]),
-            (made[3], True, (heads_wide + 2 * keys_wide) // unit, [(normed_in, whole_v), *heads_parts]),
-            (made[4], False, heads_wide // unit, [(low_in, whole_v), (mixed_in, parts_heads)]),
+            (made[2], True, (heads_wide + 2 * keys_wide) // unit, [(normed_in, whole_v), *heads_parts]),
+            (made[3], False, heads_wide // unit, [(low_in, whole_v), (mixed_in, parts_heads)]),
         ],
         share, unit,
     )
     span = one.block * GROUP
     below = depth - 1
+    attend_loads = load_all(
+        [(mixed_grad, mixed_grad_v), (attended, attended_v), (normed_in, normed_v), (q_raw, q_raw_v)],
+        attend_sem,
+    )
     loads = load_all(
         [(wq.at[depth], wq_v), (wk.at[depth], wk_v), (wv.at[depth], wv_v), (gh.at[depth], gh_v),
-         (grad_in, grad_v),
-         (wd.at[below], wd_v), (wg.at[below], wg_v), (wu.at[below], wu_v), (wo.at[below], wo_v)],
+         (wo.at[below], wo_v)],
         load_sem,
     )
+    grad_load = pltpu.make_async_copy(grad_in, grad_v, load_sem.at[5])
 
     def row_load(src, g, k):
         return pltpu.make_async_copy(src.at[rows_of(g, span)], x_v, row_sem.at[k])
 
-    tile = wg_v.shape[1] // (PARTS - 1)
+    tile = units_wide // (PARTS - 1)
+    strip_wide = wide(width)
+    fetches = PARTS - 1 + 2 * (width // strip_wide)
+    slots = ring_v.shape[0]
+
+    def fetch(k, act):
+        slot, place = lax.rem(k, slots), lax.rem(k, fetches)
+        pair = jnp.maximum(place - (PARTS - 1), 0)
+
+        @pl.when(place < PARTS - 1)
+        def _():
+            src = wd.at[below, rows_of(place, tile)]
+            act(pltpu.make_async_copy(src, ring_v.at[slot, pl.ds(0, tile)], ring_sem.at[slot]))
+
+        for which, weight in enumerate((wg, wu)):
+
+            @pl.when((place >= PARTS - 1) & (lax.rem(pair, 2) == which))
+            def _(weight=weight):
+                src = weight.at[below, rows_of(lax.div(pair, 2), strip_wide)]
+                dst = ring_v.at[slot, :, pl.ds(0, units_wide)]
+                act(pltpu.make_async_copy(src, dst, ring_sem.at[slot]))
+
+    def fetched(k):
+        fetch(k, lambda copy: copy.wait())
+
+    def used(k):
+        @pl.when(k + slots < GROUPS * fetches)
+        def _():
+            fetch(k + slots, lambda copy: copy.start())
+
+    for k in range(slots):
+        fetch(jnp.int32(k), lambda copy: copy.start())
 
     def tile_load(src, dst, g, part, k):
         col = columns(part, tile)
@@ -1201,8 +1311,8 @@
         tile_load(silu_in, silu_v, 0, part, 1).start()
 
     loop(PARTS - 1, first_tiles)
-    chain.greet(plane.partners())
-    wait_all(loads[:4])
+    chain.greet([*plane.partners(), {"ctx": 1 - half}])
+    wait_all(attend_loads)
     gain_one = attention_gain[depth : depth + 1, :]
     gain_two = feed_gain[below : below + 1, :]
 
@@ -1222,11 +1332,15 @@
         )
         one.offer(g)
 
-    loop(GROUPS, start)
     gain_v[...] = jnp.zeros_like(gain_v)
     feed_v[...] = jnp.zeros_like(feed_v)
-    wait_all(loads[4:])
-    row_load(x_in, 0, 0).wait()
+
+    def start_all():
+        grad_load.start()
+        wait_all(loads)
+        loop(GROUPS, start)
+        row_load(x_in, 0, 0).wait()
+        grad_load.wait()
 
     def local(at):
         return pl.ds(pl.multiple_of(lax.rem(at.start, span), STRIP), STRIP)
@@ -1261,7 +1375,11 @@
             col = columns(part, tile)
             tile_load(slope_in, slope_v, g, part, 0).wait()
             tile_load(silu_in, silu_v, g, part, 1).wait()
-            pulled = back_product(one.spread[at, :], wd_v[col, :])
+            k = g * fetches + part
+            fetched(k)
+            weight = ring_v[lax.rem(k, slots), pl.ds(0, tile), :]
+            pulled = back_product(one.spread[at, :], weight)
+            used(k)
             gate_v[:, col] = (pulled * slope_v[:, col].astype(F32)).astype(BF)
             up_v[:, col] = (pulled * silu_v[:, col].astype(F32)).astype(BF)
 
@@ -1272,12 +1390,19 @@
 
         @pl.when(part == PARTS - 1)
         def _():
-            fill(
-                two.part,
-                at,
-                lambda col: back_product(gate_v[...], wg_v[col, :])
-                + back_product(up_v[...], wu_v[col, :]),
-            )
+            def pair(p):
+                k = g * fetches + PARTS - 1 + 2 * p
+                fetched(k)
+                fetched(k + 1)
+                here = pl.ds(0, units_wide)
+                two.part[at, columns(p, strip_wide)] = (
+                    back_product(gate_v[...], ring_v[lax.rem(k, slots), :, here])
+                    + back_product(up_v[...], ring_v[lax.rem(k + 1, slots), :, here])
+                ).astype(BF)
+                used(k)
+                used(k + 1)
+
+            loop(width // strip_wide, pair)
             two.offer(g)
             out(1, g, gate_v, gate_o, False).start()
             out(2, g, up_v, up_o, False).start()
@@ -1310,15 +1435,26 @@
         mixed_v[...] = back_product(two.spread[at, :], wo_v[...])
         out(4, g, mixed_v, mixed_o, False).start()
 
-    pace = 3
-
-    def step(s):
-        two_sums(s, one, two, made_one, between, ahead, made_two, after)
-        begin = lax.div(s * pace, 2)
-        stop = lax.div((s + 1) * pace, 2)
-        lax.fori_loop(begin, stop, lambda i, carry: (scatter.tick(i), carry)[1], 0)
-
-    loop(max(STEPS, (2 * scatter.steps + pace - 1) // pace), step)
+    lead = len(pieces)
+
+    def ticks_before(i):
+        since = i - lead - 1
+        return jnp.where(since < 0, lax.div(i + 1, 2), BEFORE + lax.div(since * PACE, 8))
+
+    def step(i):
+        for place, piece in enumerate(pieces):
+            pl.when(i == place)(piece)
+        pl.when(i == lead)(start_all)
+        two_sums(i - lead - 1, one, two, made_one, between, ahead, made_two, after)
+        lax.fori_loop(
+            ticks_before(i), ticks_before(i + 1), lambda t, carry: (scatter.tick(t), carry)[1], 0
+        )
+
+    steps = lead + 1 + STEPS
+    while BEFORE + (steps - lead - 1) * PACE // 8 < scatter.steps:
+        steps += 1
+    loop(steps, step)
+    close_attend()
 
     @pl.when(jnp.logical_not(chain.first_mid))
     def _():
@@ -1329,6 +1465,14 @@
     feed_out = pltpu.make_async_copy(feed_v, feed_gain_o, out_sem.at[7, 0])
     gain_out.start()
     feed_out.start()
+    attend_outs = [
+        pltpu.make_async_copy(src, dst, attend_sem.at[place])
+        for place, (src, dst) in enumerate(
+            ((heads_v, heads_o), (q_gain_v, q_gain_o), (k_gain_v, k_gain_o))
+        )
+    ]
+    for copy in attend_outs:
+        copy.start()
     one.close()
     two.close()
     scatter.close()
@@ -1347,6 +1491,7 @@
     out(4, GROUPS - 1, mixed_v, mixed_o, False).wait()
     gain_out.wait()
     feed_out.wait()
+    wait_all(attend_outs)
 
 
 def last_kernel(
@@ -1426,15 +1571,16 @@
         return total_sum.astype(BF)
 
     begin = len(pieces)
-    first_two, first_one = 3, begin + 2
+    first_two, first_one = 3, begin + ONE_AFTER
     sum_ticks = 4 * -(-(BLOCKS + 1) // 3)
-    first_total = first_one + sum_ticks
+    first_total = first_one + sum_ticks - 1
+    rest_two = first_one + 4 * -(-BLOCKS // 3) - 4
 
     def sums(i):
         @pl.when(i == 0)
         def _():
             loads[5].wait()
-            loop(GROUPS, two.offer)
+            two.offer(0)
 
         for place, piece in enumerate(pieces):
             pl.when(i == place)(piece)
@@ -1443,6 +1589,7 @@
         def _():
             wait_all(loads[:5])
             loop(GROUPS, start)
+            two.offer(1)
 
         def one_step(k, sum_here, make, s):
             @pl.when((s >= 0) & (s < BLOCKS))
@@ -1459,16 +1606,18 @@
                     sum_here.receive(group)
                     out(k, group).start()
 
-        def paced(k, sum_here, make, first):
+        def paced(k, sum_here, make, first, begin_step, end_step):
             since = i - first
             take = lax.rem(since, 4)
-
-            @pl.when((since >= 0) & (take < 3))
+            s = lax.div(since, 4) * 3 + take + begin_step
+
+            @pl.when((since >= 0) & (take < 3) & (s < end_step))
             def _():
-                one_step(k, sum_here, make, lax.div(since, 4) * 3 + take)
-
-        paced(1, two, made_two, first_two)
-        paced(0, one, made_one, first_one)
+                one_step(k, sum_here, make, s)
+
+        paced(1, two, made_two, first_two, 0, GROUP)
+        paced(0, one, made_one, first_one, 0, BLOCKS + 1)
+        paced(1, two, made_two, rest_two, GROUP, BLOCKS + 1)
 
     def totals(i):
         @pl.when(i == first_total)
@@ -1486,11 +1635,11 @@
                     gains[...], axis=0, keepdims=True
                 )
             for k, heads in enumerate((heads_zero, heads_one)):
-                total.value[0, pl.ds(8 + 8 * k, 8)] = heads[...]
-
-        for k in range(total.stages):
-
-            @pl.when(i == first_total + 1 + k)
+                total.value[0, pl.ds(8 + 4 * k, 4)] = heads[pl.ds(0, 4), :]
+
+        for k in range(len(total.stages)):
+
+            @pl.when(i == first_total + total.times[k])
             def _(k=k):
                 total.start(k)
 
@@ -1499,7 +1648,8 @@
         sums(i)
         totals(i)
 
-    loop(max(scatter.steps, first_total + 1 + total.stages), step)
+    last_two = rest_two + 4 * -(-(BLOCKS + 1 - GROUP) // 3)
+    loop(max(scatter.steps, last_two, first_total + total.times[-1]), step)
     close_attend()
     total.finish(total_v)
     total_out = pltpu.make_async_copy(total_v, total_o, out_sem.at[2, 0])
@@ -1567,7 +1717,9 @@
         scratch_shapes=scratch,
         cost_estimate=pl.CostEstimate(flops=flops, bytes_accessed=40_000_000, transcendentals=0),
         compiler_params=pltpu.CompilerParams(
-            collective_id=collective_id, has_side_effects=True, vmem_limit_bytes=VMEM_LIMIT
+            collective_id=collective_id,
+            has_side_effects=collective_id is not None,
+            vmem_limit_bytes=VMEM_LIMIT,
         ),
     )
 
@@ -1620,9 +1772,10 @@
 
     key_heads = keys_wide // HD
     attend_outs = [
-        ((rows, heads_wide), BF), ((rows, heads_wide), BF), ((2, key_heads, rows, HD), BF),
-        ((2, key_heads, rows, HD), BF), ((heads_wide // HD, rows, 1), F32), ((rows, heads_wide), F32),
+        ((rows, heads_wide), BF), ((rows, heads_wide), BF), ((heads_wide // HD, rows, 1), F32),
+        ((rows, heads_wide), F32),
     ]
+    key_outs = [((2, key_heads, rows, HD), BF), ((2, key_heads, rows, HD), BF)]
     smem = pl.BlockSpec(memory_space=pltpu.SMEM)
 
     attend_back_outs = [
@@ -1637,7 +1790,7 @@
     ]
 
     def attend_back_in(mixed_grad, logits, saved, q_raw, k_raw, normed):
-        mixed, q_rot, keys, values, norm, attended = saved
+        mixed, q_rot, norm, attended, keys, values = saved
         return (
             prefixes, mixed_grad, logits, attended, q_rot, keys, values, norm, q_raw, k_raw,
             query_gain, key_gain, cos, sin, normed,
@@ -1654,6 +1807,7 @@
         4,
         [smem, WHOLE, WHOLE, ANY, ANY, ANY] + [WHOLE] * 5,
         attend_outs
+        + key_outs
         + [
             ((rows, width), BF), ((rows, heads_wide), F32), ((rows, keys_wide), F32),
             ((rows, LANES), F32),
@@ -1661,8 +1815,9 @@
         [
             pltpu.VMEM((rows, keys_wide), BF), pltpu.VMEM((width, heads_wide), BF),
             pltpu.VMEM((width, keys_wide), BF), pltpu.VMEM((width, keys_wide), BF), dma(3),
+            dma(key_heads, 2), dma(key_heads, 2),
         ]
-        + attend_scratch(rows, heads_wide, keys_wide),
+        + attend_scratch(rows, heads_wide),
         3_500_000_000,
         WHOLE,
     )(
@@ -1670,15 +1825,14 @@
         query_gain, key_gain, cos, sin,
     )
     mixed_zero = saved_zero[0]
-    middle_zero, two_zero, slope, silu, hidden_zero, x_one, normed_one, q_raw, k_raw, values, logits = call(
+    middle_zero, two_zero, slope, silu, hidden_zero, x_one, normed_one, q_raw, k_raw, logits, *keys_one = call(
         partial(forward_kernel, size, 0, rows, width),
         0,
-        [WHOLE, ANY, ANY, WHOLE, ANY, ANY, ANY, WHOLE, ANY, ANY, ANY, WHOLE],
+        [WHOLE, ANY, ANY, WHOLE, ANY, ANY, ANY, WHOLE, ANY, ANY, ANY] + [WHOLE] * 4,
         [
             ((rows, width), F32), ((rows, width), BF), ((rows, units), BF), ((rows, units), BF),
             ((rows, units), BF), ((rows, width), F32), ((rows, width), BF),
-            ((rows, heads_wide), F32), ((rows, keys_wide), F32), ((rows, keys_wide), BF),
-            ((rows, LANES), F32),
+            ((rows, heads_wide), F32), ((rows, keys_wide), F32), ((rows, LANES), F32), *key_outs,
         ],
         [
             pltpu.VMEM((heads_wide, width), BF), pltpu.VMEM((width, units), BF),
@@ -1689,32 +1843,34 @@
             pltpu.VMEM((rows, units), BF), pltpu.VMEM((rows, units), BF),
             pltpu.VMEM((rows, heads_wide), F32), pltpu.VMEM((rows, keys_wide), F32),
             pltpu.VMEM((rows, keys_wide), BF), pltpu.VMEM((rows, LANES), F32),
-            dma(8), dma(11, GROUPS),
+            dma(8), dma(11, GROUPS), pltpu.VMEM((key_heads, rows, HD), BF),
+            pltpu.VMEM((key_heads, rows, HD), BF), dma(2, GROUPS), dma(2, GROUPS), dma(2, GROUPS),
         ]
         + pair_scratch,
         13_000_000_000,
     )(
         mixed_zero, stream_flat, output_weight, feed_gain, gate_weight, up_weight, down_weight,
-        attention_gain, query_weight, key_weight, value_weight, heads_padded,
+        attention_gain, query_weight, key_weight, value_weight, heads_padded, key_gain, cos, sin,
     )
-    saved_one = call(
+    attended_one = call(
         partial(attend_kernel, 1),
-        5,
-        [smem] + [WHOLE] * 8,
+        None,
+        [smem] + [WHOLE] * 7,
         attend_outs,
-        attend_scratch(rows, heads_wide, keys_wide),
+        attend_scratch(rows, heads_wide),
         1_000_000_000,
         WHOLE,
-    )(prefixes, q_raw, k_raw, values, logits, query_gain, key_gain, cos, sin)
+    )(prefixes, q_raw, logits, query_gain, cos, sin, *keys_one)
+    saved_one = [*attended_one, *keys_one]
     mixed_one = saved_one[0]
-    two_one, hidden_one, down_part, gate_low, up_low, grad, low, mixed_grad, feed_one = call(
-        partial(turn_kernel, size, 1, rows, width),
+    two_one, down_part, gate_low, up_low, grad, low, mixed_grad, feed_one, down_made = call(
+        partial(turn_kernel, size, plane_sizes, 1, rows, width),
         1,
         [WHOLE, ANY, ANY, ANY, WHOLE, ANY, ANY, ANY],
         [
-            ((rows, width), BF), ((rows, units), BF), ((rows, width), BF), ((rows, units), BF),
+            ((rows, width), BF), ((rows, width), BF), ((rows, units), BF),
             ((rows, units), BF), ((rows, width), F32), ((rows, width), BF),
-            ((rows, heads_wide), F32), ((8, width), F32),
+            ((rows, heads_wide), F32), ((8, width), F32), made_shapes[2],
         ],
         [
             pltpu.VMEM((heads_wide, width), BF), pltpu.VMEM((width, units), BF),
@@ -1725,31 +1881,25 @@
             pltpu.VMEM((rows, width), BF), pltpu.VMEM((8, width), F32),
             dma(6), dma(9, GROUPS),
         ]
-        + pair_scratch,
+        + pair_scratch + scatter_scratch,
         24_000_000_000,
     )(mixed_one, x_one, cot_flat, output_weight, feed_gain, gate_weight, up_weight, down_weight)
-    q_low, k_low, v_low, l_low, heads_one, q_gain_one, k_gain_one = call(
-        partial(attend_back_kernel, 1),
-        6,
-        [smem] + [WHOLE] * 14,
-        attend_back_outs,
-        attend_back_scratch,
-        3_000_000_000,
-        WHOLE,
-    )(*attend_back_in(mixed_grad, logits, saved_one, q_raw, k_raw, normed_one))
-    gate_low, up_low, first_low, grad, low, mixed_grad, gain_one, feed_zero, *made_one = call(
+    (gate_low, up_low, first_low, grad, low, mixed_grad, gain_one, feed_zero, heads_one, q_gain_one,
+     k_gain_one, *made_one) = call(
         partial(back_kernel, size, plane_sizes, 1, rows, width),
         2,
-        [WHOLE] * 4 + [ANY, ANY, ANY, WHOLE] + [ANY] * 9 + [WHOLE] + [ANY] * 9,
+        [smem, ANY, WHOLE, ANY] + [WHOLE] * 4 + [ANY] + [WHOLE] * 5 + [ANY]
+        + [ANY, ANY, ANY, WHOLE] + [ANY] * 9 + [WHOLE] + [ANY] * 6,
         [
             ((rows, units), BF), ((rows, units), BF), ((rows, width), BF), ((rows, width), F32),
             ((rows, width), BF), ((rows, heads_wide), F32), ((8, width), F32), ((8, width), F32),
-            *made_shapes,
+            ((8, width), F32), ((8, HD), F32), ((8, HD), F32), *made_shapes[:2], *made_shapes[3:],
         ],
-        [
+        [pltpu.VMEM(shape, kind) for shape, kind in attend_back_outs]
+        + attend_back_scratch[:2] + attend_back_scratch[3:]
+        + [
             pltpu.VMEM((width, heads_wide), BF), pltpu.VMEM((width, keys_wide), BF),
-            pltpu.VMEM((width, keys_wide), BF), pltpu.VMEM((units, width), BF),
-            pltpu.VMEM((width, units), BF), pltpu.VMEM((width, units), BF),
+            pltpu.VMEM((width, keys_wide), BF), pltpu.VMEM((4, 512, width), BF),
             pltpu.VMEM((heads_wide, width), BF), pltpu.VMEM((span, width), F32),
             pltpu.VMEM((rows, width), F32), pltpu.VMEM((span, units), BF),
             pltpu.VMEM((span, units), BF), pltpu.VMEM((span, units), BF),
@@ -1757,17 +1907,19 @@
             pltpu.VMEM((8, width), F32), pltpu.VMEM((8, width), F32),
             pltpu.VMEM((rows, width), BF), pltpu.VMEM((rows, units), BF),
             pltpu.VMEM((width, LANES), BF),
-            dma(9), dma(3), dma(2, PARTS - 1), dma(8, GROUPS),
+            dma(6), dma(3), dma(2, PARTS - 1), dma(8, GROUPS), dma(4), dma(4),
         ]
         + pair_scratch + scatter_scratch,
-        26_000_000_000,
+        28_000_000_000,
     )(
-        q_low, k_low, v_low, l_low, heads_padded, x_one, grad, attention_gain,
+        *attend_back_in(mixed_grad, logits, saved_one, q_raw, k_raw, normed_one),
+        heads_padded, x_one, grad, attention_gain,
         query_weight, key_weight, value_weight, down_weight, gate_weight, up_weight, slope, silu,
         middle_zero, feed_gain, output_weight,
-        two_one, gate_low, up_low, cot_flat, hidden_one, normed_one, low, mixed_one,
+        two_one, gate_low, up_low, low, mixed_one,
     )
-    below_rows = 8 * LAYERS
+    made_one.insert(2, down_made)
+    below_rows = 8
     stages = plane_count.bit_length() - 1 + size.bit_length() - 1
     stream_low, result, totals, *made_zero = call(
         partial(last_kernel, size, plane_sizes, 0, rows, width),
@@ -1801,7 +1953,7 @@
 
     gains = own(totals[:4], share)
     head_gains = own(totals[4, : 4 * HD].reshape(2, 2, HD), HD // plane_count)
-    heads = own(totals[8:].reshape(LAYERS, 8, width)[:, :gates], share)
+    heads = own(totals[8:].reshape(LAYERS, 4, width)[:, :gates], share)
     return (
         result.reshape(seq_count, row_count, width),
         stream_grad.reshape(seq_count, row_count, width),

time: 639 us -> 603 us (0.944)
  Pallas kernels: 620 us -> 587 us
    pallas_call x4 -> x3, Pallas kernels: 305 us -> 284 us  [the longest x1 154 us: shards(): call(partial(back_kernel, size, plane_sizes, 1, rows, width), 2, [smem, A...]
    pallas_call x1, Pallas kernels: 165 us -> 149 us  [shards(): call(partial(last_kernel, size, plane_sizes, 0, rows, width), 3, [smem] +...]
where the time goes in v5:
time: 603 us; the launch traced here: 597 us
  Pallas kernels  587 us (97%)
  local copies, waits for them, and re-layouts  6.8 us (1%)
    pallas_call x1, Pallas kernels, shards(): call(partial(back_kernel, size, plane_sizes, 1, rows, width), 2, [smem, A...  154 us
    pallas_call x1, Pallas kernels, shards(): call(partial(last_kernel, size, plane_sizes, 0, rows, width), 3, [smem] +...  149 us
    pallas_call x1, Pallas kernels, shards(): call(partial(turn_kernel, size, plane_sizes, 1, rows, width), 1, [WHOLE,...  123 us
    pallas_call x1, Pallas kernels, shards(): call(partial(forward_kernel, size, 0, rows, width), 0, [WHOLE, ANY, ANY,...  121 us
    pallas_call x1, Pallas kernels, shards(): call(partial(first_kernel, 0), 4, [smem, WHOLE, WHOLE, ANY, ANY, ANY] + [...  23.3 us

profile of v5, /device:TPU:0, one launch (start us, length us, event | category | flops | bytes accessed | tf_op | source)
XLA Modules:
  0.0 597.4 jit_solution(10668363783862242558)
XLA Ops:
  0.6 0.0 copy-start.1
  0.7 1.0 fusion
  1.7 1.0 pad_maximum_fusion
  2.7 0.0 copy-done.1
  2.7 0.5 copy.29
  3.2 1.2 pad.4.gh.refs_15_
  5.0 23.3 %shard_map.254 = (bf16[512,512]{1,0:T(8,128)(2,1)}, bf16[512,512]{1,0:T(8,128)(2,1)}, f32[4,512,1]{2,1,0:T(8,128)}, f32[512,512]{1,0:T(8,128)}, bf16[2,2,512,128...) custom-call(s32[1]{0:T(128)S(6)} %copy.35.prefix.refs_0_, ...), custom_call_target="tpu_custom_call" | custom-call | flops 3500000000 | bytes 40000000 | tf_op jit(solution)/shard_map/pallas_call | solution.py:1805
  28.4 120.8 %shard_map.255 = (f32[512,2048]{1,0:T(8,128)}, bf16[512,2048]{1,0:T(8,128)(2,1)}, bf16[512,1536]{1,0:T(8,128)(2,1)}, bf16[512,1536]{1,0:T(8,128)(2,1)}, bf16[512...) custom-call(bf16[512,512]{1,0:T(8,128)(2,1)} %get-tuple-element.80.m, ...), custom_call_target="tpu_custom_call" | custom-call | flops 12999999488 | bytes 40000000 | tf_op jit(solution)/shard_map/pallas_call | solution.py:1828
  149.2 7.4 %shard_map.256 = (bf16[512,512]{1,0:T(8,128)(2,1)}, bf16[512,512]{1,0:T(8,128)(2,1)}, f32[4,512,1]{2,1,0:T(8,128)}, f32[512,512]{1,0:T(8,128)}) custom-call(s32[1]{0:T(128)S(6)} %copy.35.prefix.refs_0_, f32[512,512]{1,0:T(8,128)} %get-tuple-element.81.q_raw.refs_8_, f32[512,128]{1,0:T(8,128)} %get-tuple-element.82.logits.refs_2_, f32[2,128]{1,0:T(2,128)} %refs_10_.3, ...), custom_call_target="tpu_custom_call" | custom-call | flops 1000000000 | bytes 40000000 | tf_op jit(solution)/shard_map/pallas_call | solution.py:1855
  156.6 123.0 %shard_map.257 = (bf16[512,2048]{1,0:T(8,128)(2,1)}, bf16[512,2048]{1,0:T(8,128)(2,1)}, bf16[512,1536]{1,0:T(8,128)(2,1)}, bf16[512,1536]{1,0:T(8,128)(2,1)}, f3...) custom-call(bf16[512,512]{1,0:T(8,128)(2,1)} %get-tuple-element.85.m, ...), custom_call_target="tpu_custom_call" | custom-call | flops 24000000000 | bytes 40000000 | tf_op jit(solution)/shard_map/pallas_call | solution.py:1866
  279.6 153.8 %shard_map.258 = (bf16[512,1536]{1,0:T(8,128)(2,1)}, bf16[512,1536]{1,0:T(8,128)(2,1)}, bf16[512,2048]{1,0:T(8,128)(2,1)}, f32[512,2048]{1,0:T(8,128)}, bf16[512...) custom-call(s32[1]{0:T(128)S(6)} %copy.35.prefix.refs_0_, ...), custom_call_target="tpu_custom_call" | custom-call | flops 28000000000 | bytes 40000000 | tf_op jit(solution)/shard_map/pallas_call | solution.py:1888
  433.4 149.3 %shard_map.259 = (bf16[512,2048]{1,0:T(8,128)(2,1)}, bf16[512,2048]{1,0:T(8,128)(2,1)}, f32[16,2048]{1,0:T(8,128)}, bf16[256,1536]{1,0:T(8,128)(2,1)}, bf16[256,...) custom-call(s32[1]{0:T(128)S(6)} %copy.35.prefix.refs_0_, ...), custom_call_target="tpu_custom_call" | custom-call | flops 19000000512 | bytes 40000000 | tf_op jit(solution)/shard_map/pallas_call | solution.py:1924
  582.7 0.0 copy-start
  582.7 9.3 %shard_map.260 = (f32[512,2048]{1,0:T(8,128)}, f32[2,256,1536]{2,1,0:T(8,128)}, f32[2,256,1536]{2,1,0:T(8,128)}, f32[2,1536,256]{2,1,0:T(8,128)}, f32[2,256,512]...) custom-call(bf16[512,2048]{1,0:T(8,128)(2,1)} %get-tuple-element.126.low_in, ...), custom_call_target="tpu_custom_call" | custom-call | tf_op jit(solution)/shard_map/pallas_call | solution.py:1698
  592.0 0.0 copy-done
  592.1 0.6 dynamic-slice_bitcast_fusion
  592.7 0.7 fusion.1
  593.3 0.6 constant_dynamic-slice_fusion.2
  594.0 3.2 copy.36
  (6 shorter events, 0.1 us)
Async XLA Ops:
  0.6 2.0 copy-start.1
  582.7 9.3 %copy-start = (f32[16,2048]{1,0:T(8,128)S(1)}, f32[16,2048]{1,0:T(8,128)}, u32[]{:S(2)}) copy-start(f32[16,2048]{1,0:T(8,128)} %get-tuple-element.138) | copy-start | bytes 393220

commit v6 on v5

--- a/solution.py
+++ b/solution.py
@@ -2,6 +2,7 @@
 
 import jax
 import jax.numpy as jnp
+import numpy as np
 from jax import lax
 from jax.experimental import pallas as pl
 from jax.experimental.pallas import tpu as pltpu
@@ -33,11 +34,15 @@
     return values * lax.rsqrt(jnp.mean(values * values, axis=-1, keepdims=True) + epsilon) * gain
 
 
-def rotary_tables(positions, width):
-    counter = jnp.arange(width // 2, dtype=jnp.float32)
-    frequency = theta ** (-2.0 * counter / width)
-    angles = positions.astype(jnp.float32)[:, None] * frequency[None, :]
-    return (jnp.cos(angles), jnp.sin(angles))
+def rotary_tables(length):
+    counter = np.arange(HD // 2, dtype=np.float32)
+    frequency = np.power(np.float32(theta), np.float32(-2.0) * counter / np.float32(HD))
+    angles = np.arange(length, dtype=np.float32)[:, None] * frequency[None, :].astype(np.float32)
+    cos, sin = np.cos(angles), np.sin(angles)
+    return (
+        np.concatenate([cos, cos], axis=1).astype(np.float32),
+        np.concatenate([-sin, sin], axis=1).astype(np.float32),
+    )
 
 
 def matmul(left, right):
@@ -324,8 +329,11 @@
         return [self.partner(bit) for bit in self.bits]
 
 
-BEFORE = 6
-PACE = 11
+BEFORE = 8
+OUTER_MORE = 0
+PACE = 12
+ONE_PACE = 8
+PER_TICK = 1
 ONE_AFTER = 3
 EARLY = BLOCKS + GROUP - 1
 TURN_PACE = 2
@@ -516,6 +524,10 @@
             self.results(jnp.int32(k), lambda copy: copy.wait())
 
 
+Z_APART = 1
+PLANE_APART = 3
+
+
 class Total:
     def __init__(self, plane, size, refs, own):
         self.value, self.land, self.s_sem, self.r_sem = refs
@@ -528,9 +540,9 @@
         self.stages += [(plane.partner(bit), rows) for bit in rest]
         self.times = [0, 1]
         for unused in across:
-            self.times.append(self.times[-1] + 2)
+            self.times.append(self.times[-1] + Z_APART)
         for unused in rest:
-            self.times.append(self.times[-1] + 3)
+            self.times.append(self.times[-1] + PLANE_APART)
 
     @staticmethod
     def scratch(rows, width, stages):
@@ -1439,7 +1451,8 @@
 
     def ticks_before(i):
         since = i - lead - 1
-        return jnp.where(since < 0, lax.div(i + 1, 2), BEFORE + lax.div(since * PACE, 8))
+        more = jnp.where(chain.outer & (since >= GROUP), OUTER_MORE, 0)
+        return jnp.where(since < 0, lax.div(i + 1, 2), BEFORE + lax.div(since * PACE, 8) + more)
 
     def step(i):
         for place, piece in enumerate(pieces):
@@ -1570,11 +1583,11 @@
     def made_two(at, total_sum):
         return total_sum.astype(BF)
 
-    begin = len(pieces)
+    begin = -(-len(pieces) // PER_TICK)
     first_two, first_one = 3, begin + ONE_AFTER
-    sum_ticks = 4 * -(-(BLOCKS + 1) // 3)
-    first_total = first_one + sum_ticks - 1
-    rest_two = first_one + 4 * -(-BLOCKS // 3) - 4
+    sum_ticks = BLOCKS + BLOCKS // ONE_PACE + 1
+    first_total = first_one + sum_ticks
+    rest_two = first_one + sum_ticks - 1
 
     def sums(i):
         @pl.when(i == 0)
@@ -1583,7 +1596,7 @@
             two.offer(0)
 
         for place, piece in enumerate(pieces):
-            pl.when(i == place)(piece)
+            pl.when(i == place // PER_TICK)(piece)
 
         @pl.when(i == begin)
         def _():
@@ -1600,24 +1613,22 @@
             def _():
                 sum_here.finish(s - 1, make)
 
-                @pl.when(lax.rem(s, GROUP) == 0)
+                @pl.when((lax.rem(s, GROUP) == 0) & chain.mid)
                 def _():
-                    group = lax.div(s, GROUP) - 1
-                    sum_here.receive(group)
-                    out(k, group).start()
-
-        def paced(k, sum_here, make, first, begin_step, end_step):
+                    out(k, lax.div(s, GROUP) - 1).start()
+
+        def paced(k, sum_here, make, first, begin_step, end_step, pace):
             since = i - first
-            take = lax.rem(since, 4)
-            s = lax.div(since, 4) * 3 + take + begin_step
-
-            @pl.when((since >= 0) & (take < 3) & (s < end_step))
+            take = lax.rem(since, pace + 1)
+            s = lax.div(since, pace + 1) * pace + take + begin_step
+
+            @pl.when((since >= 0) & (take < pace) & (s < end_step))
             def _():
                 one_step(k, sum_here, make, s)
 
-        paced(1, two, made_two, first_two, 0, GROUP)
-        paced(0, one, made_one, first_one, 0, BLOCKS + 1)
-        paced(1, two, made_two, rest_two, GROUP, BLOCKS + 1)
+        paced(1, two, made_two, first_two, 0, GROUP, 3)
+        paced(0, one, made_one, first_one, 0, BLOCKS + 1, ONE_PACE)
+        paced(1, two, made_two, rest_two, GROUP, BLOCKS + 1, 3)
 
     def totals(i):
         @pl.when(i == first_total)
@@ -1651,6 +1662,17 @@
     last_two = rest_two + 4 * -(-(BLOCKS + 1 - GROUP) // 3)
     loop(max(scatter.steps, last_two, first_total + total.times[-1]), step)
     close_attend()
+
+    def receive(g):
+        one.receive(g)
+        two.receive(g)
+
+        @pl.when(chain.outer)
+        def _():
+            out(0, g).start()
+            out(1, g).start()
+
+    loop(GROUPS, receive)
     total.finish(total_v)
     total_out = pltpu.make_async_copy(total_v, total_o, out_sem.at[2, 0])
     total_out.start()
@@ -1666,9 +1688,10 @@
     total_out.wait()
 
 
-def widen_kernel(heads_wide, keys_wide, low_in, *refs):
+def widen_kernel(heads_wide, keys_wide, low_in, result_in, *refs):
     below, above = refs[0:5], refs[5:10]
-    stream_o, gate_o, up_o, down_o, q_o, k_o, v_o, out_o = refs[10:]
+    stream_o, result_o, gate_o, up_o, down_o, q_o, k_o, v_o, out_o = refs[10:]
+    result_o[...] = result_in[...]
     stream_o[...] = low_in[...].astype(F32)
     for depth, made in enumerate((below, above)):
         gate_o[depth] = made[0][...].astype(F32)
@@ -1680,7 +1703,7 @@
         out_o[depth] = made[4][...].astype(F32)
 
 
-def widen(stream_low, below, above, heads_wide, keys_wide):
+def widen(stream_low, result, below, above, heads_wide, keys_wide):
     cuts = 4
 
     def cut(shape):
@@ -1694,16 +1717,17 @@
         below[0].shape, below[1].shape, below[2].shape, (share, heads_wide), (share, keys_wide),
         (share, keys_wide), below[4].shape,
     ]
-    inputs = [stream_low, *below, *above]
+    inputs = [stream_low, result, *below, *above]
     return pl.pallas_call(
         partial(widen_kernel, heads_wide, keys_wide),
         grid=(cuts,),
         out_shape=(
             jax.ShapeDtypeStruct(stream_low.shape, F32),
+            jax.ShapeDtypeStruct(result.shape, BF),
             *(jax.ShapeDtypeStruct((2, *shape), F32) for shape in shapes),
         ),
         in_specs=[cut(array.shape) for array in inputs],
-        out_specs=(cut(stream_low.shape), *(pair(shape) for shape in shapes)),
+        out_specs=(cut(stream_low.shape), cut(result.shape), *(pair(shape) for shape in shapes)),
         compiler_params=pltpu.CompilerParams(vmem_limit_bytes=VMEM_LIMIT),
     )(*inputs)
 
@@ -1759,10 +1783,11 @@
     share = width // plane_count
     unit = min(256, keys_wide)
     here = lax.axis_index("dp") * plane_sizes[1] + lax.axis_index("ctx")
-    positions = lax.axis_index("ctx") * row_count + jnp.arange(row_count, dtype=jnp.int32)
-    cos_table, sin_table = rotary_tables(positions, HD)
-    cos = jnp.concatenate([cos_table, cos_table], axis=1)
-    sin = jnp.concatenate([-sin_table, sin_table], axis=1)
+    first_row = lax.axis_index("ctx") * row_count
+    cos, sin = (
+        lax.dynamic_slice_in_dim(jnp.asarray(table), first_row, row_count)
+        for table in rotary_tables(row_count * plane_sizes[1])
+    )
     stream_flat = stream.reshape(rows, width)
     cot_flat = cotangent.reshape(rows, width)
     heads_padded = jnp.pad(gate_heads, ((0, 0), (0, 0), (0, LANES - gates)))
@@ -1946,7 +1971,7 @@
         grad, attention_gain, query_weight, key_weight, value_weight, down_part,
         two_zero, gate_low, up_low, first_low, hidden_zero, low, mixed_zero,
     )
-    stream_grad, *weights = widen(stream_low, made_zero, made_one, heads_wide, keys_wide)
+    stream_grad, result, *weights = widen(stream_low, result, made_zero, made_one, heads_wide, keys_wide)
 
     def own(array, wide_share):
         return lax.dynamic_slice_in_dim(array, here * wide_share, wide_share, array.ndim - 1)

time: 603 us -> 592 us (0.982)
  Pallas kernels: 587 us -> 575 us
    pallas_call x1, Pallas kernels: 149 us -> 141 us  [shards(): call(partial(last_kernel, size, plane_sizes, 0, rows, width), 3, [smem] +...]
where the time goes in v6:
time: 592 us; the launch traced here: 584 us
  Pallas kernels  575 us (97%)
  local copies, waits for them, and re-layouts  6.25 us (1%)
    pallas_call x1, Pallas kernels, shards(): call(partial(back_kernel, size, plane_sizes, 1, rows, width), 2, [smem, A...  149 us
    pallas_call x1, Pallas kernels, shards(): call(partial(last_kernel, size, plane_sizes, 0, rows, width), 3, [smem] +...  141 us
    pallas_call x1, Pallas kernels, shards(): call(partial(turn_kernel, size, plane_sizes, 1, rows, width), 1, [WHOLE,...  123 us
    pallas_call x1, Pallas kernels, shards(): call(partial(forward_kernel, size, 0, rows, width), 0, [WHOLE, ANY, ANY,...  120 us
    pallas_call x1, Pallas kernels, shards(): call(partial(first_kernel, 0), 4, [smem, WHOLE, WHOLE, ANY, ANY, ANY] + [...  23.3 us

profile of v6, /device:TPU:0, one launch (start us, length us, event | category | flops | bytes accessed | tf_op | source)
XLA Modules:
  0.0 583.5 jit_solution(18283958715062121597)
XLA Ops:
  0.6 1.9 constant_dynamic-slice_fusion.3
  2.5 1.3 copy.31
  3.8 1.2 pad.4.gh.refs_15_
  5.6 23.3 %shard_map.272 = (bf16[512,512]{1,0:T(8,128)(2,1)}, bf16[512,512]{1,0:T(8,128)(2,1)}, f32[4,512,1]{2,1,0:T(8,128)}, f32[512,512]{1,0:T(8,128)}, bf16[2,2,512,128...) custom-call(s32[1]{0:T(128)S(6)} %copy.36.prefix.refs_0_, ...), custom_call_target="tpu_custom_call" | custom-call | flops 3500000000 | bytes 40000000 | tf_op jit(solution)/shard_map/pallas_call | solution.py:1830
  28.9 120.3 %shard_map.273 = (f32[512,2048]{1,0:T(8,128)}, bf16[512,2048]{1,0:T(8,128)(2,1)}, bf16[512,1536]{1,0:T(8,128)(2,1)}, bf16[512,1536]{1,0:T(8,128)(2,1)}, bf16[512...) custom-call(bf16[512,512]{1,0:T(8,128)(2,1)} %get-tuple-element.81.m, ...), custom_call_target="tpu_custom_call" | custom-call | flops 12999999488 | bytes 40000000 | tf_op jit(solution)/shard_map/pallas_call | solution.py:1853
  149.3 7.6 %shard_map.274 = (bf16[512,512]{1,0:T(8,128)(2,1)}, bf16[512,512]{1,0:T(8,128)(2,1)}, f32[4,512,1]{2,1,0:T(8,128)}, f32[512,512]{1,0:T(8,128)}) custom-call(s32[1]{0:T(128)S(6)} %copy.36.prefix.refs_0_, f32[512,512]{1,0:T(8,128)} %get-tuple-element.82.q_raw.refs_8_, f32[512,128]{1,0:T(8,128)} %get-tuple-element.83.logits.refs_2_, f32[2,128]{1,0:T(2,128)} %refs_10_.3, ...), custom_call_target="tpu_custom_call" | custom-call | flops 1000000000 | bytes 40000000 | tf_op jit(solution)/shard_map/pallas_call | solution.py:1880
  156.9 123.0 %shard_map.275 = (bf16[512,2048]{1,0:T(8,128)(2,1)}, bf16[512,2048]{1,0:T(8,128)(2,1)}, bf16[512,1536]{1,0:T(8,128)(2,1)}, bf16[512,1536]{1,0:T(8,128)(2,1)}, f3...) custom-call(bf16[512,512]{1,0:T(8,128)(2,1)} %get-tuple-element.86.m, ...), custom_call_target="tpu_custom_call" | custom-call | flops 24000000000 | bytes 40000000 | tf_op jit(solution)/shard_map/pallas_call | solution.py:1891
  279.9 149.5 %shard_map.276 = (bf16[512,1536]{1,0:T(8,128)(2,1)}, bf16[512,1536]{1,0:T(8,128)(2,1)}, bf16[512,2048]{1,0:T(8,128)(2,1)}, f32[512,2048]{1,0:T(8,128)}, bf16[512...) custom-call(s32[1]{0:T(128)S(6)} %copy.36.prefix.refs_0_, ...), custom_call_target="tpu_custom_call" | custom-call | flops 28000000000 | bytes 40000000 | tf_op jit(solution)/shard_map/pallas_call | solution.py:1913
  429.4 141.0 %shard_map.277 = (bf16[512,2048]{1,0:T(8,128)(2,1)}, bf16[512,2048]{1,0:T(8,128)(2,1)}, f32[16,2048]{1,0:T(8,128)}, bf16[256,1536]{1,0:T(8,128)(2,1)}, bf16[256,...) custom-call(s32[1]{0:T(128)S(6)} %copy.36.prefix.refs_0_, ...), custom_call_target="tpu_custom_call" | custom-call | flops 19000000512 | bytes 40000000 | tf_op jit(solution)/shard_map/pallas_call | solution.py:1949
  570.4 0.0 copy-start
  570.4 10.7 %shard_map.278 = (f32[512,2048]{1,0:T(8,128)}, bf16[512,2048]{1,0:T(8,128)(2,1)}, f32[2,256,1536]{2,1,0:T(8,128)}, f32[2,256,1536]{2,1,0:T(8,128)}, f32[2,1536,2...) custom-call(bf16[512,2048]{1,0:T(8,128)(2,1)} %get-tuple-element.126, ...), custom_call_target="tpu_custom_call" | custom-call | tf_op jit(solution)/shard_map/pallas_call | solution.py:1721
  581.1 0.0 copy-done
  581.1 0.6 dynamic-slice_bitcast_fusion
  581.8 0.7 fusion
  582.4 0.6 constant_dynamic-slice_fusion.2
  (4 shorter events, 0.0 us)
Async XLA Ops:
  570.4 10.7 %copy-start = (f32[16,2048]{1,0:T(8,128)S(1)}, f32[16,2048]{1,0:T(8,128)}, u32[]{:S(2)}) copy-start(f32[16,2048]{1,0:T(8,128)} %get-tuple-element.140) | copy-start | bytes 393220

commit v7 on v6

--- a/solution.py
+++ b/solution.py
@@ -286,6 +286,11 @@
     return copies
 
 
+def start_all(copies):
+    for copy in copies:
+        copy.start()
+
+
 def wait_all(copies):
     for copy in copies:
         copy.wait()
@@ -329,6 +334,9 @@
         return [self.partner(bit) for bit in self.bits]
 
 
+LEAD = 4
+LAST_LEAD = 8
+LAST_PACE = 9
 BEFORE = 8
 OUTER_MORE = 0
 PACE = 12
@@ -407,6 +415,14 @@
 
         self.copy(stage, u).start()
 
+    def loads(self, pairs):
+        return [
+            pltpu.make_async_copy(src, dst, self.load_sem.at[k]) for k, (src, dst) in enumerate(pairs)
+        ]
+
+    def prefetch(self):
+        start_all(self.loads(self.groups[0][3]))
+
     def product(self, u):
         send, keep = self.refs[0][:2]
         slot, spot = lax.rem(u, self.SLOTS[0]), lax.rem(u, self.KEPT[0])
@@ -415,15 +431,18 @@
         first = 0
         place = u
         by_rows_here = u < 0
-        for unused, by_rows, count, loads in self.groups:
+        for index, (unused, by_rows, count, loads) in enumerate(self.groups):
             here = (u >= first) & (u < first + count)
             place = jnp.where(here, u - first, place)
             if by_rows:
                 by_rows_here = by_rows_here | here
 
             @pl.when(u == first)
-            def _(loads=loads):
-                wait_all(load_all(loads, self.load_sem))
+            def _(loads=loads, index=index):
+                copies = self.loads(loads)
+                if index:
+                    start_all(copies)
+                wait_all(copies)
 
             first += count
         parts = self.parts[:, columns(place, self.tile)]
@@ -678,12 +697,56 @@
 
 
 def attend_kernel(
-    depth, prefix, q_raw, logits, query_gain, cos, sin, keys, values,
-    mixed_o, q_o, norm_o, attended_o, *scratch,
+    depth, prefix, q_raw, logits, query_gain, cos, sin, keys_in, values_in,
+    mixed_o, q_o, norm_o, attended_o, keys_o, values_o, load_sem, send_sem, land_sem, *scratch,
 ):
     half = lax.axis_index("ctx")
-    attend(prefix[0], q_raw, logits, query_gain[depth : depth + 1, :], cos, sin, keys, values,
-           mixed_o, q_o, norm_o, attended_o, scratch, half, lambda j: None)
+    rows = q_raw.shape[0]
+    span = rows // GROUPS
+    early, late = pl.ds(0, rows - span), pl.ds(rows - span, span)
+    pairs = ((keys_in, keys_o), (values_in, values_o))
+    own = [pltpu.make_async_copy(src.at[0], dst.at[0], load_sem.at[0, k]) for k, (src, dst) in enumerate(pairs)]
+    other = [
+        pltpu.make_async_copy(src.at[1, :, early], dst.at[1, :, early], load_sem.at[1, k])
+        for k, (src, dst) in enumerate(pairs)
+    ]
+    travel = [
+        pltpu.make_async_remote_copy(
+            src_ref=src.at[0, :, late],
+            dst_ref=dst.at[1, :, late],
+            send_sem=send_sem.at[k],
+            recv_sem=land_sem.at[k],
+            device_id={"ctx": 1 - half},
+            device_id_type=MESH,
+        )
+        for k, (src, dst) in enumerate(pairs)
+    ]
+    start_all(own)
+    greet([{"ctx": 1 - half}], {"ctx": 1 - half}, half < 0)
+
+    @pl.when(half == 0)
+    def _():
+        start_all(travel)
+
+    @pl.when(half == 1)
+    def _():
+        start_all(other)
+
+    wait_all(own)
+
+    def arrived(j):
+        if j == 0:
+            wait_all(other)
+            for copy in travel:
+                copy.wait_recv()
+
+    attend(prefix[0], q_raw, logits, query_gain[depth : depth + 1, :], cos, sin, keys_o, values_o,
+           mixed_o, q_o, norm_o, attended_o, scratch, half, arrived)
+
+    @pl.when(half == 0)
+    def _():
+        for copy in travel:
+            copy.wait_send()
 
 
 def first_kernel(
@@ -1016,7 +1079,7 @@
         for j in range(key_heads):
             key_strip(k_v, v_v, keys_v, values_v, key_gain[depth + 1 : depth + 2, :], cos, sin, j, at)
 
-        @pl.when(half == 0)
+        @pl.when((half == 0) & (g < GROUPS - 1))
         def _():
             give_keys(g, 0).start()
             give_keys(g, 1).start()
@@ -1048,11 +1111,11 @@
         for which in range(2):
             keep_keys(g, which).wait()
 
-            @pl.when(half == 0)
+            @pl.when((half == 0) & (g < GROUPS - 1))
             def _(which=which):
                 give_keys(g, which).wait_send()
 
-            @pl.when(half == 1)
+            @pl.when((half == 1) & (g < GROUPS - 1))
             def _(which=which):
                 give_keys(g, which).wait_recv()
 
@@ -1309,6 +1372,7 @@
 
     for k in range(slots):
         fetch(jnp.int32(k), lambda copy: copy.start())
+    scatter.prefetch()
 
     def tile_load(src, dst, g, part, k):
         col = columns(part, tile)
@@ -1347,7 +1411,7 @@
     gain_v[...] = jnp.zeros_like(gain_v)
     feed_v[...] = jnp.zeros_like(feed_v)
 
-    def start_all():
+    def begin_sums():
         grad_load.start()
         wait_all(loads)
         loop(GROUPS, start)
@@ -1452,12 +1516,12 @@
     def ticks_before(i):
         since = i - lead - 1
         more = jnp.where(chain.outer & (since >= GROUP), OUTER_MORE, 0)
-        return jnp.where(since < 0, lax.div(i + 1, 2), BEFORE + lax.div(since * PACE, 8) + more)
+        return jnp.where(since < 0, lax.div(i * LEAD + 4, 8), BEFORE + lax.div(since * PACE, 8) + more)
 
     def step(i):
         for place, piece in enumerate(pieces):
             pl.when(i == place)(piece)
-        pl.when(i == lead)(start_all)
+        pl.when(i == lead)(begin_sums)
         two_sums(i - lead - 1, one, two, made_one, between, ahead, made_two, after)
         lax.fori_loop(
             ticks_before(i), ticks_before(i + 1), lambda t, carry: (scatter.tick(t), carry)[1], 0
@@ -1553,6 +1617,7 @@
          (grad_in, grad_v), (down_in, two.part)],
         load_sem,
     )
+    scatter.prefetch()
     chain.greet([*plane.partners(), *total.across, {"ctx": 1 - half}])
     gain_one = attention_gain[depth : depth + 1, :]
 
@@ -1654,13 +1719,20 @@
             def _(k=k):
                 total.start(k)
 
+    def ticks_before(i):
+        return jnp.where(i < begin, lax.div(i * LAST_LEAD, 8), lead_ticks + lax.div((i - begin) * LAST_PACE, 8))
+
     def step(i):
-        scatter.tick(i)
+        lax.fori_loop(
+            ticks_before(i), ticks_before(i + 1), lambda t, carry: (scatter.tick(t), carry)[1], 0
+        )
         sums(i)
         totals(i)
 
     last_two = rest_two + 4 * -(-(BLOCKS + 1 - GROUP) // 3)
-    loop(max(scatter.steps, last_two, first_total + total.times[-1]), step)
+    lead_ticks = begin * LAST_LEAD // 8
+    scatter_steps = begin + -(-(scatter.steps - lead_ticks) * 8 // LAST_PACE)
+    loop(max(scatter_steps, last_two, first_total + total.times[-1]), step)
     close_attend()
 
     def receive(g):
@@ -1741,9 +1813,7 @@
         scratch_shapes=scratch,
         cost_estimate=pl.CostEstimate(flops=flops, bytes_accessed=40_000_000, transcendentals=0),
         compiler_params=pltpu.CompilerParams(
-            collective_id=collective_id,
-            has_side_effects=collective_id is not None,
-            vmem_limit_bytes=VMEM_LIMIT,
+            collective_id=collective_id, has_side_effects=True, vmem_limit_bytes=VMEM_LIMIT
         ),
     )
 
@@ -1790,7 +1860,7 @@
     )
     stream_flat = stream.reshape(rows, width)
     cot_flat = cotangent.reshape(rows, width)
-    heads_padded = jnp.pad(gate_heads, ((0, 0), (0, 0), (0, LANES - gates)))
+    heads_padded = jnp.dot(gate_heads, jnp.eye(gates, LANES, dtype=BF), preferred_element_type=F32).astype(BF)
     sum_scratch = Sum.scratch(rows, width)
     landed = [pltpu.VMEM((2, rows, width), BF)]
     pair_scratch = [pltpu.VMEM((3, rows, width), BF)] + sum_scratch + sum_scratch
@@ -1877,16 +1947,15 @@
         mixed_zero, stream_flat, output_weight, feed_gain, gate_weight, up_weight, down_weight,
         attention_gain, query_weight, key_weight, value_weight, heads_padded, key_gain, cos, sin,
     )
-    attended_one = call(
+    saved_one = call(
         partial(attend_kernel, 1),
-        None,
-        [smem] + [WHOLE] * 7,
-        attend_outs,
-        attend_scratch(rows, heads_wide),
+        5,
+        [smem] + [WHOLE] * 5 + [ANY] * 2,
+        attend_outs + key_outs,
+        [dma(2, 2), dma(2), dma(2)] + attend_scratch(rows, heads_wide),
         1_000_000_000,
         WHOLE,
     )(prefixes, q_raw, logits, query_gain, cos, sin, *keys_one)
-    saved_one = [*attended_one, *keys_one]
     mixed_one = saved_one[0]
     two_one, down_part, gate_low, up_low, grad, low, mixed_grad, feed_one, down_made = call(
         partial(turn_kernel, size, plane_sizes, 1, rows, width),

time: 592 us -> 588 us (level)
  no operation moved by 1% of the time
where the time goes in v7:
time: 588 us; the launch traced here: 579 us
  Pallas kernels  572 us (97%)
    pallas_call x1, Pallas kernels, shards(): call(partial(back_kernel, size, plane_sizes, 1, rows, width), 2, [smem, A...  148 us
    pallas_call x1, Pallas kernels, shards(): call(partial(last_kernel, size, plane_sizes, 0, rows, width), 3, [smem] +...  138 us
    pallas_call x1, Pallas kernels, shards(): call(partial(turn_kernel, size, plane_sizes, 1, rows, width), 1, [WHOLE,...  123 us
    pallas_call x1, Pallas kernels, shards(): call(partial(forward_kernel, size, 0, rows, width), 0, [WHOLE, ANY, ANY,...  118 us
    pallas_call x1, Pallas kernels, shards(): call(partial(first_kernel, 0), 4, [smem, WHOLE, WHOLE, ANY, ANY, ANY] + [...  23.4 us

profile of v7, /device:TPU:0, one launch (start us, length us, event | category | flops | bytes accessed | tf_op | source)
XLA Modules:
  0.0 579.3 jit_solution(1562437302189784393)
XLA Ops:
  0.6 0.0 copy-start
  0.7 1.9 constant_dynamic-slice_fusion.3
  2.5 0.0 copy-done
  2.5 1.5 fusion.gh.refs_15_
  4.7 23.4 %shard_map.272 = (bf16[512,512]{1,0:T(8,128)(2,1)}, bf16[512,512]{1,0:T(8,128)(2,1)}, f32[4,512,1]{2,1,0:T(8,128)}, f32[512,512]{1,0:T(8,128)}, bf16[2,2,512,128...) custom-call(s32[1]{0:T(128)S(6)} %copy.37.prefix.refs_0_, ...), custom_call_target="tpu_custom_call" | custom-call | flops 3500000000 | bytes 40000000 | tf_op jit(solution)/shard_map/pallas_call | solution.py:1900
  28.1 118.5 %shard_map.273 = (f32[512,2048]{1,0:T(8,128)}, bf16[512,2048]{1,0:T(8,128)(2,1)}, bf16[512,1536]{1,0:T(8,128)(2,1)}, bf16[512,1536]{1,0:T(8,128)(2,1)}, bf16[512...) custom-call(bf16[512,512]{1,0:T(8,128)(2,1)} %get-tuple-element.83.m, ...), custom_call_target="tpu_custom_call" | custom-call | flops 12999999488 | bytes 40000000 | tf_op jit(solution)/shard_map/pallas_call | solution.py:1923
  146.6 10.3 %shard_map.274 = (bf16[512,512]{1,0:T(8,128)(2,1)}, bf16[512,512]{1,0:T(8,128)(2,1)}, f32[4,512,1]{2,1,0:T(8,128)}, f32[512,512]{1,0:T(8,128)}, bf16[2,2,512,128...) custom-call(s32[1]{0:T(128)S(6)} %copy.37.prefix.refs_0_, f32[512,512]{1,0:T(8,128)} %get-tuple-element.84.q_raw.refs_8_, ...), custom_call_target="tpu_custom_call" | custom-call | flops 1000000000 | bytes 40000000 | tf_op jit(solution)/shard_map/pallas_call | solution.py:1950
  156.9 123.1 %shard_map.275 = (bf16[512,2048]{1,0:T(8,128)(2,1)}, bf16[512,2048]{1,0:T(8,128)(2,1)}, bf16[512,1536]{1,0:T(8,128)(2,1)}, bf16[512,1536]{1,0:T(8,128)(2,1)}, f3...) custom-call(bf16[512,512]{1,0:T(8,128)(2,1)} %get-tuple-element.88.m, ...), custom_call_target="tpu_custom_call" | custom-call | flops 24000000000 | bytes 40000000 | tf_op jit(solution)/shard_map/pallas_call | solution.py:1960
  280.0 148.1 %shard_map.276 = (bf16[512,1536]{1,0:T(8,128)(2,1)}, bf16[512,1536]{1,0:T(8,128)(2,1)}, bf16[512,2048]{1,0:T(8,128)(2,1)}, f32[512,2048]{1,0:T(8,128)}, bf16[512...) custom-call(s32[1]{0:T(128)S(6)} %copy.37.prefix.refs_0_, ...), custom_call_target="tpu_custom_call" | custom-call | flops 28000000000 | bytes 40000000 | tf_op jit(solution)/shard_map/pallas_call | solution.py:1982
  428.1 138.1 %shard_map.277 = (bf16[512,2048]{1,0:T(8,128)(2,1)}, bf16[512,2048]{1,0:T(8,128)(2,1)}, f32[16,2048]{1,0:T(8,128)}, bf16[256,1536]{1,0:T(8,128)(2,1)}, bf16[256,...) custom-call(s32[1]{0:T(128)S(6)} %copy.37.prefix.refs_0_, ...), custom_call_target="tpu_custom_call" | custom-call | flops 19000000512 | bytes 40000000 | tf_op jit(solution)/shard_map/pallas_call | solution.py:2018
  566.1 0.0 copy-start.2
  566.1 0.0 copy-start.1
  566.2 10.7 %shard_map.278 = (f32[512,2048]{1,0:T(8,128)}, bf16[512,2048]{1,0:T(8,128)(2,1)}, f32[2,256,1536]{2,1,0:T(8,128)}, f32[2,256,1536]{2,1,0:T(8,128)}, f32[2,1536,2...) custom-call(bf16[512,2048]{1,0:T(8,128)(2,1)} %get-tuple-element.130, ...), custom_call_target="tpu_custom_call" | custom-call | tf_op jit(solution)/shard_map/pallas_call | solution.py:1793
  576.9 0.0 copy-done.2
  576.9 0.6 dynamic-slice_bitcast_fusion
  577.5 0.7 fusion.3
  578.2 0.6 constant_dynamic-slice_fusion.2
  578.8 0.0 copy-done.1
  (4 shorter events, 0.0 us)
Async XLA Ops:
  0.6 1.9 copy-start
  566.1 10.7 %copy-start.2 = (f32[16,2048]{1,0:T(8,128)S(1)}, f32[16,2048]{1,0:T(8,128)}, u32[]{:S(2)}) copy-start(f32[16,2048]{1,0:T(8,128)} %get-tuple-element.144) | copy-start | bytes 393220
  566.1 12.7 %copy-start.1 = (bf16[2,2048,4]{1,2,0:T(4,128)(2,1)S(1)}, bf16[2,2048,4]{1,2,0:T(4,128)(2,1)}, u32[]{:S(2)}) copy-start(bf16[2,2048,4]{1,2,0:T(4,128)(2,1)} %param.24) | copy-start | bytes 98308

commit v8 on v7

--- a/solution.py
+++ b/solution.py
@@ -222,7 +222,7 @@
 STEPS = 2 * BLOCKS + 1
 
 
-def two_sums(s, first, second, made_one, between, ahead, made_two, after):
+def two_sums(s, first, second, made_one, between, ahead, made_two, after, late=False):
     @pl.when((s >= 0) & (s < BLOCKS))
     def _():
         first.relay(s)
@@ -260,8 +260,18 @@
         @pl.when(lax.rem(s - BLOCKS, GROUP) == 0)
         def _():
             group = lax.div(s - BLOCKS, GROUP) - 1
-            second.receive(group)
-            after(group)
+            begin, stop = group, group + 1
+            if late:
+                outer = second.chain.outer
+                begin = jnp.where(outer, jnp.where(s == 2 * BLOCKS, 0, GROUPS), begin)
+                stop = jnp.where(outer, GROUPS, stop)
+
+            def one(g, carry):
+                second.receive(g)
+                after(g)
+                return carry
+
+            lax.fori_loop(begin, stop, one, 0)
 
 
 def back_norm(value, gain, grad):
@@ -1236,7 +1246,7 @@
 
 
     def step(s):
-        two_sums(s, one, two, made_one, between, ahead, made_two, after)
+        two_sums(s, one, two, made_one, between, ahead, made_two, after, True)
         ahead_ticks = jnp.where(chain.outer, OUTER_AHEAD, 0)
 
         def ticks_before(s):
@@ -1522,7 +1532,7 @@
         for place, piece in enumerate(pieces):
             pl.when(i == place)(piece)
         pl.when(i == lead)(begin_sums)
-        two_sums(i - lead - 1, one, two, made_one, between, ahead, made_two, after)
+        two_sums(i - lead - 1, one, two, made_one, between, ahead, made_two, after, True)
         lax.fori_loop(
             ticks_before(i), ticks_before(i + 1), lambda t, carry: (scatter.tick(t), carry)[1], 0
         )
@@ -1760,9 +1770,13 @@
     total_out.wait()
 
 
-def widen_kernel(heads_wide, keys_wide, low_in, result_in, *refs):
+def widen_kernel(heads_wide, keys_wide, halves, totals, low_in, result_in, *refs):
     below, above = refs[0:5], refs[5:10]
-    stream_o, result_o, gate_o, up_o, down_o, q_o, k_o, v_o, out_o = refs[10:]
+    attention_o, feed_o, stream_o, result_o, gate_o, up_o, down_o, q_o, k_o, v_o, out_o = refs[10:]
+    here = lax.axis_index("dp") * halves + lax.axis_index("ctx")
+    gains = totals[pl.ds(0, 8), columns(here, attention_o.shape[1])]
+    attention_o[...] = gains[0:2]
+    feed_o[...] = gains[2:4]
     result_o[...] = result_in[...]
     stream_o[...] = low_in[...].astype(F32)
     for depth, made in enumerate((below, above)):
@@ -1775,11 +1789,14 @@
         out_o[depth] = made[4][...].astype(F32)
 
 
-def widen(stream_low, result, below, above, heads_wide, keys_wide):
+def widen(totals, halves, stream_low, result, below, above, heads_wide, keys_wide):
     cuts = 4
 
     def cut(shape):
         return pl.BlockSpec((shape[0] // cuts, shape[1]), lambda i: (i, 0))
+
+    def fixed(shape):
+        return pl.BlockSpec(shape, lambda i: (0, 0))
 
     def pair(shape):
         return pl.BlockSpec((2, shape[0] // cuts, shape[1]), lambda i: (0, i, 0))
@@ -1791,17 +1808,19 @@
     ]
     inputs = [stream_low, result, *below, *above]
     return pl.pallas_call(
-        partial(widen_kernel, heads_wide, keys_wide),
+        partial(widen_kernel, heads_wide, keys_wide, halves),
         grid=(cuts,),
         out_shape=(
+            jax.ShapeDtypeStruct((LAYERS, share), F32),
+            jax.ShapeDtypeStruct((LAYERS, share), F32),
             jax.ShapeDtypeStruct(stream_low.shape, F32),
             jax.ShapeDtypeStruct(result.shape, BF),
             *(jax.ShapeDtypeStruct((2, *shape), F32) for shape in shapes),
         ),
-        in_specs=[cut(array.shape) for array in inputs],
-        out_specs=(cut(stream_low.shape), cut(result.shape), *(pair(shape) for shape in shapes)),
+        in_specs=[fixed(totals.shape)] + [cut(array.shape) for array in inputs],
+        out_specs=(fixed((LAYERS, share)), fixed((LAYERS, share)), cut(stream_low.shape), cut(result.shape), *(pair(shape) for shape in shapes)),
         compiler_params=pltpu.CompilerParams(vmem_limit_bytes=VMEM_LIMIT),
-    )(*inputs)
+    )(totals, *inputs)
 
 
 def call(kernel, collective_id, in_specs, outs, scratch, flops, out_spec=ANY):
@@ -2040,18 +2059,18 @@
         grad, attention_gain, query_weight, key_weight, value_weight, down_part,
         two_zero, gate_low, up_low, first_low, hidden_zero, low, mixed_zero,
     )
-    stream_grad, result, *weights = widen(stream_low, result, made_zero, made_one, heads_wide, keys_wide)
+    attention_grad, feed_grad, stream_grad, result, *weights = widen(
+        totals, plane_sizes[1], stream_low, result, made_zero, made_one, heads_wide, keys_wide)
 
     def own(array, wide_share):
         return lax.dynamic_slice_in_dim(array, here * wide_share, wide_share, array.ndim - 1)
 
-    gains = own(totals[:4], share)
     head_gains = own(totals[4, : 4 * HD].reshape(2, 2, HD), HD // plane_count)
     heads = own(totals[8:].reshape(LAYERS, 4, width)[:, :gates], share)
     return (
         result.reshape(seq_count, row_count, width),
         stream_grad.reshape(seq_count, row_count, width),
-        gains[0:2],
+        attention_grad,
         weights[3],
         weights[4],
         weights[5],
@@ -2059,7 +2078,7 @@
         head_gains[:, 0],
         head_gains[:, 1],
         weights[6],
-        gains[2:4],
+        feed_grad,
         weights[0],
         weights[1],
         weights[2],

time: 588 us -> 588 us (level)
  no operation moved by 1% of the time
where the time goes in v8:
time: 588 us; the launch traced here: 579 us
  Pallas kernels  573 us (97%)
    pallas_call x1, Pallas kernels, shards(): call(partial(back_kernel, size, plane_sizes, 1, rows, width), 2, [smem, A...  148 us
    pallas_call x1, Pallas kernels, shards(): call(partial(last_kernel, size, plane_sizes, 0, rows, width), 3, [smem] +...  138 us
    pallas_call x1, Pallas kernels, shards(): call(partial(turn_kernel, size, plane_sizes, 1, rows, width), 1, [WHOLE,...  123 us
    pallas_call x1, Pallas kernels, shards(): call(partial(forward_kernel, size, 0, rows, width), 0, [WHOLE, ANY, ANY,...  118 us
    pallas_call x1, Pallas kernels, shards(): call(partial(first_kernel, 0), 4, [smem, WHOLE, WHOLE, ANY, ANY, ANY] + [...  23.3 us

profile of v8, /device:TPU:0, one launch (start us, length us, event | category | flops | bytes accessed | tf_op | source)
XLA Modules:
  0.0 579.3 jit_solution(15887520948962703561)
XLA Ops:
  0.6 0.0 copy-start
  0.7 1.9 constant_dynamic-slice_fusion.2
  2.5 0.0 copy-done
  2.5 1.5 fusion.gh.refs_15_
  4.7 23.3 %shard_map.272 = (bf16[512,512]{1,0:T(8,128)(2,1)}, bf16[512,512]{1,0:T(8,128)(2,1)}, f32[4,512,1]{2,1,0:T(8,128)}, f32[512,512]{1,0:T(8,128)}, bf16[2,2,512,128...) custom-call(s32[1]{0:T(128)S(6)} %copy.37.prefix.refs_0_, ...), custom_call_target="tpu_custom_call" | custom-call | flops 3500000000 | bytes 40000000 | tf_op jit(solution)/shard_map/pallas_call | solution.py:1919
  28.0 118.5 %shard_map.273 = (f32[512,2048]{1,0:T(8,128)}, bf16[512,2048]{1,0:T(8,128)(2,1)}, bf16[512,1536]{1,0:T(8,128)(2,1)}, bf16[512,1536]{1,0:T(8,128)(2,1)}, bf16[512...) custom-call(bf16[512,512]{1,0:T(8,128)(2,1)} %get-tuple-element.85.m, ...), custom_call_target="tpu_custom_call" | custom-call | flops 12999999488 | bytes 40000000 | tf_op jit(solution)/shard_map/pallas_call | solution.py:1942
  146.5 10.3 %shard_map.274 = (bf16[512,512]{1,0:T(8,128)(2,1)}, bf16[512,512]{1,0:T(8,128)(2,1)}, f32[4,512,1]{2,1,0:T(8,128)}, f32[512,512]{1,0:T(8,128)}, bf16[2,2,512,128...) custom-call(s32[1]{0:T(128)S(6)} %copy.37.prefix.refs_0_, f32[512,512]{1,0:T(8,128)} %get-tuple-element.86.q_raw.refs_8_, ...), custom_call_target="tpu_custom_call" | custom-call | flops 1000000000 | bytes 40000000 | tf_op jit(solution)/shard_map/pallas_call | solution.py:1969
  156.8 123.1 %shard_map.275 = (bf16[512,2048]{1,0:T(8,128)(2,1)}, bf16[512,2048]{1,0:T(8,128)(2,1)}, bf16[512,1536]{1,0:T(8,128)(2,1)}, bf16[512,1536]{1,0:T(8,128)(2,1)}, f3...) custom-call(bf16[512,512]{1,0:T(8,128)(2,1)} %get-tuple-element.90.m, ...), custom_call_target="tpu_custom_call" | custom-call | flops 24000000000 | bytes 40000000 | tf_op jit(solution)/shard_map/pallas_call | solution.py:1979
  279.9 148.1 %shard_map.276 = (bf16[512,1536]{1,0:T(8,128)(2,1)}, bf16[512,1536]{1,0:T(8,128)(2,1)}, bf16[512,2048]{1,0:T(8,128)(2,1)}, f32[512,2048]{1,0:T(8,128)}, bf16[512...) custom-call(s32[1]{0:T(128)S(6)} %copy.37.prefix.refs_0_, ...), custom_call_target="tpu_custom_call" | custom-call | flops 28000000000 | bytes 40000000 | tf_op jit(solution)/shard_map/pallas_call | solution.py:2001
  428.0 138.1 %shard_map.277 = (bf16[512,2048]{1,0:T(8,128)(2,1)}, bf16[512,2048]{1,0:T(8,128)(2,1)}, f32[16,2048]{1,0:T(8,128)}, bf16[256,1536]{1,0:T(8,128)(2,1)}, bf16[256,...) custom-call(s32[1]{0:T(128)S(6)} %copy.37.prefix.refs_0_, ...), custom_call_target="tpu_custom_call" | custom-call | flops 19000000512 | bytes 40000000 | tf_op jit(solution)/shard_map/pallas_call | solution.py:2037
  566.2 0.0 copy-start.2
  566.2 0.0 copy-start.1
  566.2 11.4 %shard_map.278 = (f32[2,256]{1,0:T(2,128)}, f32[2,256]{1,0:T(2,128)}, f32[512,2048]{1,0:T(8,128)}, bf16[512,2048]{1,0:T(8,128)(2,1)}, f32[2,256,1536]{2,1,0:T(8,...) custom-call(f32[16,2048]{1,0:T(8,128)} %get-tuple-element.132.totals, ...), custom_call_target="tpu_custom_call" | custom-call | tf_op jit(solution)/shard_map/pallas_call | solution.py:1810
  577.6 0.0 copy-done.2
  577.6 0.6 dynamic-slice_bitcast_fusion
  578.3 0.6 constant_dynamic-slice_fusion.1
  578.9 0.0 copy-done.1
  (3 shorter events, 0.0 us)
Async XLA Ops:
  0.6 1.9 copy-start
  566.2 11.4 %copy-start.2 = (f32[16,2048]{1,0:T(8,128)S(1)}, f32[16,2048]{1,0:T(8,128)}, u32[]{:S(2)}) copy-start(f32[16,2048]{1,0:T(8,128)} %get-tuple-element.132.totals) | copy-start | bytes 393220
  566.2 12.7 %copy-start.1 = (bf16[2,2048,4]{1,2,0:T(4,128)(2,1)S(1)}, bf16[2,2048,4]{1,2,0:T(4,128)(2,1)}, u32[]{:S(2)}) copy-start(bf16[2,2048,4]{1,2,0:T(4,128)(2,1)} %param.24) | copy-start | bytes 98308
